TPU v7x, 128 devices: a whole 4x4x4 slice. The times are simulated.
128 devices in a mesh: inl: 16 (over x, z), xl: 8 (over y, core).
Axes of the slice: x: 4, y: 4, z: 4, core: 2. Of those that a mesh axis runs over, the one named last changes fastest.
Arguments:
- traces: bfloat16 [65536, 2048], P(('inl', 'xl')), may hold values from -6 to 6
- dest_tile: int32 [65536, 1], P(('inl', 'xl')), may hold values from 0 to 127; in each aligned block of 512 rows (0 to 511, 512 to 1023, ...) at most 6 rows name the same one
- bin_in_tile: int32 [65536], P(('inl', 'xl')), may hold values from 0 to 383
- fold: int32 [256, 192], P('inl', 'xl'), may hold values from 1 to 8
- thresholds: float32 [3, 7], replicated, may hold values from 0.05 to 0.8
Outputs:
- denoised: float32 [256, 192, 2048], P('inl', 'xl')
Inputs may be any that keep to these rules, and one draw needn't show every extreme that they name: `dest_tile`: in each shot group of 512 traces no tile is named more than 6 times, a bound that some block reaches.
All inputs are finite; a program needn't handle non-finite values.
Results may differ from a plain program's by a relative error of at most 0.0003.
Values may be sent and summed in bfloat16 or wider, within the bound.
No kernel may reach another device: no remote copies, remote signals or barrier semaphores. Data moves between devices by JAX's collectives and lax.ppermute only.
A program may use at most 128 MiB of HBM per device.

v0:
```python
import functools

import jax
import jax.numpy as jnp
import ml_dtypes
import numpy as np
from jax import lax
from jax.experimental import pallas as pl
from jax.experimental.pallas import tpu as pltpu
from jax.sharding import PartitionSpec as P

LEVELS = 3
SLOTS = 6
GROUP = 8
LANES = 128
BLOCK = 256

low_taps = [
    0.0352262918857095,
    -0.0854412738820267,
    -0.1350110200102546,
    0.4598775021184914,
    0.8068915093110924,
    0.3326705529500826,
]
high_taps = [(-1) ** offset * low_taps[5 - offset] for offset in range(6)]

bf16 = jnp.bfloat16
f32 = jnp.float32


def halves(matrix):
    top = np.asarray(matrix, np.float32).astype(ml_dtypes.bfloat16)
    rest = (np.asarray(matrix, np.float64) - top.astype(np.float64)).astype(ml_dtypes.bfloat16)
    return top, rest


def triple(matrix, axis):
    top, rest = halves(matrix)
    return np.concatenate([top, top, rest], axis)


def line_parts(length):
    half = length // 2
    whole = np.zeros((length, length + 4))
    for m in range(half):
        for k in range(6):
            whole[m, 2 * m + k] = low_taps[k]
            whole[half + m, 2 * m + k] = high_taps[k]
    left, sizes, right = np.linalg.svd(whole[:, length:])
    assert sizes[2] < 1e-9
    state = np.zeros((2, length))
    state[:, :4] = right[:2]
    return whole[:, :length], left[:, :2] * sizes[:2], state


def tile_parts(rows, cols):
    own_i, edge_i, state_i = line_parts(rows)
    own_c, edge_c, state_c = line_parts(cols)
    half_r, half_c = rows // 2, cols // 2

    def outer(on_rows, on_cols, banded_rows):
        both = np.einsum("ar,bc->abrc", on_rows, on_cols)
        a, b, r, c = both.shape
        if banded_rows:
            both = both.reshape(2, half_r, 2, half_c, r, c).transpose(2, 0, 1, 3, 4, 5)
        return both.reshape(a * b, r * c)

    own = outer(own_i, own_c, True)
    edges = [outer(edge_i, own_c, True), outer(own_i, edge_c, True), outer(edge_i, edge_c, True)]
    states = [
        outer(state_i, np.eye(cols), False),
        outer(np.eye(rows), state_c, False),
        outer(state_i, state_c, False),
    ]
    sizes = [-(-e.shape[1] // 8) * 8 for e in edges]
    if sum(sizes) % 16:
        sizes[2] += 8
    edges = [np.pad(e, ((0, 0), (0, s - e.shape[1]))) for e, s in zip(edges, sizes)]
    states = [np.pad(v, ((0, s - v.shape[0]), (0, 0))) for v, s in zip(states, sizes)]
    return own, np.concatenate(edges, 1), np.concatenate(states, 0), sizes


def time_parts():
    whole = np.zeros((BLOCK + LANES, BLOCK))
    for m in range(LANES):
        for k in range(6):
            whole[2 * m + k, m] = low_taps[k]
            whole[2 * m + k, LANES + m] = high_taps[k]
    return whole[:BLOCK], whole[BLOCK:]


def split(value):
    top = value.astype(bf16)
    return top, (value - top.astype(f32)).astype(bf16)


def dot(left, right):
    return jnp.dot(left, right, preferred_element_type=f32)


def left_dot(matrix, value):
    top, rest = split(value)
    return dot(matrix, jnp.concatenate([top, rest, top], 0))


def time_analysis(blocks, matrix):
    parts = [split(block) for block in blocks]
    lows, highs = [], []
    for b in range(len(blocks)):
        top, rest = parts[b]
        next_top, next_rest = [part[:, :LANES] for part in parts[(b + 1) % len(blocks)]]
        joined = jnp.concatenate([top, rest, top, next_top, next_rest, next_top], 1)
        result = dot(joined, matrix)
        lows.append(result[:, :LANES])
        highs.append(result[:, LANES:])
    return lows, highs


def time_synthesis(blocks, matrix):
    parts = [split(block) for block in blocks]
    results = []
    for b in range(len(blocks)):
        top, rest = parts[b]
        last_top, last_rest = parts[b - 1]
        joined = jnp.concatenate([top, rest, top, last_top, last_rest, last_top], 1)
        results.append(dot(joined, matrix))
    return results


def shrink(value, limit):
    return value - jnp.clip(value, -limit, limit)


def route_kernel(dest_ref, bin_ref, traces_ref, out_ref):
    traces = traces_ref.shape[0]
    tiles = out_ref.shape[0] // GROUP
    rows = out_ref.shape[0]
    dest = dest_ref[...]
    matches = lax.broadcasted_iota(jnp.int32, (tiles, traces), 0) == dest
    before = lax.broadcasted_iota(jnp.int32, (traces, traces), 0) <= lax.broadcasted_iota(
        jnp.int32, (traces, traces), 1
    )
    counts = dot(matches.astype(f32).astype(bf16), before.astype(f32).astype(bf16))
    place = jnp.sum(jnp.where(matches, counts, 0.0), 0, keepdims=True).astype(jnp.int32) - 1
    row_at = lax.broadcasted_iota(jnp.int32, (rows, traces), 0)
    main = (row_at == dest * GROUP + place).astype(f32).astype(bf16)
    span = out_ref.shape[1] // 3 // LANES * LANES
    samples = traces_ref.shape[1]
    tail = traces_ref[:, 3 * span : samples]
    for j in range(3):
        tail_row = jnp.where(place == j, SLOTS, jnp.where(place == 3 + j, SLOTS + 1, -rows * GROUP))
        extra = (row_at == dest * GROUP + tail_row).astype(f32).astype(bf16)
        at = slice(j * span, (j + 1) * span)
        out_ref[:, at] = (dot(main, traces_ref[:, at]) + dot(extra, tail)).astype(bf16)
    code = bin_ref[...] + 1
    lane = lax.broadcasted_iota(jnp.int32, (LANES, traces), 0)
    digits = jnp.where(lane == 0, code // 2, jnp.where(lane == 1, code % 2, 0))
    labels = lax.dot_general(
        main,
        digits.astype(f32).astype(bf16),
        (((1,), (1,)), ((), ())),
        preferred_element_type=f32,
    )
    out_ref[:, 3 * span :] = labels.astype(bf16)


def bin_kernel(arrived_ref, scale_ref, time_ref, state_ref, timed_ref, *state_outs):
    rows = arrived_ref.shape[0]
    bins, samples = timed_ref.shape
    span = samples // 4
    labels = arrived_ref[:, 3 * span :]
    lane = lax.broadcasted_iota(jnp.int32, (GROUP, LANES), 1)
    weights = jnp.where(lane == 0, 2.0, jnp.where(lane == 1, 1.0, 0.0)).astype(bf16)
    code = lax.dot_general(
        weights, labels, (((1,), (1,)), ((), ())), preferred_element_type=f32
    ).astype(jnp.int32)
    at = lax.broadcasted_iota(jnp.int32, (GROUP, rows), 1) % GROUP
    code = jnp.where(at < SLOTS, code, 0) - 1
    bin_at = lax.broadcasted_iota(jnp.int32, (bins, rows), 0)
    main = (bin_at == code[:1]).astype(f32).astype(bf16)
    scale = scale_ref[...]
    pieces = [dot(main, arrived_ref[:, j * span : (j + 1) * span]) for j in range(3)]
    last = None
    for j in range(3):
        first = pltpu.roll(code, SLOTS - j, 1)
        second = pltpu.roll(code, SLOTS + 1 - 3 - j, 1)
        tail_code = jnp.where(at == SLOTS, first, jnp.where(at == SLOTS + 1, second, -1))
        onehot = (bin_at == tail_code[:1]).astype(f32).astype(bf16)
        term = dot(onehot, arrived_ref[:, j * span : (j + 1) * span])
        last = term if last is None else last + term
    pieces.append(last)
    blocks = []
    for piece in pieces:
        piece = piece * scale
        blocks += [piece[:, b : b + BLOCK] for b in range(0, span, BLOCK)]
    lows, highs = time_analysis(blocks, time_ref[...])
    half = samples // 2
    for b in range(len(blocks)):
        for base, piece in ((0, lows[b]), (half, highs[b])):
            where = slice(base + b * LANES, base + (b + 1) * LANES)
            timed_ref[:, where] = piece
    put_states(timed_ref, state_ref, state_outs, BLOCK)


def put_states(value_ref, state_ref, state_outs, step):
    matrix = state_ref[...]
    for start in range(0, value_ref.shape[1], step):
        where = slice(start, start + step)
        result = left_dot(matrix, value_ref[:, where])
        top = 0
        for out in state_outs:
            out[:, where] = result[top : top + out.shape[0]]
            top += out.shape[0]


def own_kernel(timed_ref, own_ref, bands_ref):
    matrix = own_ref[...]
    for start in range(0, timed_ref.shape[1], BLOCK):
        where = slice(start, start + BLOCK)
        bands_ref[:, where] = left_dot(matrix, timed_ref[:, where])


def forward_kernel(level, thr_ref, bands_in, edge_ref, s0, s1, s2, time_ref, state_ref, *outs):
    shrunk_ref, timed_ref = outs[0], outs[1]
    state_outs = outs[2:]
    quarter = bands_in.shape[0] // 4
    half = bands_in.shape[1] // 2
    matrix = edge_ref[...]
    coarse = []
    for start in range(0, 2 * half, BLOCK):
        where = slice(start, start + BLOCK)
        states = jnp.concatenate([s0[:, where], s1[:, where], s2[:, where]], 0)
        bands = bands_in[:, where] + left_dot(matrix, states)
        high = start >= half
        for q in range(4):
            piece = bands[q * quarter : (q + 1) * quarter]
            if q or high:
                piece = shrink(piece, thr_ref[level, 2 * q + int(high) - 1])
            else:
                coarse.append(piece)
            shrunk_ref[q * quarter : (q + 1) * quarter, where] = piece
    lows, highs = time_analysis(coarse, time_ref[...])
    for b in range(len(coarse)):
        for base, piece in ((0, lows[b]), (half // 2, highs[b])):
            timed_ref[:, base + b * LANES : base + (b + 1) * LANES] = piece
    put_states(timed_ref, state_ref, state_outs, BLOCK)


def last_kernel(level, thr_ref, timed_ref, own_ref, edge_ref, s0, s1, s2, back_ref, shrunk_ref, *state_outs):
    quarter = timed_ref.shape[0] // 4
    half = timed_ref.shape[1] // 2
    for start in range(0, 2 * half, BLOCK):
        where = slice(start, start + BLOCK)
        states = jnp.concatenate([s0[:, where], s1[:, where], s2[:, where]], 0)
        bands = left_dot(own_ref[...], timed_ref[:, where]) + left_dot(edge_ref[...], states)
        high = start >= half
        row = lax.broadcasted_iota(jnp.int32, bands.shape, 0)
        limit = jnp.full(bands.shape, thr_ref[level, 0] if high else 0.0, f32)
        for q in range(1, 4):
            limit = jnp.where(row >= q * quarter, thr_ref[level, 2 * q + int(high) - 1], limit)
        shrunk_ref[:, where] = shrink(bands, limit)
    put_states(shrunk_ref, back_ref, state_outs, BLOCK)


def own_forward_kernel(level, thr_ref, timed_in, own_ref, edge_ref, s0, s1, s2, time_ref, state_ref, *outs):
    own_bands = outs[-1]
    own_kernel(timed_in, own_ref, own_bands)
    forward_kernel(level, thr_ref, own_bands, edge_ref, s0, s1, s2, time_ref, state_ref, *outs[:-1])


def rebuilt_blocks(shrunk, own_t, state_t, s0, s1, s2, time_t):
    half = shrunk.shape[1] // 2
    blocks = []
    for start in range(0, half, LANES):
        pair = []
        for base in (0, half):
            where = slice(base + start, base + start + LANES)
            pair.append((shrunk[:, where], jnp.concatenate([s0[:, where], s1[:, where], s2[:, where]], 0)))
        bands = jnp.concatenate([pair[0][0], pair[1][0]], 1)
        states = jnp.concatenate([pair[0][1], pair[1][1]], 1)
        blocks.append(left_dot(own_t[...], bands) + left_dot(state_t[...], states))
    return time_synthesis(blocks, time_t[...])


def inverse_kernel(shrunk, own_t, state_t, s0, s1, s2, time_t, above_in, back_ref, above_out, *state_outs):
    blocks = rebuilt_blocks(shrunk, own_t, state_t, s0, s1, s2, time_t)
    rows = blocks[0].shape[0]
    half = above_in.shape[1] // 2
    above_out[rows:, :] = above_in[rows:, :]
    above_out[:rows, half:] = above_in[:rows, half:]
    for b, block in enumerate(blocks):
        above_out[:rows, b * BLOCK : (b + 1) * BLOCK] = block
    put_states(above_out, back_ref, state_outs, BLOCK)


def final_kernel(shrunk, own_t, state_t, s0, s1, s2, time_t, scale_ref, out_ref):
    blocks = rebuilt_blocks(shrunk, own_t, state_t, s0, s1, s2, time_t)
    scale = scale_ref[...]
    for b, block in enumerate(blocks):
        out_ref[:, b * BLOCK : (b + 1) * BLOCK] = block * scale


def call(kernel, outs, *args, smem=(), scratch=(), aliases=None):
    in_specs = [
        pl.BlockSpec(memory_space=pltpu.SMEM if i in smem else pltpu.VMEM) for i in range(len(args))
    ]
    return pl.pallas_call(
        kernel,
        out_shape=[jax.ShapeDtypeStruct(shape, dtype) for shape, dtype in outs],
        in_specs=in_specs,
        out_specs=[pl.BlockSpec(memory_space=pltpu.VMEM)] * len(outs),
        scratch_shapes=list(scratch),
        input_output_aliases=aliases or {},
        compiler_params=pltpu.CompilerParams(vmem_limit_bytes=48 * 1024 * 1024),
    )(*args)


def shift(block, inline_by, cross_by):
    inline_devs, cross_devs = lax.axis_size("inl"), lax.axis_size("xl")
    if not cross_by:
        return lax.ppermute(block, "inl", [((i + inline_by) % inline_devs, i) for i in range(inline_devs)])
    if not inline_by:
        return lax.ppermute(block, "xl", [((j + cross_by) % cross_devs, j) for j in range(cross_devs)])
    route = [
        ((i + inline_by) % inline_devs * cross_devs + (j + cross_by) % cross_devs, i * cross_devs + j)
        for i in range(inline_devs)
        for j in range(cross_devs)
    ]
    return lax.ppermute(block, ("inl", "xl"), route)


def exchange(states, ahead):
    return [shift(states[0], ahead, 0), shift(states[1], 0, ahead), shift(states[2], ahead, ahead)]


def on_device(traces, dest_tile, bin_in_tile, fold, thresholds):
    devices = lax.axis_size("inl") * lax.axis_size("xl")
    trace_count, samples = traces.shape
    tile_rows, tile_cols = fold.shape
    bins = tile_rows * tile_cols
    width = SLOTS * samples // GROUP + LANES
    (outgoing,) = call(
        route_kernel,
        [((devices * GROUP, width), bf16)],
        dest_tile.reshape(1, trace_count),
        bin_in_tile.reshape(1, trace_count),
        traces,
    )
    arrived = lax.all_to_all(
        outgoing.reshape(devices, GROUP, width), ("inl", "xl"), split_axis=0, concat_axis=0, tiled=True
    ).reshape(devices * GROUP, width)
    scale = (1.0 / jnp.sqrt(fold.astype(f32))).reshape(bins, 1)

    main, following = time_parts()
    time_matrix = np.concatenate([triple(main, 0), triple(following, 0)], 0)
    time_back = np.concatenate(
        [triple(main.T, 0), triple(np.pad(following.T, ((0, 0), (0, BLOCK - LANES))), 0)], 0
    )
    sizes, own, edge, state = [], [], [], []
    for level in range(LEVELS):
        own_l, edge_l, state_l, sizes_l = tile_parts(tile_rows >> level, tile_cols >> level)
        sizes.append(sizes_l)
        own.append(own_l)
        edge.append(edge_l)
        state.append(state_l)
    counts = [bins >> (2 * level) for level in range(LEVELS)]
    lengths = [samples >> level for level in range(LEVELS)]

    def state_shapes(level):
        return [((size, lengths[level]), f32) for size in sizes[level]]

    timed, *states = call(
        bin_kernel,
        [((bins, samples), f32)] + state_shapes(0),
        arrived,
        scale,
        time_matrix,
        triple(state[0], 1),
    )
    states = exchange(states, 1)
    (bands,) = call(own_kernel, [((bins, samples), f32)], timed, triple(own[0], 1))
    shrunk = [None] * LEVELS
    shrunk[0], timed, *states = call(
        functools.partial(forward_kernel, 0),
        [((bins, samples), f32), ((counts[1], lengths[1]), f32)] + state_shapes(1),
        thresholds,
        bands,
        triple(edge[0], 1),
        *states,
        time_matrix,
        triple(state[1], 1),
        smem=(0,),
    )
    states = exchange(states, 1)
    shrunk[1], timed, *states = call(
        functools.partial(own_forward_kernel, 1),
        [((counts[1], lengths[1]), f32), ((counts[2], lengths[2]), f32)] + state_shapes(2),
        thresholds,
        timed,
        triple(own[1], 1),
        triple(edge[1], 1),
        *states,
        time_matrix,
        triple(state[2], 1),
        smem=(0,),
        scratch=[pltpu.VMEM((counts[1], lengths[1]), f32)],
    )
    states = exchange(states, 1)
    shrunk[2], *states = call(
        functools.partial(last_kernel, 2),
        [((counts[2], lengths[2]), f32)] + state_shapes(2),
        thresholds,
        timed,
        triple(own[2], 1),
        triple(edge[2], 1),
        *states,
        triple(edge[2].T, 1),
        smem=(0,),
    )
    states = exchange(states, -1)
    for level in (2, 1):
        shrunk[level - 1], *states = call(
            inverse_kernel,
            [((counts[level - 1], lengths[level - 1]), f32)] + state_shapes(level - 1),
            shrunk[level],
            triple(own[level].T, 1),
            triple(state[level].T, 1),
            *states,
            time_back,
            shrunk[level - 1],
            triple(edge[level - 1].T, 1),
        )
        states = exchange(states, -1)
    (denoised,) = call(
        final_kernel,
        [((bins, samples), f32)],
        shrunk[0],
        triple(own[0].T, 1),
        triple(state[0].T, 1),
        *states,
        time_back,
        scale,
    )
    return denoised.reshape(tile_rows, tile_cols, samples)


def solution(mesh):
    placed = (P(("inl", "xl"), None), P(("inl", "xl"), None), P(("inl", "xl")), P("inl", "xl"), P())
    return jax.shard_map(
        on_device, mesh=mesh, in_specs=placed, out_specs=P("inl", "xl", None), check_vma=False
    )
```

profile of v0, /device:TPU:0, one launch (start us, length us, event | category | flops | bytes accessed | tf_op | source)
XLA Modules:
  0.0 161.0 jit_solution(10565019924250892186)
XLA Ops:
  0.0 1.6 copy-done.5
  1.6 0.7 copy-done.25
  2.3 0.7 copy-done.26
  3.0 5.7 %shard_map.235 = bf16[1024,1664]{1,0:T(8,128)(2,1)} custom-call(s32[1,512]{1,0:T(1,128)S(1)} %bitcast.5, s32[1,512]{1,0:T(1,128)S(1)} %bitcast.6, bf16[512,2048]{1,0:T(8,128)(2,1)S(1)} %copy-done.5), custom_call_target="tpu_custom_call" | custom-call | tf_op jit(solution)/shard_map/pallas_call | solution.py:308
  8.7 11.6 %all-to-all-start = ((bf16[128,8,1664]{2,1,0:T(8,128)(2,1)}), bf16[128,8,1664]{2,1,0:T(8,128)(2,1)}, u32[]{:S(2)}, u32[]{:S(2)}) async-start(bf16[128,8,1664]{2,1,0:T(8,128)(2,1)} %bitcast.2), calls=%async_computation | async-start | bytes 6815744 | tf_op jit(solution)/shard_map/all_to_all | solution.py:350
  20.3 0.0 copy-start.7
  20.3 0.1 reshape.24.scale_ref
  20.5 44.0 %all-to-all-done = bf16[128,8,1664]{2,1,0:T(8,128)(2,1)} async-done(((bf16[128,8,1664]{2,1,0:T(8,128)(2,1)}), bf16[128,8,1664]{2,1,0:T(8,128)(2,1)}, u32[]{:S(2)}, u32[]{:S(2)}) %all-to-all-start) | async-done | bytes 3407904 | tf_op jit(solution)/shard_map/all_to_all | solution.py:350
  64.5 7.5 %shard_map.236 = (f32[384,2048]{1,0:T(8,128)S(1)}, f32[48,2048]{1,0:T(8,128)S(1)}, f32[32,2048]{1,0:T(8,128)S(1)}, f32[16,2048]{1,0:T(8,128)S(1)}) custom-call(bf16[1024,1664]{1,0:T(8,128)(2,1)} %bitcast.3.arrived_ref, f32[384,1]{1,0:T(8,128)S(1)} %reshape.24.scale_ref, bf16[1152,256]{1,0:T(8,128)(2,1)S(1)} %copy-done.2, bf16[96,1152]{1,0:T(8,128)(2,1)S(1)} %copy-done.11), custom_call_target="tpu_custom_call" | custom-call | tf_op jit(solution)/shard_map/pallas_call | solution.py:308
  72.0 0.0 copy-start.3
  72.0 1.7 %copy-done.3 = f32[384,2048]{1,0:T(8,128)} copy-done((f32[384,2048]{1,0:T(8,128)}, f32[384,2048]{1,0:T(8,128)S(1)}, u32[]{:S(2)}) %copy-start.3) | copy-done | bytes 3145752
  73.7 1.2 collective-permute-start
  74.9 0.0 collective-permute-start.1
  74.9 0.5 collective-permute-start.2
  75.5 4.1 %shard_map.237.bands_in = f32[384,2048]{1,0:T(8,128)S(1)} custom-call(f32[384,2048]{1,0:T(8,128)} %copy-done.3, bf16[384,1152]{1,0:T(8,128)(2,1)S(1)} %copy-done.7), custom_call_target="tpu_custom_call" | custom-call | tf_op jit(solution)/shard_map/pallas_call | solution.py:308
  79.6 0.0 copy-start
  79.7 1.7 %copy-done = f32[384,2048]{1,0:T(8,128)} copy-done((f32[384,2048]{1,0:T(8,128)}, f32[384,2048]{1,0:T(8,128)S(1)}, u32[]{:S(2)}) %copy-start) | copy-done | bytes 3145752
  81.3 0.0 copy-start.23
  81.3 0.0 copy-start.24
  81.3 0.0 copy-start.1
  81.4 0.0 copy-start.17
  81.4 0.0 copy-start.21
  81.4 0.0 copy-start.22
  81.4 0.0 copy-start.10
  81.4 0.0 copy-start.13
  81.4 0.0 copy-start.14
  81.4 5.2 %collective-permute-done.2.s2 = f32[16,2048]{1,0:T(8,128)S(1)} collective-permute-done((f32[16,2048]{1,0:T(8,128)S(1)}, f32[16,2048]{1,0:T(8,128)S(1)}, u32[]{:S(2)}, u32[]{:S(2)}) %collective-permute-start.2) | collective-permute-done | bytes 131104 | tf_op jit(solution)/shard_map/ppermute | solution.py:330
  86.7 0.0 collective-permute-done.1.s1
  86.7 0.2 collective-permute-done.s0
  86.9 3.5 %shard_map.238 = (f32[384,2048]{1,0:T(8,128)S(1)}, f32[96,1024]{1,0:T(8,128)S(1)}, f32[24,1024]{1,0:T(8,128)S(1)}, f32[16,1024]{1,0:T(8,128)S(1)}, f32[8,1024]{1,0:T(8,128)S(1)}) custom-call(f32[3,7]{1,0:T(4,128)S(1)} %copy-done.18, f32[384,2048]{1,0:T(8,128)} %copy-done, bf16[384,288]{1,0:T(8,128)(2,1)S(1)} %copy-done.9, ...), custom_call_target="tpu_custom_call" | custom-call | tf_op jit(solution)/shard_map/pallas_call | solution.py:308
  90.5 0.0 copy-start.4
  90.5 1.7 %copy-done.4 = f32[384,2048]{1,0:T(8,128)} copy-done((f32[384,2048]{1,0:T(8,128)}, f32[384,2048]{1,0:T(8,128)S(1)}, u32[]{:S(2)}) %copy-start.4) | copy-done | bytes 3145752
  92.1 4.0 %collective-permute-start.3 = (f32[24,1024]{1,0:T(8,128)S(1)}, f32[24,1024]{1,0:T(8,128)S(1)}, u32[]{:S(2)}, u32[]{:S(2)}) collective-permute-start(f32[24,1024]{1,0:T(8,128)S(1)} %get-tuple-element.36), channel_id=1, source_target_pairs={{8,0},{16,8},{24,16},{32,24},{40,32},{48,40},{56,48},{64,56},{72,6... | collective-permute-start | bytes 294920 | tf_op jit(solution)/shard_map/ppermute | solution.py:322
  96.1 2.6 %collective-permute-start.4 = (f32[16,1024]{1,0:T(8,128)S(1)}, f32[16,1024]{1,0:T(8,128)S(1)}, u32[]{:S(2)}, u32[]{:S(2)}) collective-permute-start(f32[16,1024]{1,0:T(8,128)S(1)} %get-tuple-element.37), channel_id=1, source_target_pairs={{1,0},{2,1},{3,2},{4,3},{5,4},{6,5},{7,6},{0,7},{9,8},{10,9},{11,1... | collective-permute-start | bytes 196616 | tf_op jit(solution)/shard_map/ppermute | solution.py:324
  98.7 3.3 %collective-permute-done.5.s2 = f32[8,1024]{1,0:T(8,128)S(1)} collective-permute-done((f32[8,1024]{1,0:T(8,128)S(1)}, f32[8,1024]{1,0:T(8,128)S(1)}, u32[]{:S(2)}, u32[]{:S(2)}) %collective-permute-start.5) | collective-permute-done | bytes 32800 | tf_op jit(solution)/shard_map/ppermute | solution.py:330
  102.1 1.3 shard_map.239
  103.4 3.7 %collective-permute-start.6 = (f32[16,512]{1,0:T(8,128)S(1)}, f32[16,512]{1,0:T(8,128)S(1)}, u32[]{:S(2)}, u32[]{:S(2)}) collective-permute-start(f32[16,512]{1,0:T(8,128)S(1)} %get-tuple-element.40), channel_id=1, source_target_pairs={{8,0},{16,8},{24,16},{32,24},{40,32},{48,40},{56,48},{64,56},{72,6... | collective-permute-start | bytes 98312 | tf_op jit(solution)/shard_map/ppermute | solution.py:322
  107.1 2.1 %collective-permute-start.7 = (f32[8,512]{1,0:T(8,128)S(1)}, f32[8,512]{1,0:T(8,128)S(1)}, u32[]{:S(2)}, u32[]{:S(2)}) collective-permute-start(f32[8,512]{1,0:T(8,128)S(1)} %get-tuple-element.41), channel_id=1, source_target_pairs={{1,0},{2,1},{3,2},{4,3},{5,4},{6,5},{7,6},{0,7},{9,8},{10,9},{11,1... | collective-permute-start | bytes 49160 | tf_op jit(solution)/shard_map/ppermute | solution.py:324
  109.2 0.0 collective-permute-start.8
  109.2 1.4 collective-permute-done.7.s1
  110.6 1.7 %collective-permute-done.8.s2 = f32[8,512]{1,0:T(8,128)S(1)} collective-permute-done((f32[8,512]{1,0:T(8,128)S(1)}, f32[8,512]{1,0:T(8,128)S(1)}, u32[]{:S(2)}, u32[]{:S(2)}) %collective-permute-start.8) | collective-permute-done | bytes 16416 | tf_op jit(solution)/shard_map/ppermute | solution.py:330
  112.3 0.0 collective-permute-done.6.s0
  112.4 0.8 shard_map.240
  113.2 0.0 copy-start.8
  113.2 0.1 collective-permute-start.9
  113.3 0.0 collective-permute-start.10
  113.3 0.1 collective-permute-start.11
  113.4 4.3 %collective-permute-done.10.s1 = f32[8,512]{1,0:T(8,128)S(1)} collective-permute-done((f32[8,512]{1,0:T(8,128)S(1)}, f32[8,512]{1,0:T(8,128)S(1)}, u32[]{:S(2)}, u32[]{:S(2)}) %collective-permute-start.10) | collective-permute-done | bytes 16416 | tf_op jit(solution)/shard_map/ppermute | solution.py:324
  117.7 4.8 %collective-permute-done.11.s2 = f32[8,512]{1,0:T(8,128)S(1)} collective-permute-done((f32[8,512]{1,0:T(8,128)S(1)}, f32[8,512]{1,0:T(8,128)S(1)}, u32[]{:S(2)}, u32[]{:S(2)}) %collective-permute-start.11) | collective-permute-done | bytes 16416 | tf_op jit(solution)/shard_map/ppermute | solution.py:330
  122.5 0.7 shard_map.241
  123.2 0.1 collective-permute-start.12
  123.3 0.0 collective-permute-start.13
  123.3 0.1 collective-permute-start.14
  123.4 9.2 %collective-permute-done.14.s2 = f32[8,1024]{1,0:T(8,128)S(1)} collective-permute-done((f32[8,1024]{1,0:T(8,128)S(1)}, f32[8,1024]{1,0:T(8,128)S(1)}, u32[]{:S(2)}, u32[]{:S(2)}) %collective-permute-start.14) | collective-permute-done | bytes 32800 | tf_op jit(solution)/shard_map/ppermute | solution.py:330
  132.6 0.0 collective-permute-done.13.s1
  132.6 0.0 collective-permute-done.12.s0
  132.7 3.7 %shard_map.242 = (f32[384,2048]{1,0:T(8,128)S(1)}, f32[48,2048]{1,0:T(8,128)S(1)}, f32[32,2048]{1,0:T(8,128)S(1)}, f32[16,2048]{1,0:T(8,128)S(1)}) custom-call(f32[96,1024]{1,0:T(8,128)S(1)} %get-tuple-element.48.shrunk, bf16[96,288]{1,0:T(8,128)(2,1)S(1)} %copy-done.13, bf16[96,144]{1,0:T(8,128)(2,1)S(1)} %copy-done.14, ...), custom_call_target="tpu_custom_call" | custom-call | tf_op jit(solution)/shard_map/pallas_call | solution.py:308
  136.4 0.1 collective-permute-start.15
  136.5 0.0 collective-permute-start.16
  136.5 0.3 collective-permute-start.17
  136.8 17.0 %collective-permute-done.17.s2 = f32[16,2048]{1,0:T(8,128)S(1)} collective-permute-done((f32[16,2048]{1,0:T(8,128)S(1)}, f32[16,2048]{1,0:T(8,128)S(1)}, u32[]{:S(2)}, u32[]{:S(2)}) %collective-permute-start.17) | collective-permute-done | bytes 131104 | tf_op jit(solution)/shard_map/ppermute | solution.py:330
  153.8 0.0 collective-permute-done.16.s1
  153.8 0.0 collective-permute-done.15.s0
  153.8 7.2 %shard_map.243 = f32[384,2048]{1,0:T(8,128)} custom-call(f32[384,2048]{1,0:T(8,128)S(1)} %get-tuple-element.53.shrunk, bf16[384,1152]{1,0:T(8,128)(2,1)S(1)} %copy-done.6, bf16[384,288]{1,0:T(8,128)(2,1)S(1)} %copy-done.8, f32[48,2048]{1,0:T(8,128)S(1)} %collective-permute-done.15.s0, f32[32,2048]{1,0:T(8,128)S(1)} %collective-permute-done.16.s1, ...), custom_call_target="tpu_custom_call" | custom-call | tf_op jit(solution)/shard_map/pallas_call | solution.py:308
  (41 shorter events, 0.1 us)
Async XLA Ops:
  0.0 1.6 copy-start.5
  1.6 0.7 copy-start.25
  2.3 0.7 copy-start.26
  8.7 11.6 %copy-start.27 = (s32[16,24]{1,0:T(8,128)S(1)}, s32[16,24]{1,0:T(8,128)}, u32[]{:S(2)}) copy-start(s32[16,24]{1,0:T(8,128)} %param.28) | copy-start | bytes 4612
  8.7 55.8 %copy-start.2 = (bf16[1152,256]{1,0:T(8,128)(2,1)S(1)}, bf16[1152,256]{1,0:T(8,128)(2,1)}, u32[]{:S(2)}) copy-start(bf16[1152,256]{1,0:T(8,128)(2,1)} %constant.20.clone.time_ref) | copy-start | bytes 1769476
  8.7 55.8 %copy-start.11 = (bf16[96,1152]{1,0:T(8,128)(2,1)S(1)}, bf16[96,1152]{1,0:T(8,128)(2,1)}, u32[]{:S(2)}) copy-start(bf16[96,1152]{1,0:T(8,128)(2,1)} %constant.42.clone.state_ref) | copy-start | bytes 663556
  8.7 55.8 %all-to-all-start = ((bf16[128,8,1664]{2,1,0:T(8,128)(2,1)}), bf16[128,8,1664]{2,1,0:T(8,128)(2,1)}, u32[]{:S(2)}, u32[]{:S(2)}) async-start(bf16[128,8,1664]{2,1,0:T(8,128)(2,1)} %bitcast.2), calls=%async_computation | async-start | bytes 6815744 | tf_op jit(solution)/shard_map/all_to_all | solution.py:350
  20.3 55.2 %copy-start.7 = (bf16[384,1152]{1,0:T(8,128)(2,1)S(1)}, bf16[384,1152]{1,0:T(8,128)(2,1)}, u32[]{:S(2)}) copy-start(bf16[384,1152]{1,0:T(8,128)(2,1)} %constant.43.clone.own_ref) | copy-start | bytes 2654212
  72.0 1.7 %copy-start.3 = (f32[384,2048]{1,0:T(8,128)}, f32[384,2048]{1,0:T(8,128)S(1)}, u32[]{:S(2)}) copy-start(f32[384,2048]{1,0:T(8,128)S(1)} %get-tuple-element.31.timed_ref) | copy-start | bytes 9437188
  73.7 13.2 %collective-permute-start = (f32[48,2048]{1,0:T(8,128)S(1)}, f32[48,2048]{1,0:T(8,128)S(1)}, u32[]{:S(2)}, u32[]{:S(2)}) collective-permute-start(f32[48,2048]{1,0:T(8,128)S(1)} %get-tuple-element.32), channel_id=1, source_target_pairs={{8,0},{16,8},{24,16},{32,24},{40,32},{48,40},{56,48},{64,56},{72,6... | collective-permute-start | bytes 1179656 | tf_op jit(solution)/shard_map/ppermute | solution.py:322
  74.9 11.7 %collective-permute-start.1 = (f32[32,2048]{1,0:T(8,128)S(1)}, f32[32,2048]{1,0:T(8,128)S(1)}, u32[]{:S(2)}, u32[]{:S(2)}) collective-permute-start(f32[32,2048]{1,0:T(8,128)S(1)} %get-tuple-element.33), channel_id=1, source_target_pairs={{1,0},{2,1},{3,2},{4,3},{5,4},{6,5},{7,6},{0,7},{9,8},{10,9},{11,1... | collective-permute-start | bytes 786440 | tf_op jit(solution)/shard_map/ppermute | solution.py:324
  74.9 11.7 %collective-permute-start.2 = (f32[16,2048]{1,0:T(8,128)S(1)}, f32[16,2048]{1,0:T(8,128)S(1)}, u32[]{:S(2)}, u32[]{:S(2)}) collective-permute-start(f32[16,2048]{1,0:T(8,128)S(1)} %get-tuple-element.34), channel_id=1, source_target_pairs={{9,0},{10,1},{11,2},{12,3},{13,4},{14,5},{15,6},{8,7},{17,8},{18,9... | collective-permute-start | bytes 393224 | tf_op jit(solution)/shard_map/ppermute | solution.py:330
  75.5 11.4 %copy-start.9 = (bf16[384,288]{1,0:T(8,128)(2,1)S(1)}, bf16[384,288]{1,0:T(8,128)(2,1)}, u32[]{:S(2)}) copy-start(bf16[384,288]{1,0:T(8,128)(2,1)} %constant.44.clone.edge_ref) | copy-start | bytes 663556
  75.5 11.4 %copy-start.16 = (bf16[48,288]{1,0:T(8,128)(2,1)S(1)}, bf16[48,288]{1,0:T(8,128)(2,1)}, u32[]{:S(2)}) copy-start(bf16[48,288]{1,0:T(8,128)(2,1)} %constant.45.clone.state_ref) | copy-start | bytes 82948
  75.5 11.4 %copy-start.18 = (f32[3,7]{1,0:T(4,128)S(1)}, f32[3,7]{1,0:T(4,128)}, u32[]{:S(2)}) copy-start(f32[3,7]{1,0:T(4,128)} %thr_ref.5) | copy-start | bytes 256
  79.6 1.7 %copy-start = (f32[384,2048]{1,0:T(8,128)}, f32[384,2048]{1,0:T(8,128)S(1)}, u32[]{:S(2)}) copy-start(f32[384,2048]{1,0:T(8,128)S(1)} %shard_map.237.bands_in) | copy-start | bytes 9437188
  81.3 20.8 %copy-start.12 = (bf16[96,288]{1,0:T(8,128)(2,1)S(1)}, bf16[96,288]{1,0:T(8,128)(2,1)}, u32[]{:S(2)}) copy-start(bf16[96,288]{1,0:T(8,128)(2,1)} %constant.46.clone.own_ref) | copy-start | bytes 165892
  81.3 20.8 %copy-start.15 = (bf16[96,144]{1,0:T(8,128)(2,1)S(1)}, bf16[96,144]{1,0:T(8,128)(2,1)}, u32[]{:S(2)}) copy-start(bf16[96,144]{1,0:T(8,128)(2,1)} %constant.47.clone.edge_ref) | copy-start | bytes 82948
  81.3 20.8 %copy-start.19 = (bf16[32,72]{1,0:T(8,128)(2,1)S(1)}, bf16[32,72]{1,0:T(8,128)(2,1)}, u32[]{:S(2)}) copy-start(bf16[32,72]{1,0:T(8,128)(2,1)} %constant.48.clone.state_ref) | copy-start | bytes 13828
  81.3 31.0 %copy-start.20 = (bf16[32,72]{1,0:T(8,128)(2,1)S(1)}, bf16[32,72]{1,0:T(8,128)(2,1)}, u32[]{:S(2)}) copy-start(bf16[32,72]{1,0:T(8,128)(2,1)} %constant.51.clone.back_ref) | copy-start | bytes 13828
  81.3 31.0 %copy-start.23 = (bf16[24,96]{1,0:T(8,128)(2,1)S(1)}, bf16[24,96]{1,0:T(8,128)(2,1)}, u32[]{:S(2)}) copy-start(bf16[24,96]{1,0:T(8,128)(2,1)} %constant.50.clone.edge_ref) | copy-start | bytes 13828
  81.3 31.0 %copy-start.24 = (bf16[24,72]{1,0:T(8,128)(2,1)S(1)}, bf16[24,72]{1,0:T(8,128)(2,1)}, u32[]{:S(2)}) copy-start(bf16[24,72]{1,0:T(8,128)(2,1)} %constant.49.clone.own_ref) | copy-start | bytes 10372
  81.3 41.1 %copy-start.1 = (bf16[1536,256]{1,0:T(8,128)(2,1)S(1)}, bf16[1536,256]{1,0:T(8,128)(2,1)}, u32[]{:S(2)}) copy-start(bf16[1536,256]{1,0:T(8,128)(2,1)} %constant.54.clone.time_t) | copy-start | bytes 2359300
  81.4 41.1 %copy-start.17 = (bf16[48,288]{1,0:T(8,128)(2,1)S(1)}, bf16[48,288]{1,0:T(8,128)(2,1)}, u32[]{:S(2)}) copy-start(bf16[48,288]{1,0:T(8,128)(2,1)} %constant.55.clone.back_ref) | copy-start | bytes 82948
  81.4 41.1 %copy-start.21 = (bf16[24,96]{1,0:T(8,128)(2,1)S(1)}, bf16[24,96]{1,0:T(8,128)(2,1)}, u32[]{:S(2)}) copy-start(bf16[24,96]{1,0:T(8,128)(2,1)} %constant.53.clone.state_t) | copy-start | bytes 13828
  81.4 41.1 %copy-start.22 = (bf16[24,72]{1,0:T(8,128)(2,1)S(1)}, bf16[24,72]{1,0:T(8,128)(2,1)}, u32[]{:S(2)}) copy-start(bf16[24,72]{1,0:T(8,128)(2,1)} %constant.52.clone.own_t) | copy-start | bytes 10372
  81.4 51.3 %copy-start.10 = (bf16[96,1152]{1,0:T(8,128)(2,1)S(1)}, bf16[96,1152]{1,0:T(8,128)(2,1)}, u32[]{:S(2)}) copy-start(bf16[96,1152]{1,0:T(8,128)(2,1)} %constant.58.clone.back_ref) | copy-start | bytes 663556
  81.4 51.2 %copy-start.13 = (bf16[96,288]{1,0:T(8,128)(2,1)S(1)}, bf16[96,288]{1,0:T(8,128)(2,1)}, u32[]{:S(2)}) copy-start(bf16[96,288]{1,0:T(8,128)(2,1)} %constant.56.clone.own_t) | copy-start | bytes 165892
  81.4 51.2 %copy-start.14 = (bf16[96,144]{1,0:T(8,128)(2,1)S(1)}, bf16[96,144]{1,0:T(8,128)(2,1)}, u32[]{:S(2)}) copy-start(bf16[96,144]{1,0:T(8,128)(2,1)} %constant.57.clone.state_t) | copy-start | bytes 82948
  90.5 1.7 %copy-start.4 = (f32[384,2048]{1,0:T(8,128)}, f32[384,2048]{1,0:T(8,128)S(1)}, u32[]{:S(2)}) copy-start(f32[384,2048]{1,0:T(8,128)S(1)} %get-tuple-element.52.above_in) | copy-start | bytes 9437188
  92.1 10.0 %collective-permute-start.3 = (f32[24,1024]{1,0:T(8,128)S(1)}, f32[24,1024]{1,0:T(8,128)S(1)}, u32[]{:S(2)}, u32[]{:S(2)}) collective-permute-start(f32[24,1024]{1,0:T(8,128)S(1)} %get-tuple-element.36), channel_id=1, source_target_pairs={{8,0},{16,8},{24,16},{32,24},{40,32},{48,40},{56,48},{64,56},{72,6... | collective-permute-start | bytes 294920 | tf_op jit(solution)/shard_map/ppermute | solution.py:322
  96.1 6.0 %collective-permute-start.4 = (f32[16,1024]{1,0:T(8,128)S(1)}, f32[16,1024]{1,0:T(8,128)S(1)}, u32[]{:S(2)}, u32[]{:S(2)}) collective-permute-start(f32[16,1024]{1,0:T(8,128)S(1)} %get-tuple-element.37), channel_id=1, source_target_pairs={{1,0},{2,1},{3,2},{4,3},{5,4},{6,5},{7,6},{0,7},{9,8},{10,9},{11,1... | collective-permute-start | bytes 196616 | tf_op jit(solution)/shard_map/ppermute | solution.py:324
  98.7 3.3 %collective-permute-start.5 = (f32[8,1024]{1,0:T(8,128)S(1)}, f32[8,1024]{1,0:T(8,128)S(1)}, u32[]{:S(2)}, u32[]{:S(2)}) collective-permute-start(f32[8,1024]{1,0:T(8,128)S(1)} %get-tuple-element.38), channel_id=1, source_target_pairs={{9,0},{10,1},{11,2},{12,3},{13,4},{14,5},{15,6},{8,7},{17,8},{18,9... | collective-permute-start | bytes 98312 | tf_op jit(solution)/shard_map/ppermute | solution.py:330
  103.4 8.9 %collective-permute-start.6 = (f32[16,512]{1,0:T(8,128)S(1)}, f32[16,512]{1,0:T(8,128)S(1)}, u32[]{:S(2)}, u32[]{:S(2)}) collective-permute-start(f32[16,512]{1,0:T(8,128)S(1)} %get-tuple-element.40), channel_id=1, source_target_pairs={{8,0},{16,8},{24,16},{32,24},{40,32},{48,40},{56,48},{64,56},{72,6... | collective-permute-start | bytes 98312 | tf_op jit(solution)/shard_map/ppermute | solution.py:322
  107.1 3.6 %collective-permute-start.7 = (f32[8,512]{1,0:T(8,128)S(1)}, f32[8,512]{1,0:T(8,128)S(1)}, u32[]{:S(2)}, u32[]{:S(2)}) collective-permute-start(f32[8,512]{1,0:T(8,128)S(1)} %get-tuple-element.41), channel_id=1, source_target_pairs={{1,0},{2,1},{3,2},{4,3},{5,4},{6,5},{7,6},{0,7},{9,8},{10,9},{11,1... | collective-permute-start | bytes 49160 | tf_op jit(solution)/shard_map/ppermute | solution.py:324
  109.2 3.2 %collective-permute-start.8 = (f32[8,512]{1,0:T(8,128)S(1)}, f32[8,512]{1,0:T(8,128)S(1)}, u32[]{:S(2)}, u32[]{:S(2)}) collective-permute-start(f32[8,512]{1,0:T(8,128)S(1)} %get-tuple-element.42), channel_id=1, source_target_pairs={{9,0},{10,1},{11,2},{12,3},{13,4},{14,5},{15,6},{8,7},{17,8},{18,9... | collective-permute-start | bytes 49160 | tf_op jit(solution)/shard_map/ppermute | solution.py:330
  113.2 40.6 %copy-start.6 = (bf16[384,1152]{1,0:T(8,128)(2,1)S(1)}, bf16[384,1152]{1,0:T(8,128)(2,1)}, u32[]{:S(2)}) copy-start(bf16[384,1152]{1,0:T(8,128)(2,1)} %constant.59.clone.own_t) | copy-start | bytes 2654212
  113.2 40.6 %copy-start.8 = (bf16[384,288]{1,0:T(8,128)(2,1)S(1)}, bf16[384,288]{1,0:T(8,128)(2,1)}, u32[]{:S(2)}) copy-start(bf16[384,288]{1,0:T(8,128)(2,1)} %constant.60.clone.state_t) | copy-start | bytes 663556
  113.2 9.2 %collective-permute-start.9 = (f32[16,512]{1,0:T(8,128)S(1)}, f32[16,512]{1,0:T(8,128)S(1)}, u32[]{:S(2)}, u32[]{:S(2)}) collective-permute-start(f32[16,512]{1,0:T(8,128)S(1)} %get-tuple-element.44), channel_id=1, source_target_pairs={{120,0},{0,8},{8,16},{16,24},{24,32},{32,40},{40,48},{48,56},{56,6... | collective-permute-start | bytes 98312 | tf_op jit(solution)/shard_map/ppermute | solution.py:322
  113.3 4.4 %collective-permute-start.10 = (f32[8,512]{1,0:T(8,128)S(1)}, f32[8,512]{1,0:T(8,128)S(1)}, u32[]{:S(2)}, u32[]{:S(2)}) collective-permute-start(f32[8,512]{1,0:T(8,128)S(1)} %get-tuple-element.45), channel_id=1, source_target_pairs={{7,0},{0,1},{1,2},{2,3},{3,4},{4,5},{5,6},{6,7},{15,8},{8,9},{9,10... | collective-permute-start | bytes 49160 | tf_op jit(solution)/shard_map/ppermute | solution.py:324
  113.3 9.1 %collective-permute-start.11 = (f32[8,512]{1,0:T(8,128)S(1)}, f32[8,512]{1,0:T(8,128)S(1)}, u32[]{:S(2)}, u32[]{:S(2)}) collective-permute-start(f32[8,512]{1,0:T(8,128)S(1)} %get-tuple-element.46), channel_id=1, source_target_pairs={{127,0},{120,1},{121,2},{122,3},{123,4},{124,5},{125,6},{126,7},{7... | collective-permute-start | bytes 49160 | tf_op jit(solution)/shard_map/ppermute | solution.py:330
  123.2 9.4 %collective-permute-start.12 = (f32[24,1024]{1,0:T(8,128)S(1)}, f32[24,1024]{1,0:T(8,128)S(1)}, u32[]{:S(2)}, u32[]{:S(2)}) collective-permute-start(f32[24,1024]{1,0:T(8,128)S(1)} %get-tuple-element.49), channel_id=1, source_target_pairs={{120,0},{0,8},{8,16},{16,24},{24,32},{32,40},{40,48},{48,56},{56,6... | collective-permute-start | bytes 294920 | tf_op jit(solution)/shard_map/ppermute | solution.py:322
  123.3 9.4 %collective-permute-start.13 = (f32[16,1024]{1,0:T(8,128)S(1)}, f32[16,1024]{1,0:T(8,128)S(1)}, u32[]{:S(2)}, u32[]{:S(2)}) collective-permute-start(f32[16,1024]{1,0:T(8,128)S(1)} %get-tuple-element.50), channel_id=1, source_target_pairs={{7,0},{0,1},{1,2},{2,3},{3,4},{4,5},{5,6},{6,7},{15,8},{8,9},{9,10... | collective-permute-start | bytes 196616 | tf_op jit(solution)/shard_map/ppermute | solution.py:324
  123.3 9.3 %collective-permute-start.14 = (f32[8,1024]{1,0:T(8,128)S(1)}, f32[8,1024]{1,0:T(8,128)S(1)}, u32[]{:S(2)}, u32[]{:S(2)}) collective-permute-start(f32[8,1024]{1,0:T(8,128)S(1)} %get-tuple-element.51), channel_id=1, source_target_pairs={{127,0},{120,1},{121,2},{122,3},{123,4},{124,5},{125,6},{126,7},{7... | collective-permute-start | bytes 98312 | tf_op jit(solution)/shard_map/ppermute | solution.py:330
  136.4 17.4 %collective-permute-start.15 = (f32[48,2048]{1,0:T(8,128)S(1)}, f32[48,2048]{1,0:T(8,128)S(1)}, u32[]{:S(2)}, u32[]{:S(2)}) collective-permute-start(f32[48,2048]{1,0:T(8,128)S(1)} %get-tuple-element.54), channel_id=1, source_target_pairs={{120,0},{0,8},{8,16},{16,24},{24,32},{32,40},{40,48},{48,56},{56,6... | collective-permute-start | bytes 1179656 | tf_op jit(solution)/shard_map/ppermute | solution.py:322
  136.5 17.3 %collective-permute-start.16 = (f32[32,2048]{1,0:T(8,128)S(1)}, f32[32,2048]{1,0:T(8,128)S(1)}, u32[]{:S(2)}, u32[]{:S(2)}) collective-permute-start(f32[32,2048]{1,0:T(8,128)S(1)} %get-tuple-element.55), channel_id=1, source_target_pairs={{7,0},{0,1},{1,2},{2,3},{3,4},{4,5},{5,6},{6,7},{15,8},{8,9},{9,10... | collective-permute-start | bytes 786440 | tf_op jit(solution)/shard_map/ppermute | solution.py:324
  136.5 17.3 %collective-permute-start.17 = (f32[16,2048]{1,0:T(8,128)S(1)}, f32[16,2048]{1,0:T(8,128)S(1)}, u32[]{:S(2)}, u32[]{:S(2)}) collective-permute-start(f32[16,2048]{1,0:T(8,128)S(1)} %get-tuple-element.56), channel_id=1, source_target_pairs={{127,0},{120,1},{121,2},{122,3},{123,4},{124,5},{125,6},{126,7},{7... | collective-permute-start | bytes 393224 | tf_op jit(solution)/shard_map/ppermute | solution.py:330
where the time goes:
time: 161 us
  waiting for transfers between devices  91.3 us (57%)
  Pallas kernels  34.7 us (22%)
  starting transfers between devices  26.5 us (16%)
  local copies, waits for them, and re-layouts  8.18 us (5%)
    all_to_all x1, waiting for transfers between devices, on_device(): lax.all_to_all(outgoing.reshape(devices, GROUP, width), ('inl', 'xl'), sp...  44 us
    ppermute x6, waiting for transfers between devices, shift(): return lax.ppermute(block, ('inl', 'xl'), route)  41.2 us
    pallas_call x9, Pallas kernels, call(): pl.pallas_call(kernel, out_shape=[jax.ShapeDtypeStruct(shape, dtype) for...  34.7 us
    all_to_all x1, starting transfers between devices, on_device(): lax.all_to_all(outgoing.reshape(devices, GROUP, width), ('inl', 'xl'), sp...  11.6 us
    ppermute x6, starting transfers between devices, shift(): lax.ppermute(block, 'inl', [((i + inline_by) % inline_devs, i) for i in r...  9.13 us
    unnamed x56, local copies, waits for them, and re-layouts  8.06 us
    ppermute x6, waiting for transfers between devices, shift(): lax.ppermute(block, 'xl', [((j + cross_by) % cross_devs, j) for j in rang...  5.73 us
    ppermute x6, starting transfers between devices, shift(): lax.ppermute(block, 'xl', [((j + cross_by) % cross_devs, j) for j in rang...  4.78 us
  transfers between devices with their start and end apart: 19, of which 10 were waited for; matrix products, arithmetic and copies ran while one was open for 0% of the time, Pallas kernels for 3%

commit v1 on v0

v1 whole, which is shorter than its diff:
```python
import functools

import jax
import jax.numpy as jnp
import ml_dtypes
import numpy as np
from jax import lax
from jax.experimental import pallas as pl
from jax.experimental.pallas import tpu as pltpu
from jax.sharding import PartitionSpec as P

LEVELS = 3
SLOTS = 6
GROUP = 8
LANES = 128
BLOCK = 256
VMEM_LIMIT = 32 * 1024 * 1024

low_taps = [
    0.0352262918857095,
    -0.0854412738820267,
    -0.1350110200102546,
    0.4598775021184914,
    0.8068915093110924,
    0.3326705529500826,
]
high_taps = [(-1) ** offset * low_taps[5 - offset] for offset in range(6)]

bf16 = jnp.bfloat16
f32 = jnp.float32


def halves(matrix):
    top = np.asarray(matrix, np.float32).astype(ml_dtypes.bfloat16)
    rest = (np.asarray(matrix, np.float64) - top.astype(np.float64)).astype(ml_dtypes.bfloat16)
    return top, rest


def triple(matrix, axis):
    top, rest = halves(matrix)
    return np.concatenate([top, top, rest], axis)


def line_parts(length):
    half = length // 2
    whole = np.zeros((length, length + 4))
    for m in range(half):
        for k in range(6):
            whole[m, 2 * m + k] = low_taps[k]
            whole[half + m, 2 * m + k] = high_taps[k]
    left, sizes, right = np.linalg.svd(whole[:, length:])
    assert sizes[2] < 1e-9
    state = np.zeros((2, length))
    state[:, :4] = right[:2]
    return whole[:, :length], left[:, :2] * sizes[:2], state


def outer(on_rows, on_cols, banded):
    both = np.einsum("ar,bc->abrc", on_rows, on_cols)
    a, b, r, c = both.shape
    if banded:
        both = both.reshape(2, a // 2, 2, b // 2, r, c).transpose(2, 0, 1, 3, 4, 5)
    return both.reshape(a * b, r * c)


def two_levels(length):
    own0, edge0, state0 = line_parts(length)
    own1, edge1, state1 = line_parts(length // 2)
    low = slice(0, length // 2)
    assert np.abs(state1 @ edge0[low]).max() < 1e-9
    further = state1 @ own0[low]
    return dict(
        own0=own0,
        edge0=edge0,
        state0=state0,
        own1=own1 @ own0[low],
        far1=own1 @ edge0[low],
        edge1=edge1,
        further=further,
        states=np.concatenate([state0, further]),
    )


def joint_matrices(rows, cols):
    i, c = two_levels(rows), two_levels(cols)
    wide = [np.concatenate([d["edge0"], np.zeros_like(d["edge0"])], 1) for d in (i, c)]
    both = [np.concatenate([d["far1"], d["edge1"]], 1) for d in (i, c)]
    own0 = outer(i["own0"], c["own0"], True)
    edge0 = [outer(i["edge0"], c["own0"], True), outer(i["own0"], c["edge0"], True), outer(*wide, True)]
    own1 = outer(i["own1"], c["own1"], True)
    edge1 = [
        outer(i["far1"], c["own1"], True),
        outer(i["own1"], c["far1"], True),
        outer(*both, True),
        outer(i["edge1"], np.eye(cols // 2), True),
        outer(np.eye(rows // 2), c["edge1"], True),
    ]
    states = [
        outer(i["state0"], np.eye(cols), False),
        outer(np.eye(rows), c["state0"], False),
        outer(i["states"], c["states"], False),
        outer(i["further"], c["own1"], False),
        outer(i["own1"], c["further"], False),
    ]
    sizes = [len(part) for part in states]
    return own0, np.concatenate(edge0, 1), own1, np.concatenate(edge1, 1), np.concatenate(states, 0), sizes


def tile_parts(rows, cols):
    own_i, edge_i, state_i = line_parts(rows)
    own_c, edge_c, state_c = line_parts(cols)
    own = outer(own_i, own_c, True)
    edges = [outer(edge_i, own_c, True), outer(own_i, edge_c, True), outer(edge_i, edge_c, True)]
    states = [
        outer(state_i, np.eye(cols), False),
        outer(np.eye(rows), state_c, False),
        outer(state_i, state_c, False),
    ]
    sizes = [-(-e.shape[1] // 8) * 8 for e in edges]
    if sum(sizes) % 16:
        sizes[2] += 8
    edges = [np.pad(e, ((0, 0), (0, s - e.shape[1]))) for e, s in zip(edges, sizes)]
    states = [np.pad(v, ((0, s - v.shape[0]), (0, 0))) for v, s in zip(states, sizes)]
    return own, np.concatenate(edges, 1), np.concatenate(states, 0), sizes


def time_parts():
    whole = np.zeros((BLOCK + LANES, BLOCK))
    for m in range(LANES):
        for k in range(6):
            whole[2 * m + k, m] = low_taps[k]
            whole[2 * m + k, LANES + m] = high_taps[k]
    return whole[:BLOCK], whole[BLOCK:]


def split(value):
    top = value.astype(bf16)
    return top, (value - top.astype(f32)).astype(bf16)


def dot(left, right):
    return jnp.dot(left, right, preferred_element_type=f32)


def left_dot(matrix, value):
    top, rest = split(value)
    return dot(matrix, jnp.concatenate([top, rest, top], 0))


def time_analysis(blocks, matrix):
    parts = [split(block) for block in blocks]
    lows, highs = [], []
    for b in range(len(blocks)):
        top, rest = parts[b]
        next_top, next_rest = [part[:, :LANES] for part in parts[(b + 1) % len(blocks)]]
        joined = jnp.concatenate([top, rest, top, next_top, next_rest, next_top], 1)
        result = dot(joined, matrix)
        lows.append(result[:, :LANES])
        highs.append(result[:, LANES:])
    return lows, highs


def time_synthesis(blocks, matrix):
    parts = [split(block) for block in blocks]
    results = []
    for b in range(len(blocks)):
        top, rest = parts[b]
        last_top, last_rest = parts[b - 1]
        joined = jnp.concatenate([top, rest, top, last_top, last_rest, last_top], 1)
        results.append(dot(joined, matrix))
    return results


def synthesis_from_low(lows, matrix):
    parts = [split(low) for low in lows]
    results = []
    for b in range(len(lows)):
        top, rest = parts[b]
        last_top, last_rest = parts[b - 1]
        joined = jnp.concatenate([top, rest, top, last_top, last_rest, last_top], 1)
        results.append(dot(joined, matrix))
    return results


def shrink(value, limit):
    return value - jnp.clip(value, -limit, limit)


def route_kernel(dest_far, bin_far, traces_far, out_far, dest_ref, bin_ref, traces_ref, out_ref, in_sems, out_sems):
    traces, samples = traces_ref.shape
    rows = out_ref.shape[0]
    tiles = rows // GROUP
    span = samples // 4
    coming = [
        pltpu.make_async_copy(dest_far, dest_ref, in_sems.at[4]),
        pltpu.make_async_copy(bin_far, bin_ref, in_sems.at[5]),
    ]
    for j in (3, 0, 1, 2):
        at = pl.ds(j * span, span)
        coming.append(pltpu.make_async_copy(traces_far.at[:, at], traces_ref.at[:, at], in_sems.at[j]))
    for copy in coming:
        copy.start()
    before = lax.broadcasted_iota(jnp.int32, (traces, traces), 0) <= lax.broadcasted_iota(
        jnp.int32, (traces, traces), 1
    )
    before = before.astype(f32).astype(bf16)
    coming[0].wait()
    coming[1].wait()
    dest = dest_ref[...]
    matches = lax.broadcasted_iota(jnp.int32, (tiles, traces), 0) == dest
    counts = dot(matches.astype(f32).astype(bf16), before)
    place = jnp.sum(jnp.where(matches, counts, 0.0), 0, keepdims=True).astype(jnp.int32) - 1
    row_at = lax.broadcasted_iota(jnp.int32, (rows, traces), 0)
    main = (row_at == dest * GROUP + place).astype(f32).astype(bf16)
    going = []

    def send(number, first, width):
        at = pl.ds(first, width)
        going.append(pltpu.make_async_copy(out_ref.at[:, at], out_far.at[:, at], out_sems.at[number]))
        going[-1].start()

    code = bin_ref[...] + 1
    lane = lax.broadcasted_iota(jnp.int32, (LANES, traces), 0)
    digits = jnp.where(lane == 0, code // 2, jnp.where(lane == 1, code % 2, 0))
    labels = lax.dot_general(
        main,
        digits.astype(f32).astype(bf16),
        (((1,), (1,)), ((), ())),
        preferred_element_type=f32,
    )
    out_ref[:, 3 * span :] = labels.astype(bf16)
    send(3, 3 * span, LANES)
    coming[2].wait()
    tail = traces_ref[:, 3 * span : samples]
    for j in range(3):
        tail_row = jnp.where(place == j, SLOTS, jnp.where(place == 3 + j, SLOTS + 1, -rows * GROUP))
        extra = (row_at == dest * GROUP + tail_row).astype(f32).astype(bf16)
        at = slice(j * span, (j + 1) * span)
        coming[3 + j].wait()
        out_ref[:, at] = (dot(main, traces_ref[:, at]) + dot(extra, tail)).astype(bf16)
        send(j, j * span, span)
    for copy in going:
        copy.wait()


def bin_kernel(
    arrived_far, scale_ref, time_far, state_far, summed_ref, s0, s1, s2, arrived_ref, time_ref, state_ref, sems
):
    outs = (s0, s1, s2)
    width = summed_ref.shape[1] // 4
    coming = []
    for j, (first, size) in enumerate([(3 * width, LANES)] + [(j * width, width) for j in range(3)]):
        at = pl.ds(first, size)
        coming.append(pltpu.make_async_copy(arrived_far.at[:, at], arrived_ref.at[:, at], sems.at[j]))
    coming.append(pltpu.make_async_copy(state_far, state_ref, sems.at[4]))
    coming.append(pltpu.make_async_copy(time_far, time_ref, sems.at[5]))
    for copy in coming:
        copy.start()
    coming[0].wait()
    rows = arrived_ref.shape[0]
    bins, samples = summed_ref.shape
    span = samples // 4
    labels = arrived_ref[:, 3 * span :]
    lane = lax.broadcasted_iota(jnp.int32, (GROUP, LANES), 1)
    weights = jnp.where(lane == 0, 2.0, jnp.where(lane == 1, 1.0, 0.0)).astype(bf16)
    code = lax.dot_general(
        weights, labels, (((1,), (1,)), ((), ())), preferred_element_type=f32
    ).astype(jnp.int32)
    at = lax.broadcasted_iota(jnp.int32, (GROUP, rows), 1) % GROUP
    code = jnp.where(at < SLOTS, code, 0) - 1
    bin_at = lax.broadcasted_iota(jnp.int32, (bins, rows), 0)
    main = (bin_at == code[:1]).astype(f32).astype(bf16)
    scale = scale_ref[...]
    pieces = []
    for j in range(3):
        coming[1 + j].wait()
        pieces.append(dot(main, arrived_ref[:, j * span : (j + 1) * span]))
    last = None
    for j in range(3):
        first = pltpu.roll(code, SLOTS - j, 1)
        second = pltpu.roll(code, SLOTS + 1 - 3 - j, 1)
        tail_code = jnp.where(at == SLOTS, first, jnp.where(at == SLOTS + 1, second, -1))
        onehot = (bin_at == tail_code[:1]).astype(f32).astype(bf16)
        term = dot(onehot, arrived_ref[:, j * span : (j + 1) * span])
        last = term if last is None else last + term
    pieces.append(last)
    coming[4].wait()
    coming[5].wait()
    matrix = state_ref[...]
    blocks = []
    for p, piece in enumerate(pieces):
        piece = piece * scale
        summed_ref[:, p * span : (p + 1) * span] = piece
        states = left_dot(matrix, piece)
        blocks += [states[:, b : b + BLOCK] for b in range(0, span, BLOCK)]
    lows, highs = time_analysis(blocks, time_ref[...])
    for b in range(len(blocks)):
        put_joint(outs, slice(b * LANES, (b + 1) * LANES), lows[b], highs[b])


def put_joint(outs, where, low, high):
    rows, cols, corner = [out.shape[0] for out in outs]
    ends = [0]
    for size in (rows * 2 // 5, cols * 2 // 5, corner // 2, rows // 5, cols // 5):
        ends.append(ends[-1] + size)
    part = [slice(ends[k], ends[k + 1]) for k in range(5)]
    put_rows([outs[0]], where, jnp.concatenate([low[part[0]], high[part[0]], low[part[3]]], 0))
    put_rows([outs[1]], where, jnp.concatenate([low[part[1]], high[part[1]], low[part[4]]], 0))
    put_rows([outs[2]], where, jnp.concatenate([low[part[2]], high[part[2]]], 0))


def take_joint(refs, where):
    rows, cols, corner = [ref.shape[0] for ref in refs]
    r, c, d = rows * 2 // 5, cols * 2 // 5, corner // 2
    m0, m1, m2 = [ref[:, where] for ref in refs]
    low = jnp.concatenate([m0[:r], m1[:c], m2[:d], m0[2 * r :], m1[2 * c :]], 0)
    high = jnp.concatenate([m0[r : 2 * r], m1[c : 2 * c], m2[d:]], 0)
    return low, high


def put_rows(outs, where, value):
    top = 0
    for out in outs:
        out[:, where] = value[top : top + out.shape[0]]
        top += out.shape[0]


def join_rows(refs, where):
    return jnp.concatenate([ref[:, where] for ref in refs], 0)


def put_states(value_ref, state_ref, state_outs, step):
    matrix = state_ref[...]
    for start in range(0, value_ref.shape[1], step):
        where = slice(start, start + step)
        result = left_dot(matrix, value_ref[:, where])
        put_rows(state_outs, where, result)


def steps(ref):
    return [slice(start, start + BLOCK) for start in range(0, ref.shape[1], BLOCK)]


def own_kernel(summed_ref, time_ref, own_ref, next_ref, low_ref, high_ref, next_out):
    blocks = [summed_ref[:, where] for where in steps(summed_ref)]
    lows, highs = time_analysis(blocks, time_ref[...])
    for b in range(0, len(blocks), 2):
        where = slice(b * LANES, (b + 2) * LANES)
        low = jnp.concatenate([lows[b], lows[b + 1]], 1)
        next_out[:, where] = left_dot(next_ref[...], low)
        low_ref[:, where] = left_dot(own_ref[...], low)
        high_ref[:, where] = left_dot(own_ref[...], jnp.concatenate([highs[b], highs[b + 1]], 1))


def middle_kernel(thr_ref, own_ref, edge_ref, s0, s1, s2, time_ref, state_ref, shrunk_ref, timed_ref, *state_outs):
    quarter = shrunk_ref.shape[0] // 4
    half = shrunk_ref.shape[1] // 2
    matrix = edge_ref[...]
    blocks = []
    for where in steps(own_ref):
        low, _ = take_joint((s0, s1, s2), where)
        blocks.append(own_ref[:, where] + left_dot(matrix, low))
    lows, highs = time_analysis(blocks, time_ref[...])
    for b in range(len(blocks)):
        for base, piece, high in ((0, lows[b], 0), (half, highs[b], 1)):
            where = slice(base + b * LANES, base + (b + 1) * LANES)
            for q in range(4):
                at = slice(q * quarter, (q + 1) * quarter)
                if q or high:
                    shrunk_ref[at, where] = shrink(piece[at], thr_ref[1, 2 * q + high - 1])
                else:
                    shrunk_ref[at, where] = jnp.zeros_like(piece[at])
    coarse = [jnp.concatenate([lows[b][:quarter], lows[b + 1][:quarter]], 1) for b in range(0, len(lows), 2)]
    lows, highs = time_analysis(coarse, time_ref[...])
    for b in range(len(coarse)):
        for base, piece in ((0, lows[b]), (half // 2, highs[b])):
            timed_ref[:, base + b * LANES : base + (b + 1) * LANES] = piece
    put_states(timed_ref, state_ref, state_outs, BLOCK)


def details_kernel(thr_ref, low_in, high_in, edge_ref, s0, s1, s2, back_low, back_ref, low_out, high_out, *state_outs):
    quarter = low_in.shape[0] // 4
    for where in steps(low_in):
        low, high = take_joint((s0, s1, s2), where)
        bands = low_in[quarter:, where] + left_dot(edge_ref[quarter:], low[: high.shape[0]])
        bands = [shrink(bands[(q - 1) * quarter : q * quarter], thr_ref[0, 2 * q - 1]) for q in range(1, 4)]
        bands = jnp.concatenate(bands, 0)
        low_out[:, where] = bands
        state_outs[0][:, where] = left_dot(back_low[...], bands)
        bands = high_in[:, where] + left_dot(edge_ref[...], high)
        bands = [shrink(bands[q * quarter : (q + 1) * quarter], thr_ref[0, 2 * q]) for q in range(4)]
        bands = jnp.concatenate(bands, 0)
        high_out[:, where] = bands
        state_outs[1][:, where] = left_dot(back_ref[...], bands)


def spread_kernel(low_in, high_in, low_matrix, own_matrix, shrunk_in, time_t, low_out, high_out, next_out):
    for where in steps(low_in):
        low_out[:, where] = left_dot(low_matrix[...], low_in[:, where])
        high_out[:, where] = left_dot(own_matrix[...], high_in[:, where])
    half = shrunk_in.shape[1] // 2
    blocks = []
    for b in range(0, half, LANES):
        blocks.append(jnp.concatenate([shrunk_in[:, b : b + LANES], shrunk_in[:, half + b : half + b + LANES]], 1))
    for b, block in enumerate(time_synthesis(blocks, time_t[...])):
        next_out[:, b * BLOCK : (b + 1) * BLOCK] = block


def rejoin_kernel(
    shrunk, own_t, state_t, s0, s1, s2, time_t, time_low, next_in, low_states, high_states, back_ref, next_out, *outs
):
    coarse = rebuilt_blocks(shrunk, own_t, state_t, s0, s1, s2, time_t)
    rows = coarse[0].shape[0]
    lows = []
    for block in coarse:
        lows += [block[:, b : b + LANES] for b in range(0, BLOCK, LANES)]
    count = low_states.shape[0]
    for b, block in enumerate(synthesis_from_low(lows, time_low[...])):
        where = slice(b * BLOCK, (b + 1) * BLOCK)
        bands = jnp.concatenate([next_in[:rows, where] + block, next_in[rows:, where]], 0)
        next_out[:, where] = bands
        states = left_dot(back_ref[...], bands)
        low = jnp.concatenate([states[:count] + low_states[:, where], states[count:]], 0)
        put_joint(outs, where, low, high_states[:, where])


def own_back_kernel(low_in, high_in, next_in, next_t, time_t, out_ref):
    blocks = []
    for where in steps(low_in):
        low = low_in[:, where] + left_dot(next_t[...], next_in[:, where])
        high = high_in[:, where]
        for b in range(0, BLOCK, LANES):
            blocks.append(jnp.concatenate([low[:, b : b + LANES], high[:, b : b + LANES]], 1))
    for b, block in enumerate(time_synthesis(blocks, time_t[...])):
        out_ref[:, b * BLOCK : (b + 1) * BLOCK] = block


def final_kernel(own_ref, s0, s1, s2, time_t, state_t, scale_ref, out_ref):
    pairs, lows = [], []
    for start in range(0, s0.shape[1], LANES):
        low, high = take_joint((s0, s1, s2), slice(start, start + LANES))
        count = high.shape[0]
        pairs.append(jnp.concatenate([low[:count], high], 1))
        lows.append(low[count:])
    level0 = time_synthesis(pairs, time_t[...])
    level1 = synthesis_from_low(lows, low_rows(time_t))
    scale = scale_ref[...]
    for b in range(len(pairs)):
        where = slice(b * BLOCK, (b + 1) * BLOCK)
        states = jnp.concatenate([level0[b], level1[b]], 0)
        out_ref[:, where] = (own_ref[:, where] + left_dot(state_t[...], states)) * scale


def low_rows(time_t):
    count = time_t.shape[0] // BLOCK
    return jnp.concatenate([time_t[k * BLOCK : k * BLOCK + LANES] for k in range(count)], 0)


def last_kernel(level, thr_ref, timed_ref, own_ref, edge_ref, s0, s1, s2, back_ref, shrunk_ref, *state_outs):
    quarter = timed_ref.shape[0] // 4
    half = timed_ref.shape[1] // 2
    for start in range(0, 2 * half, BLOCK):
        where = slice(start, start + BLOCK)
        states = join_rows((s0, s1, s2), where)
        bands = left_dot(own_ref[...], timed_ref[:, where]) + left_dot(edge_ref[...], states)
        high = start >= half
        row = lax.broadcasted_iota(jnp.int32, bands.shape, 0)
        limit = jnp.full(bands.shape, thr_ref[level, 0] if high else 0.0, f32)
        for q in range(1, 4):
            limit = jnp.where(row >= q * quarter, thr_ref[level, 2 * q + int(high) - 1], limit)
        shrunk_ref[:, where] = shrink(bands, limit)
    put_states(shrunk_ref, back_ref, state_outs, BLOCK)


def rebuilt_blocks(shrunk, own_t, state_t, s0, s1, s2, time_t):
    half = shrunk.shape[1] // 2
    blocks = []
    for start in range(0, half, LANES):
        pair = []
        for base in (0, half):
            where = slice(base + start, base + start + LANES)
            pair.append((shrunk[:, where], join_rows((s0, s1, s2), where)))
        bands = jnp.concatenate([pair[0][0], pair[1][0]], 1)
        states = jnp.concatenate([pair[0][1], pair[1][1]], 1)
        blocks.append(left_dot(own_t[...], bands) + left_dot(state_t[...], states))
    return time_synthesis(blocks, time_t[...])


def call(kernel, outs, *args, smem=(), far=(), far_outs=(), scratch=(), after=(), cost=None):
    spaces = [pltpu.SMEM if i in smem else pltpu.HBM if i in far else pltpu.VMEM for i in range(len(args))]
    spaces += [pl.ANY] * len(after)
    count = len(args)

    def body(*refs):
        kernel(*refs[:count], *refs[count + len(after) :])

    return pl.pallas_call(
        body,
        out_shape=[jax.ShapeDtypeStruct(shape, dtype) for shape, dtype in outs],
        in_specs=[pl.BlockSpec(memory_space=space) for space in spaces],
        out_specs=[
            pl.BlockSpec(memory_space=pltpu.HBM if i in far_outs else pltpu.VMEM) for i in range(len(outs))
        ],
        scratch_shapes=list(scratch),
        compiler_params=pltpu.CompilerParams(vmem_limit_bytes=VMEM_LIMIT),
        cost_estimate=None
        if cost is None
        else pl.CostEstimate(flops=int(cost), bytes_accessed=0, transcendentals=0),
    )(*args, *after)


def shift(block, inline_by, cross_by):
    inline_devs, cross_devs = lax.axis_size("inl"), lax.axis_size("xl")
    if not cross_by:
        return lax.ppermute(block, "inl", [((i + inline_by) % inline_devs, i) for i in range(inline_devs)])
    if not inline_by:
        return lax.ppermute(block, "xl", [((j + cross_by) % cross_devs, j) for j in range(cross_devs)])
    route = [
        ((i + inline_by) % inline_devs * cross_devs + (j + cross_by) % cross_devs, i * cross_devs + j)
        for i in range(inline_devs)
        for j in range(cross_devs)
    ]
    return lax.ppermute(block, ("inl", "xl"), route)


def exchange(states, ahead):
    return [shift(states[0], ahead, 0), shift(states[1], 0, ahead), shift(states[2], ahead, ahead)]


def on_device(traces, dest_tile, bin_in_tile, fold, thresholds):
    devices = lax.axis_size("inl") * lax.axis_size("xl")
    trace_count, samples = traces.shape
    tile_rows, tile_cols = fold.shape
    bins = tile_rows * tile_cols
    width = SLOTS * samples // GROUP + LANES
    (outgoing,) = call(
        route_kernel,
        [((devices * GROUP, width), bf16)],
        dest_tile.reshape(1, trace_count),
        bin_in_tile.reshape(1, trace_count),
        traces,
        far=(0, 1, 2),
        far_outs=(0,),
        scratch=[
            pltpu.VMEM((1, trace_count), jnp.int32),
            pltpu.VMEM((1, trace_count), jnp.int32),
            pltpu.VMEM((trace_count, samples), bf16),
            pltpu.VMEM((devices * GROUP, width), bf16),
            pltpu.SemaphoreType.DMA((6,)),
            pltpu.SemaphoreType.DMA((4,)),
        ],
    )
    arrived = lax.all_to_all(
        outgoing.reshape(devices, GROUP, width), ("inl", "xl"), split_axis=0, concat_axis=0, tiled=True
    ).reshape(devices * GROUP, width)
    scale = (1.0 / jnp.sqrt(fold.astype(f32))).reshape(bins, 1)

    main, following = time_parts()
    time_matrix = np.concatenate([triple(main, 0), triple(following, 0)], 0)
    back_main, back_last = main.T, np.pad(following.T, ((0, 0), (0, BLOCK - LANES)))
    time_back = np.concatenate([triple(back_main, 0), triple(back_last, 0)], 0)
    time_back_low = np.concatenate([triple(back_main[:LANES], 0), triple(back_last[:LANES], 0)], 0)
    half, rows2, cols2 = samples // 2, tile_rows // 4, tile_cols // 4
    quarter, last = bins // 4, bins // 16
    own0, edge0, own1, edge1, states01, sizes = joint_matrices(tile_rows, tile_cols)
    own2, edge2, states2, sizes2 = tile_parts(rows2, cols2)
    count0 = sum(sizes[:3])
    joint_shapes = [
        ((2 * sizes[0] + sizes[3], half), f32),
        ((2 * sizes[1] + sizes[4], half), f32),
        ((2 * sizes[2], half), f32),
    ]
    shapes2 = [((size, samples // 4), f32) for size in sizes2]

    summed, *states = call(
        bin_kernel,
        [((bins, samples), f32)] + joint_shapes,
        arrived,
        scale,
        time_matrix,
        triple(states01, 1),
        far=(0, 2, 3),
        scratch=[
            pltpu.VMEM((devices * GROUP, width), bf16),
            pltpu.VMEM(time_matrix.shape, bf16),
            pltpu.VMEM((sum(sizes), 3 * bins), bf16),
            pltpu.SemaphoreType.DMA((6,)),
        ],
    )
    states = exchange(states, 1)
    own_low, own_high, own_next = call(
        own_kernel,
        [((bins, half), f32)] * 2 + [((quarter, half), f32)],
        summed,
        time_matrix,
        triple(own0, 1),
        triple(own1, 1),
        cost=8e9,
    )
    shrunk1, timed, *states2_out = call(
        middle_kernel,
        [((quarter, half), f32), ((last, half // 2), f32)] + shapes2,
        thresholds,
        own_next,
        triple(edge1, 1),
        *states,
        time_matrix,
        triple(states2, 1),
        smem=(0,),
    )
    ahead = exchange(states2_out, 1)
    low_details, high_details, low_states, high_states = call(
        details_kernel,
        [((bins - quarter, half), f32), ((bins, half), f32)] + [((count0, half), f32)] * 2,
        thresholds,
        own_low,
        own_high,
        triple(edge0, 1),
        *states,
        triple(edge0[quarter:].T, 1),
        triple(edge0.T, 1),
        smem=(0,),
        after=(timed,),
        cost=6e9,
    )
    shrunk2, *states2_out = call(
        functools.partial(last_kernel, 2),
        [((last, half // 2), f32)] + shapes2,
        thresholds,
        timed,
        triple(own2, 1),
        triple(edge2, 1),
        *ahead,
        triple(edge2.T, 1),
        smem=(0,),
        after=(low_details,),
    )
    behind = exchange(states2_out, -1)
    spread_low, spread_high, spread_next = call(
        spread_kernel,
        [((bins, half), f32)] * 2 + [((quarter, half), f32)],
        low_details,
        high_details,
        triple(own0[quarter:].T, 1),
        triple(own0.T, 1),
        shrunk1,
        time_back,
        after=(shrunk2,),
        cost=6e9,
    )
    bands1, *states = call(
        rejoin_kernel,
        [((quarter, half), f32)] + joint_shapes,
        shrunk2,
        triple(own2.T, 1),
        triple(states2.T, 1),
        *behind,
        time_back,
        time_back_low,
        spread_next,
        low_states,
        high_states,
        triple(edge1.T, 1),
    )
    states = exchange(states, -1)
    (own_back,) = call(
        own_back_kernel,
        [((bins, samples), f32)],
        spread_low,
        spread_high,
        bands1,
        triple(own1.T, 1),
        time_back,
        cost=6e9,
    )
    (denoised,) = call(
        final_kernel,
        [((bins, samples), f32)],
        own_back,
        *states,
        time_back,
        triple(states01.T, 1),
        scale,
    )
    return denoised.reshape(tile_rows, tile_cols, samples)


def solution(mesh):
    placed = (P(("inl", "xl"), None), P(("inl", "xl"), None), P(("inl", "xl")), P("inl", "xl"), P())
    return jax.shard_map(
        on_device, mesh=mesh, in_specs=placed, out_specs=P("inl", "xl", None), check_vma=False
    )
```

time: 161 us -> 139 us (0.86)
  waiting for transfers between devices: 91.3 us -> 74.2 us
  starting transfers between devices: 26.5 us -> 22.1 us
    ppermute x6 -> x4, waiting for transfers between devices: 41.2 us -> 12.7 us  [shift(): return lax.ppermute(block, ('inl', 'xl'), route)]
    ppermute x6 -> x4, waiting for transfers between devices: 0.26 us -> 17.4 us  [shift(): lax.ppermute(block, 'inl', [((i + inline_by) % inline_devs, i) for i in r...]
    ppermute x6 -> x4, starting transfers between devices: 9.13 us -> 0.73 us  [shift(): lax.ppermute(block, 'inl', [((i + inline_by) % inline_devs, i) for i in r...]
    ppermute x6 -> x4, starting transfers between devices: 1 us -> 8.25 us  [shift(): return lax.ppermute(block, ('inl', 'xl'), route)]
    ppermute x6 -> x4, waiting for transfers between devices: 5.73 us -> 0.44 us  [shift(): lax.ppermute(block, 'xl', [((j + cross_by) % cross_devs, j) for j in rang...]
    ppermute x6 -> x4, starting transfers between devices: 4.78 us -> 1.93 us  [shift(): lax.ppermute(block, 'xl', [((j + cross_by) % cross_devs, j) for j in rang...]
    unnamed x56 -> x58, local copies, waits for them, and re-layouts: 8.06 us -> 6.05 us
    pallas_call x9 -> x10, Pallas kernels: 34.7 us -> 34 us  [call(): pl.pallas_call(body, out_shape=[jax.ShapeDtypeStruct(shape, dtype) for sh...]
  transfers between devices with their start and end apart: 19 -> 13, of which waited for: 10 -> 7; matrix products, arithmetic and copies ran while one was open for 0% -> 1% of each run, Pallas kernels for 3% -> 10%
where the time goes in v1:
time: 139 us; the launch traced here: 137 us
  waiting for transfers between devices  74.2 us (53%)
  Pallas kernels  34 us (24%)
  starting transfers between devices  22.1 us (16%)
  local copies, waits for them, and re-layouts  6.84 us (5%)
    all_to_all x1, waiting for transfers between devices, on_device(): lax.all_to_all(outgoing.reshape(devices, GROUP, width), ('inl', 'xl'), sp...  43.7 us
    pallas_call x10, Pallas kernels, call(): pl.pallas_call(body, out_shape=[jax.ShapeDtypeStruct(shape, dtype) for sh...  34 us
    ppermute x4, waiting for transfers between devices, shift(): lax.ppermute(block, 'inl', [((i + inline_by) % inline_devs, i) for i in r...  17.4 us
    ppermute x4, waiting for transfers between devices, shift(): return lax.ppermute(block, ('inl', 'xl'), route)  12.7 us
    all_to_all x1, starting transfers between devices, on_device(): lax.all_to_all(outgoing.reshape(devices, GROUP, width), ('inl', 'xl'), sp...  11.1 us
    ppermute x4, starting transfers between devices, shift(): return lax.ppermute(block, ('inl', 'xl'), route)  8.25 us
    unnamed x58, local copies, waits for them, and re-layouts  6.05 us
  transfers between devices with their start and end apart: 13, of which 7 were waited for; matrix products, arithmetic and copies ran while one was open for 1% of the time, Pallas kernels for 10%

profile of v1, /device:TPU:0, one launch (start us, length us, event | category | flops | bytes accessed | tf_op | source)
XLA Modules:
  0.0 137.5 jit_solution(14602257994444267696)
XLA Ops:
  0.0 1.6 %copy-done.3 = bf16[512,2048]{1,0:T(8,128)(2,1)S(1)} copy-done((bf16[512,2048]{1,0:T(8,128)(2,1)S(1)}, bf16[512,2048]{1,0:T(8,128)(2,1)}, u32[]{:S(2)}) %copy-start.3) | copy-done | bytes 2097176
  1.6 0.7 copy-done.18
  2.3 0.7 copy-done.19
  3.0 6.6 %shard_map.244 = bf16[1024,1664]{1,0:T(8,128)(2,1)} custom-call(s32[1,512]{1,0:T(1,128)S(1)} %bitcast.6, s32[1,512]{1,0:T(1,128)S(1)} %bitcast.7, bf16[512,2048]{1,0:T(8,128)(2,1)S(1)} %copy-done.3), custom_call_target="tpu_custom_call" | custom-call | tf_op jit(solution)/shard_map/pallas_call | solution.py:497
  9.5 0.0 copy-start.28
  9.5 11.1 %all-to-all-start = ((bf16[128,8,1664]{2,1,0:T(8,128)(2,1)}), bf16[128,8,1664]{2,1,0:T(8,128)(2,1)S(1)}, u32[]{:S(2)}, u32[]{:S(2)}) async-start(bf16[128,8,1664]{2,1,0:T(8,128)(2,1)} %bitcast.2), calls=%async_computation | async-start | bytes 6815744 | tf_op jit(solution)/shard_map/all_to_all | solution.py:553
  20.7 0.8 reshape.24.refs_1_.refs_6_
  21.5 43.7 %all-to-all-done = bf16[128,8,1664]{2,1,0:T(8,128)(2,1)S(1)} async-done(((bf16[128,8,1664]{2,1,0:T(8,128)(2,1)}), bf16[128,8,1664]{2,1,0:T(8,128)(2,1)S(1)}, u32[]{:S(2)}, u32[]{:S(2)}) %all-to-all-start) | async-done | bytes 3407904 | tf_op jit(solution)/shard_map/all_to_all | solution.py:553
  65.2 1.1 copy-done.1
  66.3 0.9 copy-done.4
  67.2 1.0 copy-done.8
  68.2 5.8 %shard_map.245 = (f32[384,2048]{1,0:T(8,128)S(1)}, f32[120,1024]{1,0:T(8,128)S(1)}, f32[80,1024]{1,0:T(8,128)S(1)}, f32[32,1024]{1,0:T(8,128)S(1)}) custom-call(bf16[1024,1664]{1,0:T(8,128)(2,1)S(1)} %bitcast.5, f32[384,1]{1,0:T(8,128)S(1)} %copy-done.4, bf16[1152,256]{1,0:T(8,128)(2,1)S(1)} %copy-done.1, bf16[136,1152]{1,0:T(8,128)(2,1)S(1)} %copy-done.8), custom_call_target="tpu_custom_call" | custom-call | tf_op jit(solution)/shard_map/pallas_call | solution.py:497
  74.0 0.5 collective-permute-start.2
  74.6 1.2 collective-permute-start.1
  75.8 0.3 collective-permute-start
  76.1 0.0 copy-done.2
  76.1 0.0 copy-start.12
  76.1 0.0 copy-start.13
  76.1 0.0 copy-start.24
  76.1 0.0 copy-start.25
  76.1 0.0 copy-start.27
  76.2 4.6 %shard_map.246 = (f32[384,1024]{1,0:T(8,128)S(1)}, f32[384,1024]{1,0:T(8,128)S(1)}, f32[96,1024]{1,0:T(8,128)S(1)}) custom-call(f32[384,2048]{1,0:T(8,128)S(1)} %get-tuple-element.32.refs_0_, bf16[1152,256]{1,0:T(8,128)(2,1)S(1)} %copy-done.2, bf16[384,1152]{1,0:T(8,128)(2,1)S(1)} %copy-done.21, bf16[96,1152]{1,0:T(8,128)(2,1)S(1)} %copy-done.26), custom_call_target="tpu_custom_call" | custom-call | flops 8000000000 | tf_op jit(solution)/shard_map/pallas_call | solution.py:497
  80.8 0.0 collective-permute-done.2.refs_5_.refs_6_
  80.8 0.4 collective-permute-done.1.refs_4_.refs_5_
  81.2 8.7 %collective-permute-done.refs_3_.refs_4_ = f32[120,1024]{1,0:T(8,128)S(1)} collective-permute-done((f32[120,1024]{1,0:T(8,128)S(1)}, f32[120,1024]{1,0:T(8,128)S(1)}, u32[]{:S(2)}, u32[]{:S(2)}) %collective-permute-start) | collective-permute-done | bytes 491552 | tf_op jit(solution)/shard_map/ppermute | solution.py:515
  89.9 0.0 copy-done.10
  90.0 0.0 copy-done.13
  90.0 1.6 %shard_map.247 = (f32[96,1024]{1,0:T(8,128)S(1)}, f32[24,512]{1,0:T(8,128)S(1)}, f32[16,512]{1,0:T(8,128)S(1)}, f32[8,512]{1,0:T(8,128)S(1)}, f32[8,512]{1,0:T(8,128)S(1)}) custom-call(f32[3,7]{1,0:T(4,128)S(1)} %copy-done.13, f32[96,1024]{1,0:T(8,128)S(1)} %get-tuple-element.38.refs_1_, bf16[96,408]{1,0:T(8,128)(2,1)S(1)} %copy-done.10, ...), custom_call_target="tpu_custom_call" | custom-call | tf_op jit(solution)/shard_map/pallas_call | solution.py:497
  91.6 0.6 collective-permute-start.4
  92.2 5.5 %collective-permute-start.5 = (f32[8,512]{1,0:T(8,128)S(1)}, f32[8,512]{1,0:T(8,128)S(1)}, u32[]{:S(2)}, u32[]{:S(2)}) collective-permute-start(f32[8,512]{1,0:T(8,128)S(1)} %get-tuple-element.45), channel_id=1, source_target_pairs={{9,0},{10,1},{11,2},{12,3},{13,4},{14,5},{15,6},{8,7},{17,8},{18,9... | collective-permute-start | bytes 49160 | tf_op jit(solution)/shard_map/ppermute | solution.py:523
  97.7 0.1 collective-permute-start.3
  97.8 0.0 copy-start.14
  97.8 0.0 copy-start.15
  97.9 0.0 copy-start
  97.9 0.0 copy-start.20
  97.9 0.0 copy-start.22
  97.9 3.6 %shard_map.248 = (f32[288,1024]{1,0:T(8,128)S(1)}, f32[384,1024]{1,0:T(8,128)S(1)}, f32[96,1024]{1,0:T(8,128)S(1)}, f32[96,1024]{1,0:T(8,128)S(1)}) custom-call(f32[3,7]{1,0:T(4,128)S(1)} %copy-done.13, f32[384,1024]{1,0:T(8,128)S(1)} %get-tuple-element.33.refs_1_, f32[384,1024]{1,0:T(8,128)S(1)} %get-tuple-element.34.refs_2_, ...), custom_call_target="tpu_custom_call" | custom-call | flops 6000000000 | tf_op jit(solution)/shard_map/pallas_call | solution.py:497
  101.6 0.0 collective-permute-done.4.refs_5_
  101.6 0.0 collective-permute-done.5.refs_6_
  101.6 0.0 collective-permute-done.3.refs_4_
  101.6 0.8 shard_map.249
  102.5 0.1 collective-permute-start.7
  102.6 2.1 %collective-permute-start.8 = (f32[8,512]{1,0:T(8,128)S(1)}, f32[8,512]{1,0:T(8,128)S(1)}, u32[]{:S(2)}, u32[]{:S(2)}) collective-permute-start(f32[8,512]{1,0:T(8,128)S(1)} %get-tuple-element.51), channel_id=1, source_target_pairs={{127,0},{120,1},{121,2},{122,3},{123,4},{124,5},{125,6},{126,7},{7... | collective-permute-start | bytes 49160 | tf_op jit(solution)/shard_map/ppermute | solution.py:523
  104.7 0.0 collective-permute-start.6
  104.7 0.0 copy-start.7
  104.8 0.0 copy-start.9
  104.8 0.0 copy-start.16
  104.8 0.0 copy-start.17
  104.8 2.5 %shard_map.250 = (f32[384,1024]{1,0:T(8,128)S(1)}, f32[384,1024]{1,0:T(8,128)S(1)}, f32[96,1024]{1,0:T(8,128)S(1)}) custom-call(f32[288,1024]{1,0:T(8,128)S(1)} %get-tuple-element.40.refs_8_.refs_0_, f32[384,1024]{1,0:T(8,128)S(1)} %get-tuple-element.41.refs_1_, bf16[384,864]{1,0:T(8,128)(2,1)S(1)} %copy-done.22, bf16[384,1152]{1,0:T(8,128)(2,1)S(1)} %copy-done.20, ...), custom_call_target="tpu_custom_call" | custom-call | flops 6000000000 | tf_op jit(solution)/shard_map/pallas_call | solution.py:497
  107.3 0.0 copy-start.23
  107.3 0.0 collective-permute-done.7.refs_4_
  107.3 3.8 %collective-permute-done.8.refs_5_ = f32[8,512]{1,0:T(8,128)S(1)} collective-permute-done((f32[8,512]{1,0:T(8,128)S(1)}, f32[8,512]{1,0:T(8,128)S(1)}, u32[]{:S(2)}, u32[]{:S(2)}) %collective-permute-start.8) | collective-permute-done | bytes 16416 | tf_op jit(solution)/shard_map/ppermute | solution.py:523
  111.2 0.8 collective-permute-done.6.refs_3_
  112.0 1.1 shard_map.251
  113.1 0.1 collective-permute-start.11
  113.2 0.0 collective-permute-start.10
  113.2 0.3 collective-permute-start.9
  113.5 0.0 copy-start.5
  113.5 0.0 copy-start.6
  113.5 3.0 %shard_map.252.refs_0_ = f32[384,2048]{1,0:T(8,128)S(1)} custom-call(f32[384,1024]{1,0:T(8,128)S(1)} %get-tuple-element.47.refs_0_, f32[384,1024]{1,0:T(8,128)S(1)} %get-tuple-element.48.refs_1_, f32[96,1024]{1,0:T(8,128)S(1)} %get-tuple-element.55.refs_2_, bf16[384,288]{1,0:T(8,128)(2,1)S(1)} %copy-done.23, bf16[1536,256]{1,0:T(8,128)(2,1)S(1)} %copy-done), custom_call_target="tpu_custom_call" | custom-call | flops 6000000000 | tf_op jit(solution)/shard_map/pallas_call | solution.py:497
  116.5 8.8 %collective-permute-done.11.refs_3_ = f32[32,1024]{1,0:T(8,128)S(1)} collective-permute-done((f32[32,1024]{1,0:T(8,128)S(1)}, f32[32,1024]{1,0:T(8,128)S(1)}, u32[]{:S(2)}, u32[]{:S(2)}) %collective-permute-start.11) | collective-permute-done | bytes 131104 | tf_op jit(solution)/shard_map/ppermute | solution.py:523
  125.4 0.0 collective-permute-done.10.refs_2_
  125.4 7.9 %collective-permute-done.9.refs_1_ = f32[120,1024]{1,0:T(8,128)S(1)} collective-permute-done((f32[120,1024]{1,0:T(8,128)S(1)}, f32[120,1024]{1,0:T(8,128)S(1)}, u32[]{:S(2)}, u32[]{:S(2)}) %collective-permute-start.9) | collective-permute-done | bytes 491552 | tf_op jit(solution)/shard_map/ppermute | solution.py:515
  133.3 4.2 %shard_map.253 = f32[384,2048]{1,0:T(8,128)} custom-call(f32[384,2048]{1,0:T(8,128)S(1)} %shard_map.252.refs_0_, f32[120,1024]{1,0:T(8,128)S(1)} %collective-permute-done.9.refs_1_, f32[80,1024]{1,0:T(8,128)S(1)} %collective-permute-done.10.refs_2_, f32[32,1024]{1,0:T(8,128)S(1)} %collective-permute-done.11.refs_3_, bf16[1536,256]{1,0:T(8,128)(2,1)S(1)} %copy-done, ...), custom_call_target="tpu_custom_call" | custom-call | tf_op jit(solution)/shard_map/pallas_call | solution.py:497
  (32 shorter events, 0.1 us)
Async XLA Ops:
  0.0 1.6 %copy-start.3 = (bf16[512,2048]{1,0:T(8,128)(2,1)S(1)}, bf16[512,2048]{1,0:T(8,128)(2,1)}, u32[]{:S(2)}) copy-start(bf16[512,2048]{1,0:T(8,128)(2,1)} %refs_2_.7) | copy-start | bytes 6291460
  1.6 0.7 copy-start.18
  2.3 0.7 copy-start.19
  9.5 11.2 %copy-start.28 = (s32[16,24]{1,0:T(8,128)S(1)}, s32[16,24]{1,0:T(8,128)}, u32[]{:S(2)}) copy-start(s32[16,24]{1,0:T(8,128)} %param.29) | copy-start | bytes 4612
  9.5 55.7 %all-to-all-start = ((bf16[128,8,1664]{2,1,0:T(8,128)(2,1)}), bf16[128,8,1664]{2,1,0:T(8,128)(2,1)S(1)}, u32[]{:S(2)}, u32[]{:S(2)}) async-start(bf16[128,8,1664]{2,1,0:T(8,128)(2,1)} %bitcast.2), calls=%async_computation | async-start | bytes 6815744 | tf_op jit(solution)/shard_map/all_to_all | solution.py:553
  65.2 1.1 copy-start.1
  66.3 0.9 copy-start.4
  67.2 1.0 copy-start.8
  68.2 7.9 %copy-start.2 = (bf16[1152,256]{1,0:T(8,128)(2,1)S(1)}, bf16[1152,256]{1,0:T(8,128)(2,1)}, u32[]{:S(2)}) copy-start(bf16[1152,256]{1,0:T(8,128)(2,1)} %constant.21.clone.refs_2_.refs_1_.refs_6_) | copy-start | bytes 1769476
  68.2 7.9 %copy-start.21 = (bf16[384,1152]{1,0:T(8,128)(2,1)S(1)}, bf16[384,1152]{1,0:T(8,128)(2,1)}, u32[]{:S(2)}) copy-start(bf16[384,1152]{1,0:T(8,128)(2,1)} %constant.45.clone.refs_2_) | copy-start | bytes 2654212
  68.2 7.9 %copy-start.26 = (bf16[96,1152]{1,0:T(8,128)(2,1)S(1)}, bf16[96,1152]{1,0:T(8,128)(2,1)}, u32[]{:S(2)}) copy-start(bf16[96,1152]{1,0:T(8,128)(2,1)} %constant.46.clone.refs_3_) | copy-start | bytes 663556
  74.0 6.8 %collective-permute-start.2 = (f32[32,1024]{1,0:T(8,128)S(1)}, f32[32,1024]{1,0:T(8,128)S(1)}, u32[]{:S(2)}, u32[]{:S(2)}) collective-permute-start(f32[32,1024]{1,0:T(8,128)S(1)} %get-tuple-element.37), channel_id=1, source_target_pairs={{9,0},{10,1},{11,2},{12,3},{13,4},{14,5},{15,6},{8,7},{17,8},{18,9... | collective-permute-start | bytes 393224 | tf_op jit(solution)/shard_map/ppermute | solution.py:523
  74.6 6.7 %collective-permute-start.1 = (f32[80,1024]{1,0:T(8,128)S(1)}, f32[80,1024]{1,0:T(8,128)S(1)}, u32[]{:S(2)}, u32[]{:S(2)}) collective-permute-start(f32[80,1024]{1,0:T(8,128)S(1)} %get-tuple-element.36), channel_id=1, source_target_pairs={{1,0},{2,1},{3,2},{4,3},{5,4},{6,5},{7,6},{0,7},{9,8},{10,9},{11,1... | collective-permute-start | bytes 983048 | tf_op jit(solution)/shard_map/ppermute | solution.py:517
  75.8 14.2 %collective-permute-start = (f32[120,1024]{1,0:T(8,128)S(1)}, f32[120,1024]{1,0:T(8,128)S(1)}, u32[]{:S(2)}, u32[]{:S(2)}) collective-permute-start(f32[120,1024]{1,0:T(8,128)S(1)} %get-tuple-element.35), channel_id=1, source_target_pairs={{8,0},{16,8},{24,16},{32,24},{40,32},{48,40},{56,48},{64,56},{72,6... | collective-permute-start | bytes 1474568 | tf_op jit(solution)/shard_map/ppermute | solution.py:515
  76.1 13.9 %copy-start.10 = (bf16[96,408]{1,0:T(8,128)(2,1)S(1)}, bf16[96,408]{1,0:T(8,128)(2,1)}, u32[]{:S(2)}) copy-start(bf16[96,408]{1,0:T(8,128)(2,1)} %constant.47.clone.refs_2_) | copy-start | bytes 235012
  76.1 13.9 %copy-start.12 = (bf16[32,72]{1,0:T(8,128)(2,1)S(1)}, bf16[32,72]{1,0:T(8,128)(2,1)}, u32[]{:S(2)}) copy-start(bf16[32,72]{1,0:T(8,128)(2,1)} %constant.48.clone.refs_7_) | copy-start | bytes 13828
  76.1 13.9 %copy-start.13 = (f32[3,7]{1,0:T(4,128)S(1)}, f32[3,7]{1,0:T(4,128)}, u32[]{:S(2)}) copy-start(f32[3,7]{1,0:T(4,128)} %refs_0_.5) | copy-start | bytes 256
  76.1 21.7 %copy-start.24 = (bf16[384,288]{1,0:T(8,128)(2,1)S(1)}, bf16[384,288]{1,0:T(8,128)(2,1)}, u32[]{:S(2)}) copy-start(bf16[384,288]{1,0:T(8,128)(2,1)} %constant.49.clone.refs_3_) | copy-start | bytes 663556
  76.1 21.7 %copy-start.25 = (bf16[96,1152]{1,0:T(8,128)(2,1)S(1)}, bf16[96,1152]{1,0:T(8,128)(2,1)}, u32[]{:S(2)}) copy-start(bf16[96,1152]{1,0:T(8,128)(2,1)} %constant.51.clone.refs_8_) | copy-start | bytes 663556
  76.1 21.7 %copy-start.27 = (bf16[96,864]{1,0:T(8,128)(2,1)S(1)}, bf16[96,864]{1,0:T(8,128)(2,1)}, u32[]{:S(2)}) copy-start(bf16[96,864]{1,0:T(8,128)(2,1)} %constant.50.clone.refs_7_) | copy-start | bytes 497668
  91.6 10.0 %collective-permute-start.4 = (f32[8,512]{1,0:T(8,128)S(1)}, f32[8,512]{1,0:T(8,128)S(1)}, u32[]{:S(2)}, u32[]{:S(2)}) collective-permute-start(f32[8,512]{1,0:T(8,128)S(1)} %get-tuple-element.44), channel_id=1, source_target_pairs={{1,0},{2,1},{3,2},{4,3},{5,4},{6,5},{7,6},{0,7},{9,8},{10,9},{11,1... | collective-permute-start | bytes 49160 | tf_op jit(solution)/shard_map/ppermute | solution.py:517
  92.2 9.4 %collective-permute-start.5 = (f32[8,512]{1,0:T(8,128)S(1)}, f32[8,512]{1,0:T(8,128)S(1)}, u32[]{:S(2)}, u32[]{:S(2)}) collective-permute-start(f32[8,512]{1,0:T(8,128)S(1)} %get-tuple-element.45), channel_id=1, source_target_pairs={{9,0},{10,1},{11,2},{12,3},{13,4},{14,5},{15,6},{8,7},{17,8},{18,9... | collective-permute-start | bytes 49160 | tf_op jit(solution)/shard_map/ppermute | solution.py:523
  97.7 3.9 %collective-permute-start.3 = (f32[16,512]{1,0:T(8,128)S(1)}, f32[16,512]{1,0:T(8,128)S(1)}, u32[]{:S(2)}, u32[]{:S(2)}) collective-permute-start(f32[16,512]{1,0:T(8,128)S(1)} %get-tuple-element.43), channel_id=1, source_target_pairs={{8,0},{16,8},{24,16},{32,24},{40,32},{48,40},{56,48},{64,56},{72,6... | collective-permute-start | bytes 98312 | tf_op jit(solution)/shard_map/ppermute | solution.py:515
  97.8 3.8 %copy-start.11 = (bf16[32,72]{1,0:T(8,128)(2,1)S(1)}, bf16[32,72]{1,0:T(8,128)(2,1)}, u32[]{:S(2)}) copy-start(bf16[32,72]{1,0:T(8,128)(2,1)} %constant.54.clone.refs_7_) | copy-start | bytes 13828
  97.8 3.8 %copy-start.14 = (bf16[24,96]{1,0:T(8,128)(2,1)S(1)}, bf16[24,96]{1,0:T(8,128)(2,1)}, u32[]{:S(2)}) copy-start(bf16[24,96]{1,0:T(8,128)(2,1)} %constant.53.clone.refs_3_) | copy-start | bytes 13828
  97.8 3.8 %copy-start.15 = (bf16[24,72]{1,0:T(8,128)(2,1)S(1)}, bf16[24,72]{1,0:T(8,128)(2,1)}, u32[]{:S(2)}) copy-start(bf16[24,72]{1,0:T(8,128)(2,1)} %constant.52.clone.refs_2_) | copy-start | bytes 10372
  97.9 6.9 %copy-start = (bf16[1536,256]{1,0:T(8,128)(2,1)S(1)}, bf16[1536,256]{1,0:T(8,128)(2,1)}, u32[]{:S(2)}) copy-start(bf16[1536,256]{1,0:T(8,128)(2,1)} %constant.57.clone.refs_5_.refs_6_.refs_4_) | copy-start | bytes 2359300
  97.9 6.9 %copy-start.20 = (bf16[384,1152]{1,0:T(8,128)(2,1)S(1)}, bf16[384,1152]{1,0:T(8,128)(2,1)}, u32[]{:S(2)}) copy-start(bf16[384,1152]{1,0:T(8,128)(2,1)} %constant.56.clone.refs_3_) | copy-start | bytes 2654212
  97.9 6.8 %copy-start.22 = (bf16[384,864]{1,0:T(8,128)(2,1)S(1)}, bf16[384,864]{1,0:T(8,128)(2,1)}, u32[]{:S(2)}) copy-start(bf16[384,864]{1,0:T(8,128)(2,1)} %constant.55.clone.refs_2_) | copy-start | bytes 1990660
  102.5 4.9 %collective-permute-start.7 = (f32[8,512]{1,0:T(8,128)S(1)}, f32[8,512]{1,0:T(8,128)S(1)}, u32[]{:S(2)}, u32[]{:S(2)}) collective-permute-start(f32[8,512]{1,0:T(8,128)S(1)} %get-tuple-element.50), channel_id=1, source_target_pairs={{7,0},{0,1},{1,2},{2,3},{3,4},{4,5},{5,6},{6,7},{15,8},{8,9},{9,10... | collective-permute-start | bytes 49160 | tf_op jit(solution)/shard_map/ppermute | solution.py:517
  102.6 8.6 %collective-permute-start.8 = (f32[8,512]{1,0:T(8,128)S(1)}, f32[8,512]{1,0:T(8,128)S(1)}, u32[]{:S(2)}, u32[]{:S(2)}) collective-permute-start(f32[8,512]{1,0:T(8,128)S(1)} %get-tuple-element.51), channel_id=1, source_target_pairs={{127,0},{120,1},{121,2},{122,3},{123,4},{124,5},{125,6},{126,7},{7... | collective-permute-start | bytes 49160 | tf_op jit(solution)/shard_map/ppermute | solution.py:523
  104.7 7.2 %collective-permute-start.6 = (f32[16,512]{1,0:T(8,128)S(1)}, f32[16,512]{1,0:T(8,128)S(1)}, u32[]{:S(2)}, u32[]{:S(2)}) collective-permute-start(f32[16,512]{1,0:T(8,128)S(1)} %get-tuple-element.49), channel_id=1, source_target_pairs={{120,0},{0,8},{8,16},{16,24},{24,32},{32,40},{40,48},{48,56},{56,6... | collective-permute-start | bytes 98312 | tf_op jit(solution)/shard_map/ppermute | solution.py:515
  104.7 7.2 %copy-start.7 = (bf16[768,256]{1,0:T(8,128)(2,1)S(1)}, bf16[768,256]{1,0:T(8,128)(2,1)}, u32[]{:S(2)}) copy-start(bf16[768,256]{1,0:T(8,128)(2,1)} %constant.60.clone.refs_7_) | copy-start | bytes 1179652
  104.8 7.2 %copy-start.9 = (bf16[136,288]{1,0:T(8,128)(2,1)S(1)}, bf16[136,288]{1,0:T(8,128)(2,1)}, u32[]{:S(2)}) copy-start(bf16[136,288]{1,0:T(8,128)(2,1)} %constant.61.clone.refs_11_) | copy-start | bytes 235012
  104.8 7.2 %copy-start.16 = (bf16[24,96]{1,0:T(8,128)(2,1)S(1)}, bf16[24,96]{1,0:T(8,128)(2,1)}, u32[]{:S(2)}) copy-start(bf16[24,96]{1,0:T(8,128)(2,1)} %constant.59.clone.refs_2_) | copy-start | bytes 13828
  104.8 7.2 %copy-start.17 = (bf16[24,72]{1,0:T(8,128)(2,1)S(1)}, bf16[24,72]{1,0:T(8,128)(2,1)}, u32[]{:S(2)}) copy-start(bf16[24,72]{1,0:T(8,128)(2,1)} %constant.58.clone.refs_1_) | copy-start | bytes 10372
  107.3 6.2 %copy-start.23 = (bf16[384,288]{1,0:T(8,128)(2,1)S(1)}, bf16[384,288]{1,0:T(8,128)(2,1)}, u32[]{:S(2)}) copy-start(bf16[384,288]{1,0:T(8,128)(2,1)} %constant.62.clone.refs_3_) | copy-start | bytes 663556
  113.1 12.3 %collective-permute-start.11 = (f32[32,1024]{1,0:T(8,128)S(1)}, f32[32,1024]{1,0:T(8,128)S(1)}, u32[]{:S(2)}, u32[]{:S(2)}) collective-permute-start(f32[32,1024]{1,0:T(8,128)S(1)} %get-tuple-element.58), channel_id=1, source_target_pairs={{127,0},{120,1},{121,2},{122,3},{123,4},{124,5},{125,6},{126,7},{7... | collective-permute-start | bytes 393224 | tf_op jit(solution)/shard_map/ppermute | solution.py:523
  113.2 12.2 %collective-permute-start.10 = (f32[80,1024]{1,0:T(8,128)S(1)}, f32[80,1024]{1,0:T(8,128)S(1)}, u32[]{:S(2)}, u32[]{:S(2)}) collective-permute-start(f32[80,1024]{1,0:T(8,128)S(1)} %get-tuple-element.57), channel_id=1, source_target_pairs={{7,0},{0,1},{1,2},{2,3},{3,4},{4,5},{5,6},{6,7},{15,8},{8,9},{9,10... | collective-permute-start | bytes 983048 | tf_op jit(solution)/shard_map/ppermute | solution.py:517
  113.2 20.1 %collective-permute-start.9 = (f32[120,1024]{1,0:T(8,128)S(1)}, f32[120,1024]{1,0:T(8,128)S(1)}, u32[]{:S(2)}, u32[]{:S(2)}) collective-permute-start(f32[120,1024]{1,0:T(8,128)S(1)} %get-tuple-element.56), channel_id=1, source_target_pairs={{120,0},{0,8},{8,16},{16,24},{24,32},{32,40},{40,48},{48,56},{56,6... | collective-permute-start | bytes 1474568 | tf_op jit(solution)/shard_map/ppermute | solution.py:515
  113.5 19.8 %copy-start.5 = (f32[384,1]{1,0:T(8,128)S(1)}, f32[384,1]{1,0:T(8,128)}, u32[]{:S(2)}) copy-start(f32[384,1]{1,0:T(8,128)} %reshape.24.refs_1_.refs_6_) | copy-start | bytes 4612
  113.5 19.8 %copy-start.6 = (bf16[384,408]{1,0:T(8,128)(2,1)S(1)}, bf16[384,408]{1,0:T(8,128)(2,1)}, u32[]{:S(2)}) copy-start(bf16[384,408]{1,0:T(8,128)(2,1)} %constant.63.clone.refs_5_) | copy-start | bytes 940036

commit v2 on v1

--- a/solution.py
+++ b/solution.py
@@ -15,6 +15,9 @@
 LANES = 128
 BLOCK = 256
 VMEM_LIMIT = 32 * 1024 * 1024
+LARGE_LIMIT = 62 * 1024 * 1024
+MIDDLE_LIMIT = 48 * 1024 * 1024
+SIDE = 4
 
 low_taps = [
     0.0352262918857095,
@@ -85,20 +88,21 @@
     i, c = two_levels(rows), two_levels(cols)
     wide = [np.concatenate([d["edge0"], np.zeros_like(d["edge0"])], 1) for d in (i, c)]
     both = [np.concatenate([d["far1"], d["edge1"]], 1) for d in (i, c)]
+    first = [0, 1, 4, 5] + [k for k in range(16) if k not in (0, 1, 4, 5)]
     own0 = outer(i["own0"], c["own0"], True)
-    edge0 = [outer(i["edge0"], c["own0"], True), outer(i["own0"], c["edge0"], True), outer(*wide, True)]
+    edge0 = [outer(i["edge0"], c["own0"], True), outer(i["own0"], c["edge0"], True), outer(*wide, True)[:, first]]
     own1 = outer(i["own1"], c["own1"], True)
     edge1 = [
         outer(i["far1"], c["own1"], True),
         outer(i["own1"], c["far1"], True),
-        outer(*both, True),
+        outer(*both, True)[:, first],
         outer(i["edge1"], np.eye(cols // 2), True),
         outer(np.eye(rows // 2), c["edge1"], True),
     ]
     states = [
         outer(i["state0"], np.eye(cols), False),
         outer(np.eye(rows), c["state0"], False),
-        outer(i["states"], c["states"], False),
+        outer(i["states"], c["states"], False)[first],
         outer(i["further"], c["own1"], False),
         outer(i["own1"], c["further"], False),
     ]
@@ -106,22 +110,31 @@
     return own0, np.concatenate(edge0, 1), own1, np.concatenate(edge1, 1), np.concatenate(states, 0), sizes
 
 
-def tile_parts(rows, cols):
-    own_i, edge_i, state_i = line_parts(rows)
-    own_c, edge_c, state_c = line_parts(cols)
-    own = outer(own_i, own_c, True)
-    edges = [outer(edge_i, own_c, True), outer(own_i, edge_c, True), outer(edge_i, edge_c, True)]
-    states = [
-        outer(state_i, np.eye(cols), False),
-        outer(np.eye(rows), state_c, False),
-        outer(state_i, state_c, False),
-    ]
-    sizes = [-(-e.shape[1] // 8) * 8 for e in edges]
-    if sum(sizes) % 16:
-        sizes[2] += 8
-    edges = [np.pad(e, ((0, 0), (0, s - e.shape[1]))) for e, s in zip(edges, sizes)]
-    states = [np.pad(v, ((0, s - v.shape[0]), (0, 0))) for v, s in zip(states, sizes)]
-    return own, np.concatenate(edges, 1), np.concatenate(states, 0), sizes
+def side_parts(length):
+    firsts = range(-SIDE // 2, length // 2)
+    count = len(firsts)
+    bands = np.zeros((2 * count, length + 2 * SIDE))
+    back = np.zeros((length, 2 * count))
+    for m, first in enumerate(firsts):
+        for k in range(6):
+            for part, taps in ((0, low_taps), (count, high_taps)):
+                bands[part + m, SIDE + 2 * first + k] = taps[k]
+                if 0 <= 2 * first + k < length:
+                    back[2 * first + k, part + m] = taps[k]
+    return bands, back
+
+
+def side_matrices(rows, cols):
+    bands_i, back_i = side_parts(rows)
+    bands_c, back_c = side_parts(cols)
+    bands = outer(bands_i, bands_c, True)
+    wide = cols + 2 * SIDE
+    order = []
+    for block in range(3):
+        for first, size in ((0, SIDE), (SIDE, cols), (SIDE + cols, SIDE)):
+            order += [(block * rows + r) * wide + first + c for r in range(rows) for c in range(size)]
+    back = outer(back_i.T, back_c.T, True).T
+    return bands[:, order], back
 
 
 def time_parts():
@@ -237,25 +250,21 @@
         extra = (row_at == dest * GROUP + tail_row).astype(f32).astype(bf16)
         at = slice(j * span, (j + 1) * span)
         coming[3 + j].wait()
-        out_ref[:, at] = (dot(main, traces_ref[:, at]) + dot(extra, tail)).astype(bf16)
+        both = jnp.concatenate([traces_ref[:, at], tail], 0)
+        out_ref[:, at] = dot(jnp.concatenate([main, extra], 1), both).astype(bf16)
         send(j, j * span, span)
     for copy in going:
         copy.wait()
 
 
-def bin_kernel(
-    arrived_far, scale_ref, time_far, state_far, summed_ref, s0, s1, s2, arrived_ref, time_ref, state_ref, sems
-):
+def bin_kernel(arrived_far, scale_ref, time_ref, state_ref, summed_ref, s0, s1, s2, arrived_ref, sems):
     outs = (s0, s1, s2)
     width = summed_ref.shape[1] // 4
     coming = []
     for j, (first, size) in enumerate([(3 * width, LANES)] + [(j * width, width) for j in range(3)]):
         at = pl.ds(first, size)
         coming.append(pltpu.make_async_copy(arrived_far.at[:, at], arrived_ref.at[:, at], sems.at[j]))
-    coming.append(pltpu.make_async_copy(state_far, state_ref, sems.at[4]))
-    coming.append(pltpu.make_async_copy(time_far, time_ref, sems.at[5]))
-    for copy in coming:
-        copy.start()
+        coming[-1].start()
     coming[0].wait()
     rows = arrived_ref.shape[0]
     bins, samples = summed_ref.shape
@@ -284,8 +293,6 @@
         term = dot(onehot, arrived_ref[:, j * span : (j + 1) * span])
         last = term if last is None else last + term
     pieces.append(last)
-    coming[4].wait()
-    coming[5].wait()
     matrix = state_ref[...]
     blocks = []
     for p, piece in enumerate(pieces):
@@ -299,42 +306,31 @@
 
 
 def put_joint(outs, where, low, high):
-    rows, cols, corner = [out.shape[0] for out in outs]
+    part = joint_parts(outs)
+    outs[0][:, where] = jnp.concatenate([low[part[0]], high[part[0]], low[part[3]]], 0)
+    outs[1][:, where] = jnp.concatenate([low[part[1]], high[part[1]], low[part[4]]], 0)
+    outs[2][:, where] = jnp.concatenate([low[part[2]], high[part[2]][:8]], 0)
+
+
+def joint_parts(refs):
+    rows, cols, corner = [ref.shape[0] for ref in refs]
     ends = [0]
-    for size in (rows * 2 // 5, cols * 2 // 5, corner // 2, rows // 5, cols // 5):
+    for size in (rows * 2 // 5, cols * 2 // 5, corner - 8, rows // 5, cols // 5):
         ends.append(ends[-1] + size)
-    part = [slice(ends[k], ends[k + 1]) for k in range(5)]
-    put_rows([outs[0]], where, jnp.concatenate([low[part[0]], high[part[0]], low[part[3]]], 0))
-    put_rows([outs[1]], where, jnp.concatenate([low[part[1]], high[part[1]], low[part[4]]], 0))
-    put_rows([outs[2]], where, jnp.concatenate([low[part[2]], high[part[2]]], 0))
+    return [slice(ends[k], ends[k + 1]) for k in range(5)]
 
 
 def take_joint(refs, where):
     rows, cols, corner = [ref.shape[0] for ref in refs]
-    r, c, d = rows * 2 // 5, cols * 2 // 5, corner // 2
+    r, c, d = rows * 2 // 5, cols * 2 // 5, corner - 8
     m0, m1, m2 = [ref[:, where] for ref in refs]
     low = jnp.concatenate([m0[:r], m1[:c], m2[:d], m0[2 * r :], m1[2 * c :]], 0)
-    high = jnp.concatenate([m0[r : 2 * r], m1[c : 2 * c], m2[d:]], 0)
+    high = jnp.concatenate([m0[r : 2 * r], m1[c : 2 * c], m2[d:], jnp.zeros((d - 8, m2.shape[1]), f32)], 0)
     return low, high
-
-
-def put_rows(outs, where, value):
-    top = 0
-    for out in outs:
-        out[:, where] = value[top : top + out.shape[0]]
-        top += out.shape[0]
 
 
 def join_rows(refs, where):
     return jnp.concatenate([ref[:, where] for ref in refs], 0)
-
-
-def put_states(value_ref, state_ref, state_outs, step):
-    matrix = state_ref[...]
-    for start in range(0, value_ref.shape[1], step):
-        where = slice(start, start + step)
-        result = left_dot(matrix, value_ref[:, where])
-        put_rows(state_outs, where, result)
 
 
 def steps(ref):
@@ -352,7 +348,7 @@
         high_ref[:, where] = left_dot(own_ref[...], jnp.concatenate([highs[b], highs[b + 1]], 1))
 
 
-def middle_kernel(thr_ref, own_ref, edge_ref, s0, s1, s2, time_ref, state_ref, shrunk_ref, timed_ref, *state_outs):
+def middle_kernel(cols, thr_ref, own_ref, edge_ref, s0, s1, s2, time_ref, shrunk_ref, timed_ref, first_out, last_out):
     quarter = shrunk_ref.shape[0] // 4
     half = shrunk_ref.shape[1] // 2
     matrix = edge_ref[...]
@@ -375,10 +371,18 @@
     for b in range(len(coarse)):
         for base, piece in ((0, lows[b]), (half // 2, highs[b])):
             timed_ref[:, base + b * LANES : base + (b + 1) * LANES] = piece
-    put_states(timed_ref, state_ref, state_outs, BLOCK)
-
-
-def details_kernel(thr_ref, low_in, high_in, edge_ref, s0, s1, s2, back_low, back_ref, low_out, high_out, *state_outs):
+    starts = range(0, timed_ref.shape[0], cols)
+    first_out[...] = jnp.concatenate([timed_ref[at : at + SIDE] for at in starts], 0)
+    last_out[...] = jnp.concatenate([timed_ref[at + cols - SIDE : at + cols] for at in starts], 0)
+
+
+def join_kernel(left_ref, own_ref, right_ref, out_ref):
+    out_ref[...] = jnp.concatenate([left_ref[...], own_ref[...], right_ref[...]], 0)
+
+
+def details_kernel(
+    thr_ref, low_in, high_in, edge_ref, s0, s1, s2, back_low, back_ref, low_out, high_out, low_states, high_states
+):
     quarter = low_in.shape[0] // 4
     for where in steps(low_in):
         low, high = take_joint((s0, s1, s2), where)
@@ -386,56 +390,62 @@
         bands = [shrink(bands[(q - 1) * quarter : q * quarter], thr_ref[0, 2 * q - 1]) for q in range(1, 4)]
         bands = jnp.concatenate(bands, 0)
         low_out[:, where] = bands
-        state_outs[0][:, where] = left_dot(back_low[...], bands)
+        low_states[:, where] = left_dot(back_low[...], bands)
         bands = high_in[:, where] + left_dot(edge_ref[...], high)
         bands = [shrink(bands[q * quarter : (q + 1) * quarter], thr_ref[0, 2 * q]) for q in range(4)]
         bands = jnp.concatenate(bands, 0)
         high_out[:, where] = bands
-        state_outs[1][:, where] = left_dot(back_ref[...], bands)
-
-
-def spread_kernel(low_in, high_in, low_matrix, own_matrix, shrunk_in, time_t, low_out, high_out, next_out):
-    for where in steps(low_in):
-        low_out[:, where] = left_dot(low_matrix[...], low_in[:, where])
-        high_out[:, where] = left_dot(own_matrix[...], high_in[:, where])
-    half = shrunk_in.shape[1] // 2
-    blocks = []
+        high_states[:, where] = left_dot(back_ref[...], bands)
+
+
+def time_pairs(bands, matrix):
+    half = bands.shape[1] // 2
+    pairs = []
     for b in range(0, half, LANES):
-        blocks.append(jnp.concatenate([shrunk_in[:, b : b + LANES], shrunk_in[:, half + b : half + b + LANES]], 1))
-    for b, block in enumerate(time_synthesis(blocks, time_t[...])):
-        next_out[:, b * BLOCK : (b + 1) * BLOCK] = block
-
-
-def rejoin_kernel(
-    shrunk, own_t, state_t, s0, s1, s2, time_t, time_low, next_in, low_states, high_states, back_ref, next_out, *outs
+        pairs.append(jnp.concatenate([bands[:, b : b + LANES], bands[:, half + b : half + b + LANES]], 1))
+    return time_synthesis(pairs, matrix)
+
+
+def deepest_kernel(
+    thr_ref, before, own, after, bands_m, back_m, time_t, time_low, next_in, low_states, high_states, back_ref, next_out, *outs
 ):
-    coarse = rebuilt_blocks(shrunk, own_t, state_t, s0, s1, s2, time_t)
-    rows = coarse[0].shape[0]
+    stack = jnp.concatenate([before[...], own[...], after[...]], 0)
+    bands = left_dot(bands_m[...], stack)
+    row = lax.broadcasted_iota(jnp.int32, bands.shape, 0)
+    high = lax.broadcasted_iota(jnp.int32, bands.shape, 1) >= bands.shape[1] // 2
+    limit = jnp.where(high, thr_ref[2, 0], 0.0)
+    quarter = bands.shape[0] // 4
+    for q in range(1, 4):
+        limit = jnp.where(row >= q * quarter, jnp.where(high, thr_ref[2, 2 * q], thr_ref[2, 2 * q - 1]), limit)
+    rebuilt = left_dot(back_m[...], shrink(bands, limit))
+    details = time_pairs(next_in[...], time_t[...])
     lows = []
-    for block in coarse:
+    for block in time_pairs(rebuilt, time_t[...]):
         lows += [block[:, b : b + LANES] for b in range(0, BLOCK, LANES)]
+    rows = rebuilt.shape[0]
     count = low_states.shape[0]
     for b, block in enumerate(synthesis_from_low(lows, time_low[...])):
         where = slice(b * BLOCK, (b + 1) * BLOCK)
-        bands = jnp.concatenate([next_in[:rows, where] + block, next_in[rows:, where]], 0)
+        bands = jnp.concatenate([details[b][:rows] + block, details[b][rows:]], 0)
         next_out[:, where] = bands
         states = left_dot(back_ref[...], bands)
         low = jnp.concatenate([states[:count] + low_states[:, where], states[count:]], 0)
         put_joint(outs, where, low, high_states[:, where])
 
 
-def own_back_kernel(low_in, high_in, next_in, next_t, time_t, out_ref):
+def own_back_kernel(low_in, high_in, next_in, low_t, high_t, next_t, time_t, scale_ref, out_ref):
     blocks = []
     for where in steps(low_in):
-        low = low_in[:, where] + left_dot(next_t[...], next_in[:, where])
-        high = high_in[:, where]
+        low = left_dot(low_t[...], low_in[:, where]) + left_dot(next_t[...], next_in[:, where])
+        high = left_dot(high_t[...], high_in[:, where])
         for b in range(0, BLOCK, LANES):
             blocks.append(jnp.concatenate([low[:, b : b + LANES], high[:, b : b + LANES]], 1))
+    scale = scale_ref[...]
     for b, block in enumerate(time_synthesis(blocks, time_t[...])):
-        out_ref[:, b * BLOCK : (b + 1) * BLOCK] = block
-
-
-def final_kernel(own_ref, s0, s1, s2, time_t, state_t, scale_ref, out_ref):
+        out_ref[:, b * BLOCK : (b + 1) * BLOCK] = block * scale
+
+
+def final_kernel(own_ref, s0, s1, s2, time_t, time_low, state_t, scale_ref, out_far, out_ref, sems):
     pairs, lows = [], []
     for start in range(0, s0.shape[1], LANES):
         low, high = take_joint((s0, s1, s2), slice(start, start + LANES))
@@ -443,50 +453,20 @@
         pairs.append(jnp.concatenate([low[:count], high], 1))
         lows.append(low[count:])
     level0 = time_synthesis(pairs, time_t[...])
-    level1 = synthesis_from_low(lows, low_rows(time_t))
+    level1 = synthesis_from_low(lows, time_low[...])
     scale = scale_ref[...]
+    going = []
     for b in range(len(pairs)):
         where = slice(b * BLOCK, (b + 1) * BLOCK)
         states = jnp.concatenate([level0[b], level1[b]], 0)
-        out_ref[:, where] = (own_ref[:, where] + left_dot(state_t[...], states)) * scale
-
-
-def low_rows(time_t):
-    count = time_t.shape[0] // BLOCK
-    return jnp.concatenate([time_t[k * BLOCK : k * BLOCK + LANES] for k in range(count)], 0)
-
-
-def last_kernel(level, thr_ref, timed_ref, own_ref, edge_ref, s0, s1, s2, back_ref, shrunk_ref, *state_outs):
-    quarter = timed_ref.shape[0] // 4
-    half = timed_ref.shape[1] // 2
-    for start in range(0, 2 * half, BLOCK):
-        where = slice(start, start + BLOCK)
-        states = join_rows((s0, s1, s2), where)
-        bands = left_dot(own_ref[...], timed_ref[:, where]) + left_dot(edge_ref[...], states)
-        high = start >= half
-        row = lax.broadcasted_iota(jnp.int32, bands.shape, 0)
-        limit = jnp.full(bands.shape, thr_ref[level, 0] if high else 0.0, f32)
-        for q in range(1, 4):
-            limit = jnp.where(row >= q * quarter, thr_ref[level, 2 * q + int(high) - 1], limit)
-        shrunk_ref[:, where] = shrink(bands, limit)
-    put_states(shrunk_ref, back_ref, state_outs, BLOCK)
-
-
-def rebuilt_blocks(shrunk, own_t, state_t, s0, s1, s2, time_t):
-    half = shrunk.shape[1] // 2
-    blocks = []
-    for start in range(0, half, LANES):
-        pair = []
-        for base in (0, half):
-            where = slice(base + start, base + start + LANES)
-            pair.append((shrunk[:, where], join_rows((s0, s1, s2), where)))
-        bands = jnp.concatenate([pair[0][0], pair[1][0]], 1)
-        states = jnp.concatenate([pair[0][1], pair[1][1]], 1)
-        blocks.append(left_dot(own_t[...], bands) + left_dot(state_t[...], states))
-    return time_synthesis(blocks, time_t[...])
-
-
-def call(kernel, outs, *args, smem=(), far=(), far_outs=(), scratch=(), after=(), cost=None):
+        out_ref[:, where] = own_ref[:, where] + left_dot(state_t[...], states) * scale
+        going.append(pltpu.make_async_copy(out_ref.at[:, where], out_far.at[:, where], sems.at[b]))
+        going[-1].start()
+    for copy in going:
+        copy.wait()
+
+
+def call(kernel, outs, *args, smem=(), far=(), far_outs=(), scratch=(), after=(), cost=None, limit=VMEM_LIMIT):
     spaces = [pltpu.SMEM if i in smem else pltpu.HBM if i in far else pltpu.VMEM for i in range(len(args))]
     spaces += [pl.ANY] * len(after)
     count = len(args)
@@ -502,7 +482,7 @@
             pl.BlockSpec(memory_space=pltpu.HBM if i in far_outs else pltpu.VMEM) for i in range(len(outs))
         ],
         scratch_shapes=list(scratch),
-        compiler_params=pltpu.CompilerParams(vmem_limit_bytes=VMEM_LIMIT),
+        compiler_params=pltpu.CompilerParams(vmem_limit_bytes=limit),
         cost_estimate=None
         if cost is None
         else pl.CostEstimate(flops=int(cost), bytes_accessed=0, transcendentals=0),
@@ -541,6 +521,7 @@
         traces,
         far=(0, 1, 2),
         far_outs=(0,),
+        limit=LARGE_LIMIT,
         scratch=[
             pltpu.VMEM((1, trace_count), jnp.int32),
             pltpu.VMEM((1, trace_count), jnp.int32),
@@ -563,14 +544,14 @@
     half, rows2, cols2 = samples // 2, tile_rows // 4, tile_cols // 4
     quarter, last = bins // 4, bins // 16
     own0, edge0, own1, edge1, states01, sizes = joint_matrices(tile_rows, tile_cols)
-    own2, edge2, states2, sizes2 = tile_parts(rows2, cols2)
+    assert rows2 == SIDE and cols2 >= SIDE
+    bands2, back2 = side_matrices(rows2, cols2)
     count0 = sum(sizes[:3])
     joint_shapes = [
         ((2 * sizes[0] + sizes[3], half), f32),
         ((2 * sizes[1] + sizes[4], half), f32),
-        ((2 * sizes[2], half), f32),
+        ((sizes[2] + 8, half), f32),
     ]
-    shapes2 = [((size, samples // 4), f32) for size in sizes2]
 
     summed, *states = call(
         bin_kernel,
@@ -579,13 +560,9 @@
         scale,
         time_matrix,
         triple(states01, 1),
-        far=(0, 2, 3),
-        scratch=[
-            pltpu.VMEM((devices * GROUP, width), bf16),
-            pltpu.VMEM(time_matrix.shape, bf16),
-            pltpu.VMEM((sum(sizes), 3 * bins), bf16),
-            pltpu.SemaphoreType.DMA((6,)),
-        ],
+        far=(0,),
+        limit=MIDDLE_LIMIT,
+        scratch=[pltpu.VMEM((devices * GROUP, width), bf16), pltpu.SemaphoreType.DMA((4,))],
     )
     states = exchange(states, 1)
     own_low, own_high, own_next = call(
@@ -597,18 +574,26 @@
         triple(own1, 1),
         cost=8e9,
     )
-    shrunk1, timed, *states2_out = call(
-        middle_kernel,
-        [((quarter, half), f32), ((last, half // 2), f32)] + shapes2,
+    side_shape = ((rows2 * SIDE, samples // 4), f32)
+    shrunk1, timed, firsts, lasts = call(
+        functools.partial(middle_kernel, cols2),
+        [((quarter, half), f32), ((last, half // 2), f32), side_shape, side_shape],
         thresholds,
         own_next,
         triple(edge1, 1),
         *states,
         time_matrix,
-        triple(states2, 1),
         smem=(0,),
     )
-    ahead = exchange(states2_out, 1)
+    sides = shift(lasts, 0, -1), shift(firsts, 0, 1)
+    (wide,) = call(
+        join_kernel,
+        [((last + 2 * rows2 * SIDE, samples // 4), f32)],
+        sides[0],
+        timed,
+        sides[1],
+    )
+    before, behind = shift(wide, -1, 0), shift(wide, 1, 0)
     low_details, high_details, low_states, high_states = call(
         details_kernel,
         [((bins - quarter, half), f32), ((bins, half), f32)] + [((count0, half), f32)] * 2,
@@ -620,57 +605,38 @@
         triple(edge0[quarter:].T, 1),
         triple(edge0.T, 1),
         smem=(0,),
-        after=(timed,),
+        after=(wide,),
         cost=6e9,
     )
-    shrunk2, *states2_out = call(
-        functools.partial(last_kernel, 2),
-        [((last, half // 2), f32)] + shapes2,
+    bands1, *states = call(
+        deepest_kernel,
+        [((quarter, half), f32)] + joint_shapes,
         thresholds,
-        timed,
-        triple(own2, 1),
-        triple(edge2, 1),
-        *ahead,
-        triple(edge2.T, 1),
-        smem=(0,),
-        after=(low_details,),
-    )
-    behind = exchange(states2_out, -1)
-    spread_low, spread_high, spread_next = call(
-        spread_kernel,
-        [((bins, half), f32)] * 2 + [((quarter, half), f32)],
-        low_details,
-        high_details,
-        triple(own0[quarter:].T, 1),
-        triple(own0.T, 1),
-        shrunk1,
-        time_back,
-        after=(shrunk2,),
-        cost=6e9,
-    )
-    bands1, *states = call(
-        rejoin_kernel,
-        [((quarter, half), f32)] + joint_shapes,
-        shrunk2,
-        triple(own2.T, 1),
-        triple(states2.T, 1),
-        *behind,
+        before,
+        wide,
+        behind,
+        triple(bands2, 1),
+        triple(back2, 1),
         time_back,
         time_back_low,
-        spread_next,
+        shrunk1,
         low_states,
         high_states,
         triple(edge1.T, 1),
+        smem=(0,),
     )
     states = exchange(states, -1)
     (own_back,) = call(
         own_back_kernel,
         [((bins, samples), f32)],
-        spread_low,
-        spread_high,
+        low_details,
+        high_details,
         bands1,
+        triple(own0[quarter:].T, 1),
+        triple(own0.T, 1),
         triple(own1.T, 1),
         time_back,
+        scale,
         cost=6e9,
     )
     (denoised,) = call(
@@ -679,8 +645,11 @@
         own_back,
         *states,
         time_back,
+        time_back_low,
         triple(states01.T, 1),
         scale,
+        far_outs=(0,),
+        scratch=[pltpu.VMEM((bins, samples), f32), pltpu.SemaphoreType.DMA((samples // BLOCK,))],
     )
     return denoised.reshape(tile_rows, tile_cols, samples)
 

time: 139 us -> 128 us (0.921); the launches traced: 137 us -> 128 us
  local copies, waits for them, and re-layouts: 6.84 us -> 0.24 us
  waiting for transfers between devices: 74.2 us -> 71.7 us
    ppermute x4 -> x2, starting transfers between devices: 8.25 us -> 0.64 us  [shift(): return lax.ppermute(block, ('inl', 'xl'), route)]
    ppermute x4 -> x2, waiting for transfers between devices: 12.7 us -> 6.13 us  [shift(): return lax.ppermute(block, ('inl', 'xl'), route)]
    unnamed x58 -> x38, local copies, waits for them, and re-layouts: 6.05 us -> 0.12 us
    ppermute x4, starting transfers between devices: 0.73 us -> 5.36 us  [shift(): lax.ppermute(block, 'inl', [((i + inline_by) % inline_devs, i) for i in r...]
    ppermute x4, waiting for transfers between devices: 17.4 us -> 19.8 us  [shift(): lax.ppermute(block, 'inl', [((i + inline_by) % inline_devs, i) for i in r...]
    ppermute x4, starting transfers between devices: 1.93 us -> 4.19 us  [shift(): lax.ppermute(block, 'xl', [((j + cross_by) % cross_devs, j) for j in rang...]
    pallas_call x10 -> x9, Pallas kernels: 34 us -> 33.7 us  [call(): pl.pallas_call(body, out_shape=[jax.ShapeDtypeStruct(shape, dtype) for sh...]
  transfers between devices with their start and end apart: 13 -> 11, of which waited for: 7 -> 7; matrix products, arithmetic and copies ran while one was open for 1% -> 0% of each run, Pallas kernels for 10% -> 10%
where the time goes in v2:
time: 128 us
  waiting for transfers between devices  71.7 us (56%)
  Pallas kernels  33.7 us (26%)
  starting transfers between devices  21.8 us (17%)
    all_to_all x1, waiting for transfers between devices, on_device(): lax.all_to_all(outgoing.reshape(devices, GROUP, width), ('inl', 'xl'), sp...  44 us
    pallas_call x9, Pallas kernels, call(): pl.pallas_call(body, out_shape=[jax.ShapeDtypeStruct(shape, dtype) for sh...  33.7 us
    ppermute x4, waiting for transfers between devices, shift(): lax.ppermute(block, 'inl', [((i + inline_by) % inline_devs, i) for i in r...  19.8 us
    all_to_all x1, starting transfers between devices, on_device(): lax.all_to_all(outgoing.reshape(devices, GROUP, width), ('inl', 'xl'), sp...  11.6 us
    ppermute x2, waiting for transfers between devices, shift(): return lax.ppermute(block, ('inl', 'xl'), route)  6.13 us
    ppermute x4, starting transfers between devices, shift(): lax.ppermute(block, 'inl', [((i + inline_by) % inline_devs, i) for i in r...  5.36 us
    ppermute x4, starting transfers between devices, shift(): lax.ppermute(block, 'xl', [((j + cross_by) % cross_devs, j) for j in rang...  4.19 us
  transfers between devices with their start and end apart: 11, of which 7 were waited for; matrix products, arithmetic and copies ran while one was open for 0% of the time, Pallas kernels for 10%

profile of v2, /device:TPU:0, one launch (start us, length us, event | category | flops | bytes accessed | tf_op | source)
XLA Modules:
  0.0 128.0 jit_solution(15322600322743085900)
XLA Ops:
  0.0 7.0 %shard_map.208 = bf16[1024,1664]{1,0:T(8,128)(2,1)} custom-call(s32[1,512]{1,0:T(1,128)} %bitcast.6, s32[1,512]{1,0:T(1,128)} %bitcast.7, bf16[512,2048]{1,0:T(8,128)(2,1)} %refs_2_.4), custom_call_target="tpu_custom_call" | custom-call | tf_op jit(solution)/shard_map/pallas_call | solution.py:477
  7.0 0.0 copy-start.18
  7.0 0.0 copy-start.1
  7.0 0.0 copy-start.4
  7.0 11.6 %all-to-all-start = ((bf16[128,8,1664]{2,1,0:T(8,128)(2,1)}), bf16[128,8,1664]{2,1,0:T(8,128)(2,1)}, u32[]{:S(2)}, u32[]{:S(2)}) async-start(bf16[128,8,1664]{2,1,0:T(8,128)(2,1)} %bitcast.5), calls=%async_computation | async-start | bytes 6815744 | tf_op jit(solution)/shard_map/all_to_all | solution.py:534
  18.6 0.0 copy-done.18
  18.6 0.0 copy-start.11
  18.7 0.0 copy-start.16
  18.7 0.1 reshape.24.refs_1_.refs_7_
  18.8 44.0 %all-to-all-done = bf16[128,8,1664]{2,1,0:T(8,128)(2,1)} async-done(((bf16[128,8,1664]{2,1,0:T(8,128)(2,1)}), bf16[128,8,1664]{2,1,0:T(8,128)(2,1)}, u32[]{:S(2)}, u32[]{:S(2)}) %all-to-all-start) | async-done | bytes 3407904 | tf_op jit(solution)/shard_map/all_to_all | solution.py:534
  62.8 0.0 copy-done.1
  62.8 0.0 copy-done.4
  62.8 6.1 %shard_map.209 = (f32[384,2048]{1,0:T(8,128)S(1)}, f32[120,1024]{1,0:T(8,128)S(1)}, f32[80,1024]{1,0:T(8,128)S(1)}, f32[24,1024]{1,0:T(8,128)S(1)}) custom-call(bf16[1024,1664]{1,0:T(8,128)(2,1)} %bitcast.3.refs_0_, f32[384,1]{1,0:T(8,128)S(1)} %reshape.24.refs_1_.refs_7_, bf16[1152,256]{1,0:T(8,128)(2,1)S(1)} %copy-done.1, bf16[136,1152]{1,0:T(8,128)(2,1)S(1)} %copy-done.4), custom_call_target="tpu_custom_call" | custom-call | tf_op jit(solution)/shard_map/pallas_call | solution.py:477
  68.9 0.6 collective-permute-start.2
  69.5 1.2 collective-permute-start.1
  70.7 0.3 collective-permute-start
  71.0 0.0 copy-done.11
  71.0 0.0 copy-done.16
  71.0 0.0 copy-start.14
  71.0 0.0 copy-start.15
  71.0 0.0 copy-start.17
  71.0 4.6 %shard_map.210 = (f32[384,1024]{1,0:T(8,128)S(1)}, f32[384,1024]{1,0:T(8,128)S(1)}, f32[96,1024]{1,0:T(8,128)S(1)}) custom-call(f32[384,2048]{1,0:T(8,128)S(1)} %get-tuple-element.24.refs_0_, bf16[1152,256]{1,0:T(8,128)(2,1)S(1)} %copy-done.1, bf16[384,1152]{1,0:T(8,128)(2,1)S(1)} %copy-done.11, bf16[96,1152]{1,0:T(8,128)(2,1)S(1)} %copy-done.16), custom_call_target="tpu_custom_call" | custom-call | flops 8000000000 | tf_op jit(solution)/shard_map/pallas_call | solution.py:477
  75.6 0.0 collective-permute-done.2.refs_5_.refs_6_
  75.6 0.2 collective-permute-done.1.refs_4_.refs_5_
  75.8 8.8 %collective-permute-done.refs_3_.refs_4_ = f32[120,1024]{1,0:T(8,128)S(1)} collective-permute-done((f32[120,1024]{1,0:T(8,128)S(1)}, f32[120,1024]{1,0:T(8,128)S(1)}, u32[]{:S(2)}, u32[]{:S(2)}) %collective-permute-start) | collective-permute-done | bytes 491552 | tf_op jit(solution)/shard_map/ppermute | solution.py:495
  84.6 0.0 copy-done.6
  84.6 0.0 copy-done.9
  84.6 1.5 %shard_map.211 = (f32[96,1024]{1,0:T(8,128)S(1)}, f32[24,512]{1,0:T(8,128)S(1)}, f32[16,512]{1,0:T(8,128)S(1)}, f32[16,512]{1,0:T(8,128)S(1)}) custom-call(f32[3,7]{1,0:T(4,128)S(1)} %copy-done.9, f32[96,1024]{1,0:T(8,128)S(1)} %get-tuple-element.30.refs_1_, bf16[96,408]{1,0:T(8,128)(2,1)S(1)} %copy-done.6, ...), custom_call_target="tpu_custom_call" | custom-call | tf_op jit(solution)/shard_map/pallas_call | solution.py:477
  86.1 0.0 collective-permute-start.3
  86.2 2.9 %collective-permute-start.4 = (f32[16,512]{1,0:T(8,128)S(1)}, f32[16,512]{1,0:T(8,128)S(1)}, u32[]{:S(2)}, u32[]{:S(2)}) collective-permute-start(f32[16,512]{1,0:T(8,128)S(1)} %get-tuple-element.33), channel_id=1, source_target_pairs={{1,0},{2,1},{3,2},{4,3},{5,4},{6,5},{7,6},{0,7},{9,8},{10,9},{11,1... | collective-permute-start | bytes 98312 | tf_op jit(solution)/shard_map/ppermute | solution.py:497
  89.1 1.6 %collective-permute-done.3.refs_0_ = f32[16,512]{1,0:T(8,128)S(1)} collective-permute-done((f32[16,512]{1,0:T(8,128)S(1)}, f32[16,512]{1,0:T(8,128)S(1)}, u32[]{:S(2)}, u32[]{:S(2)}) %collective-permute-start.3) | collective-permute-done | bytes 32800 | tf_op jit(solution)/shard_map/ppermute | solution.py:497
  90.7 0.0 collective-permute-done.4.refs_2_
  90.7 4.8 %collective-permute-start.6 = (f32[56,512]{1,0:T(8,128)S(1)}, f32[56,512]{1,0:T(8,128)S(1)}, u32[]{:S(2)}, u32[]{:S(2)}) collective-permute-start(f32[56,512]{1,0:T(8,128)S(1)} %shard_map.212.refs_9_.refs_2_), channel_id=1, source_target_pairs={{8,0},{16,8},{24,16},{32,24},{40,32},{48,40},{56,48},{64,56},{72,6... | collective-permute-start | bytes 344072 | tf_op jit(solution)/shard_map/ppermute | solution.py:495
  95.5 0.0 collective-permute-start.5
  95.5 0.0 copy-done.14
  95.5 0.0 copy-done.15
  95.5 0.0 copy-done.17
  95.5 0.0 copy-start
  95.5 0.0 copy-start.2
  95.6 0.0 copy-start.5
  95.6 0.0 copy-start.7
  95.6 0.0 copy-start.8
  95.6 0.0 copy-start.10
  95.6 0.0 copy-start.12
  95.6 0.0 copy-start.13
  95.6 3.6 %shard_map.213 = (f32[288,1024]{1,0:T(8,128)S(1)}, f32[384,1024]{1,0:T(8,128)S(1)}, f32[96,1024]{1,0:T(8,128)S(1)}, f32[96,1024]{1,0:T(8,128)S(1)}) custom-call(f32[3,7]{1,0:T(4,128)S(1)} %copy-done.9, f32[384,1024]{1,0:T(8,128)S(1)} %get-tuple-element.25.refs_1_, f32[384,1024]{1,0:T(8,128)S(1)} %get-tuple-element.26.refs_2_, ...), custom_call_target="tpu_custom_call" | custom-call | flops 6000000000 | tf_op jit(solution)/shard_map/pallas_call | solution.py:477
  99.3 0.0 collective-permute-done.6.refs_3_
  99.3 4.3 %collective-permute-done.5.refs_1_ = f32[56,512]{1,0:T(8,128)S(1)} collective-permute-done((f32[56,512]{1,0:T(8,128)S(1)}, f32[56,512]{1,0:T(8,128)S(1)}, u32[]{:S(2)}, u32[]{:S(2)}) %collective-permute-start.5) | collective-permute-done | bytes 114720 | tf_op jit(solution)/shard_map/ppermute | solution.py:495
  103.6 0.0 copy-done
  103.6 0.0 copy-done.2
  103.6 0.0 copy-done.5
  103.7 2.3 %shard_map.214 = (f32[96,1024]{1,0:T(8,128)S(1)}, f32[120,1024]{1,0:T(8,128)S(1)}, f32[80,1024]{1,0:T(8,128)S(1)}, f32[24,1024]{1,0:T(8,128)S(1)}) custom-call(f32[3,7]{1,0:T(4,128)S(1)} %copy-done.9, f32[56,512]{1,0:T(8,128)S(1)} %collective-permute-done.5.refs_1_, f32[56,512]{1,0:T(8,128)S(1)} %shard_map.212.refs_9_.refs_2_, ...), custom_call_target="tpu_custom_call" | custom-call | tf_op jit(solution)/shard_map/pallas_call | solution.py:477
  106.0 0.1 collective-permute-start.9
  106.1 0.0 collective-permute-start.8
  106.1 0.3 collective-permute-start.7
  106.4 0.0 copy-done.10
  106.4 0.0 copy-done.12
  106.4 0.0 copy-done.13
  106.4 0.0 copy-start.3
  106.4 5.0 %shard_map.215.refs_0_ = f32[384,2048]{1,0:T(8,128)S(1)} custom-call(f32[288,1024]{1,0:T(8,128)S(1)} %get-tuple-element.34.refs_0_, f32[384,1024]{1,0:T(8,128)S(1)} %get-tuple-element.35.refs_1_, f32[96,1024]{1,0:T(8,128)S(1)} %get-tuple-element.39.refs_2_, bf16[384,864]{1,0:T(8,128)(2,1)S(1)} %copy-done.12, bf16[384,1152]{1,0:T(8,128)(2,1)S(1)} %copy-done.10, ...), custom_call_target="tpu_custom_call" | custom-call | flops 6000000000 | tf_op jit(solution)/shard_map/pallas_call | solution.py:477
  111.4 6.1 %collective-permute-done.9.refs_3_ = f32[24,1024]{1,0:T(8,128)S(1)} collective-permute-done((f32[24,1024]{1,0:T(8,128)S(1)}, f32[24,1024]{1,0:T(8,128)S(1)}, u32[]{:S(2)}, u32[]{:S(2)}) %collective-permute-start.9) | collective-permute-done | bytes 98336 | tf_op jit(solution)/shard_map/ppermute | solution.py:503
  117.6 0.0 collective-permute-done.8.refs_2_
  117.6 6.6 %collective-permute-done.7.refs_1_ = f32[120,1024]{1,0:T(8,128)S(1)} collective-permute-done((f32[120,1024]{1,0:T(8,128)S(1)}, f32[120,1024]{1,0:T(8,128)S(1)}, u32[]{:S(2)}, u32[]{:S(2)}) %collective-permute-start.7) | collective-permute-done | bytes 491552 | tf_op jit(solution)/shard_map/ppermute | solution.py:495
  124.2 3.6 %shard_map.216 = f32[384,2048]{1,0:T(8,128)} custom-call(f32[384,2048]{1,0:T(8,128)S(1)} %shard_map.215.refs_0_, f32[120,1024]{1,0:T(8,128)S(1)} %collective-permute-done.7.refs_1_, f32[80,1024]{1,0:T(8,128)S(1)} %collective-permute-done.8.refs_2_, f32[24,1024]{1,0:T(8,128)S(1)} %collective-permute-done.9.refs_3_, bf16[1536,256]{1,0:T(8,128)(2,1)S(1)} %copy-done, ...), custom_call_target="tpu_custom_call" | custom-call | tf_op jit(solution)/shard_map/pallas_call | solution.py:477
  (7 shorter events, 0.0 us)
Async XLA Ops:
  7.0 11.7 %copy-start.18 = (s32[16,24]{1,0:T(8,128)S(1)}, s32[16,24]{1,0:T(8,128)}, u32[]{:S(2)}) copy-start(s32[16,24]{1,0:T(8,128)} %param.25) | copy-start | bytes 4612
  7.0 55.8 %copy-start.1 = (bf16[1152,256]{1,0:T(8,128)(2,1)S(1)}, bf16[1152,256]{1,0:T(8,128)(2,1)}, u32[]{:S(2)}) copy-start(bf16[1152,256]{1,0:T(8,128)(2,1)} %constant.17.clone.refs_2_.refs_1_.refs_6_) | copy-start | bytes 1769476
  7.0 55.8 %copy-start.4 = (bf16[136,1152]{1,0:T(8,128)(2,1)S(1)}, bf16[136,1152]{1,0:T(8,128)(2,1)}, u32[]{:S(2)}) copy-start(bf16[136,1152]{1,0:T(8,128)(2,1)} %constant.36.clone.refs_3_) | copy-start | bytes 940036
  7.0 55.8 %all-to-all-start = ((bf16[128,8,1664]{2,1,0:T(8,128)(2,1)}), bf16[128,8,1664]{2,1,0:T(8,128)(2,1)}, u32[]{:S(2)}, u32[]{:S(2)}) async-start(bf16[128,8,1664]{2,1,0:T(8,128)(2,1)} %bitcast.5), calls=%async_computation | async-start | bytes 6815744 | tf_op jit(solution)/shard_map/all_to_all | solution.py:534
  18.6 52.3 %copy-start.11 = (bf16[384,1152]{1,0:T(8,128)(2,1)S(1)}, bf16[384,1152]{1,0:T(8,128)(2,1)}, u32[]{:S(2)}) copy-start(bf16[384,1152]{1,0:T(8,128)(2,1)} %constant.37.clone.refs_2_) | copy-start | bytes 2654212
  18.7 52.3 %copy-start.16 = (bf16[96,1152]{1,0:T(8,128)(2,1)S(1)}, bf16[96,1152]{1,0:T(8,128)(2,1)}, u32[]{:S(2)}) copy-start(bf16[96,1152]{1,0:T(8,128)(2,1)} %constant.38.clone.refs_3_) | copy-start | bytes 663556
  68.9 6.7 %collective-permute-start.2 = (f32[24,1024]{1,0:T(8,128)S(1)}, f32[24,1024]{1,0:T(8,128)S(1)}, u32[]{:S(2)}, u32[]{:S(2)}) collective-permute-start(f32[24,1024]{1,0:T(8,128)S(1)} %get-tuple-element.29), channel_id=1, source_target_pairs={{9,0},{10,1},{11,2},{12,3},{13,4},{14,5},{15,6},{8,7},{17,8},{18,9... | collective-permute-start | bytes 294920 | tf_op jit(solution)/shard_map/ppermute | solution.py:503
  69.5 6.3 %collective-permute-start.1 = (f32[80,1024]{1,0:T(8,128)S(1)}, f32[80,1024]{1,0:T(8,128)S(1)}, u32[]{:S(2)}, u32[]{:S(2)}) collective-permute-start(f32[80,1024]{1,0:T(8,128)S(1)} %get-tuple-element.28), channel_id=1, source_target_pairs={{1,0},{2,1},{3,2},{4,3},{5,4},{6,5},{7,6},{0,7},{9,8},{10,9},{11,1... | collective-permute-start | bytes 983048 | tf_op jit(solution)/shard_map/ppermute | solution.py:497
  70.7 13.9 %collective-permute-start = (f32[120,1024]{1,0:T(8,128)S(1)}, f32[120,1024]{1,0:T(8,128)S(1)}, u32[]{:S(2)}, u32[]{:S(2)}) collective-permute-start(f32[120,1024]{1,0:T(8,128)S(1)} %get-tuple-element.27), channel_id=1, source_target_pairs={{8,0},{16,8},{24,16},{32,24},{40,32},{48,40},{56,48},{64,56},{72,6... | collective-permute-start | bytes 1474568 | tf_op jit(solution)/shard_map/ppermute | solution.py:495
  71.0 13.7 %copy-start.6 = (bf16[96,408]{1,0:T(8,128)(2,1)S(1)}, bf16[96,408]{1,0:T(8,128)(2,1)}, u32[]{:S(2)}) copy-start(bf16[96,408]{1,0:T(8,128)(2,1)} %constant.39.clone.refs_2_) | copy-start | bytes 235012
  71.0 13.7 %copy-start.9 = (f32[3,7]{1,0:T(4,128)S(1)}, f32[3,7]{1,0:T(4,128)}, u32[]{:S(2)}) copy-start(f32[3,7]{1,0:T(4,128)} %refs_0_.5) | copy-start | bytes 256
  71.0 24.5 %copy-start.14 = (bf16[384,288]{1,0:T(8,128)(2,1)S(1)}, bf16[384,288]{1,0:T(8,128)(2,1)}, u32[]{:S(2)}) copy-start(bf16[384,288]{1,0:T(8,128)(2,1)} %constant.40.clone.refs_3_) | copy-start | bytes 663556
  71.0 24.5 %copy-start.15 = (bf16[96,1152]{1,0:T(8,128)(2,1)S(1)}, bf16[96,1152]{1,0:T(8,128)(2,1)}, u32[]{:S(2)}) copy-start(bf16[96,1152]{1,0:T(8,128)(2,1)} %constant.42.clone.refs_8_) | copy-start | bytes 663556
  71.0 24.5 %copy-start.17 = (bf16[96,864]{1,0:T(8,128)(2,1)S(1)}, bf16[96,864]{1,0:T(8,128)(2,1)}, u32[]{:S(2)}) copy-start(bf16[96,864]{1,0:T(8,128)(2,1)} %constant.41.clone.refs_7_) | copy-start | bytes 497668
  86.1 4.6 %collective-permute-start.3 = (f32[16,512]{1,0:T(8,128)S(1)}, f32[16,512]{1,0:T(8,128)S(1)}, u32[]{:S(2)}, u32[]{:S(2)}) collective-permute-start(f32[16,512]{1,0:T(8,128)S(1)} %get-tuple-element.31), channel_id=1, source_target_pairs={{7,0},{0,1},{1,2},{2,3},{3,4},{4,5},{5,6},{6,7},{15,8},{8,9},{9,10... | collective-permute-start | bytes 98312 | tf_op jit(solution)/shard_map/ppermute | solution.py:497
  86.2 4.5 %collective-permute-start.4 = (f32[16,512]{1,0:T(8,128)S(1)}, f32[16,512]{1,0:T(8,128)S(1)}, u32[]{:S(2)}, u32[]{:S(2)}) collective-permute-start(f32[16,512]{1,0:T(8,128)S(1)} %get-tuple-element.33), channel_id=1, source_target_pairs={{1,0},{2,1},{3,2},{4,3},{5,4},{6,5},{7,6},{0,7},{9,8},{10,9},{11,1... | collective-permute-start | bytes 98312 | tf_op jit(solution)/shard_map/ppermute | solution.py:497
  90.7 8.6 %collective-permute-start.6 = (f32[56,512]{1,0:T(8,128)S(1)}, f32[56,512]{1,0:T(8,128)S(1)}, u32[]{:S(2)}, u32[]{:S(2)}) collective-permute-start(f32[56,512]{1,0:T(8,128)S(1)} %shard_map.212.refs_9_.refs_2_), channel_id=1, source_target_pairs={{8,0},{16,8},{24,16},{32,24},{40,32},{48,40},{56,48},{64,56},{72,6... | collective-permute-start | bytes 344072 | tf_op jit(solution)/shard_map/ppermute | solution.py:495
  95.5 8.1 %collective-permute-start.5 = (f32[56,512]{1,0:T(8,128)S(1)}, f32[56,512]{1,0:T(8,128)S(1)}, u32[]{:S(2)}, u32[]{:S(2)}) collective-permute-start(f32[56,512]{1,0:T(8,128)S(1)} %shard_map.212.refs_9_.refs_2_), channel_id=1, source_target_pairs={{120,0},{0,8},{8,16},{16,24},{24,32},{32,40},{40,48},{48,56},{56,6... | collective-permute-start | bytes 344072 | tf_op jit(solution)/shard_map/ppermute | solution.py:495
  95.5 8.1 %copy-start = (bf16[1536,256]{1,0:T(8,128)(2,1)S(1)}, bf16[1536,256]{1,0:T(8,128)(2,1)}, u32[]{:S(2)}) copy-start(bf16[1536,256]{1,0:T(8,128)(2,1)} %constant.45.clone.refs_6_.refs_4_) | copy-start | bytes 2359300
  95.5 8.1 %copy-start.2 = (bf16[768,256]{1,0:T(8,128)(2,1)S(1)}, bf16[768,256]{1,0:T(8,128)(2,1)}, u32[]{:S(2)}) copy-start(bf16[768,256]{1,0:T(8,128)(2,1)} %constant.46.clone.refs_7_.refs_5_) | copy-start | bytes 1179652
  95.6 8.1 %copy-start.5 = (bf16[136,288]{1,0:T(8,128)(2,1)S(1)}, bf16[136,288]{1,0:T(8,128)(2,1)}, u32[]{:S(2)}) copy-start(bf16[136,288]{1,0:T(8,128)(2,1)} %constant.47.clone.refs_11_) | copy-start | bytes 235012
  95.6 8.1 %copy-start.7 = (bf16[80,504]{1,0:T(8,128)(2,1)S(1)}, bf16[80,504]{1,0:T(8,128)(2,1)}, u32[]{:S(2)}) copy-start(bf16[80,504]{1,0:T(8,128)(2,1)} %constant.43.clone.refs_4_) | copy-start | bytes 241924
  95.6 8.1 %copy-start.8 = (bf16[24,240]{1,0:T(8,128)(2,1)S(1)}, bf16[24,240]{1,0:T(8,128)(2,1)}, u32[]{:S(2)}) copy-start(bf16[24,240]{1,0:T(8,128)(2,1)} %constant.44.clone.refs_5_) | copy-start | bytes 34564
  95.6 10.8 %copy-start.10 = (bf16[384,1152]{1,0:T(8,128)(2,1)S(1)}, bf16[384,1152]{1,0:T(8,128)(2,1)}, u32[]{:S(2)}) copy-start(bf16[384,1152]{1,0:T(8,128)(2,1)} %constant.49.clone.refs_4_) | copy-start | bytes 2654212
  95.6 10.8 %copy-start.12 = (bf16[384,864]{1,0:T(8,128)(2,1)S(1)}, bf16[384,864]{1,0:T(8,128)(2,1)}, u32[]{:S(2)}) copy-start(bf16[384,864]{1,0:T(8,128)(2,1)} %constant.48.clone.refs_3_) | copy-start | bytes 1990660
  95.6 10.8 %copy-start.13 = (bf16[384,288]{1,0:T(8,128)(2,1)S(1)}, bf16[384,288]{1,0:T(8,128)(2,1)}, u32[]{:S(2)}) copy-start(bf16[384,288]{1,0:T(8,128)(2,1)} %constant.50.clone.refs_5_) | copy-start | bytes 663556
  106.0 11.6 %collective-permute-start.9 = (f32[24,1024]{1,0:T(8,128)S(1)}, f32[24,1024]{1,0:T(8,128)S(1)}, u32[]{:S(2)}, u32[]{:S(2)}) collective-permute-start(f32[24,1024]{1,0:T(8,128)S(1)} %get-tuple-element.42), channel_id=1, source_target_pairs={{127,0},{120,1},{121,2},{122,3},{123,4},{124,5},{125,6},{126,7},{7... | collective-permute-start | bytes 294920 | tf_op jit(solution)/shard_map/ppermute | solution.py:503
  106.1 11.5 %collective-permute-start.8 = (f32[80,1024]{1,0:T(8,128)S(1)}, f32[80,1024]{1,0:T(8,128)S(1)}, u32[]{:S(2)}, u32[]{:S(2)}) collective-permute-start(f32[80,1024]{1,0:T(8,128)S(1)} %get-tuple-element.41), channel_id=1, source_target_pairs={{7,0},{0,1},{1,2},{2,3},{3,4},{4,5},{5,6},{6,7},{15,8},{8,9},{9,10... | collective-permute-start | bytes 983048 | tf_op jit(solution)/shard_map/ppermute | solution.py:497
  106.1 18.1 %collective-permute-start.7 = (f32[120,1024]{1,0:T(8,128)S(1)}, f32[120,1024]{1,0:T(8,128)S(1)}, u32[]{:S(2)}, u32[]{:S(2)}) collective-permute-start(f32[120,1024]{1,0:T(8,128)S(1)} %get-tuple-element.40), channel_id=1, source_target_pairs={{120,0},{0,8},{8,16},{16,24},{24,32},{32,40},{40,48},{48,56},{56,6... | collective-permute-start | bytes 1474568 | tf_op jit(solution)/shard_map/ppermute | solution.py:495
  106.4 17.8 %copy-start.3 = (bf16[384,408]{1,0:T(8,128)(2,1)S(1)}, bf16[384,408]{1,0:T(8,128)(2,1)}, u32[]{:S(2)}) copy-start(bf16[384,408]{1,0:T(8,128)(2,1)} %constant.51.clone.refs_6_) | copy-start | bytes 940036

commit v3 on v2

--- a/solution.py
+++ b/solution.py
@@ -130,9 +130,8 @@
     bands = outer(bands_i, bands_c, True)
     wide = cols + 2 * SIDE
     order = []
-    for block in range(3):
-        for first, size in ((0, SIDE), (SIDE, cols), (SIDE + cols, SIDE)):
-            order += [(block * rows + r) * wide + first + c for r in range(rows) for c in range(size)]
+    for first, size in ((0, SIDE), (SIDE, cols), (SIDE + cols, SIDE)):
+        order += [r * wide + first + c for r in range(rows + 2 * SIDE) for c in range(size)]
     back = outer(back_i.T, back_c.T, True).T
     return bands[:, order], back
 
@@ -197,6 +196,13 @@
 
 def shrink(value, limit):
     return value - jnp.clip(value, -limit, limit)
+
+
+def tail_rows(rows, count):
+    row = lax.broadcasted_iota(jnp.int32, (rows, count), 0)
+    tail = lax.broadcasted_iota(jnp.int32, (rows, count), 1)
+    each = GROUP - SLOTS
+    return (row == tail // each * GROUP + SLOTS + tail % each).astype(f32).astype(bf16)
 
 
 def route_kernel(dest_far, bin_far, traces_far, out_far, dest_ref, bin_ref, traces_ref, out_ref, in_sems, out_sems):
@@ -243,15 +249,19 @@
     )
     out_ref[:, 3 * span :] = labels.astype(bf16)
     send(3, 3 * span, LANES)
+    count = GROUP - SLOTS
+    tail_at = lax.broadcasted_iota(jnp.int32, (count * tiles, traces), 0)
+    put = tail_rows(rows, count * tiles)
     coming[2].wait()
     tail = traces_ref[:, 3 * span : samples]
     for j in range(3):
-        tail_row = jnp.where(place == j, SLOTS, jnp.where(place == 3 + j, SLOTS + 1, -rows * GROUP))
-        extra = (row_at == dest * GROUP + tail_row).astype(f32).astype(bf16)
+        tail_row = jnp.where(place == j, 0, jnp.where(place == 3 + j, 1, -rows))
+        extra = (tail_at == dest * count + tail_row).astype(f32).astype(bf16)
+        rest = dot(extra, tail).astype(bf16)
         at = slice(j * span, (j + 1) * span)
         coming[3 + j].wait()
-        both = jnp.concatenate([traces_ref[:, at], tail], 0)
-        out_ref[:, at] = dot(jnp.concatenate([main, extra], 1), both).astype(bf16)
+        both = jnp.concatenate([traces_ref[:, at], rest], 0)
+        out_ref[:, at] = dot(jnp.concatenate([main, put], 1), both).astype(bf16)
         send(j, j * span, span)
     for copy in going:
         copy.wait()
@@ -348,7 +358,7 @@
         high_ref[:, where] = left_dot(own_ref[...], jnp.concatenate([highs[b], highs[b + 1]], 1))
 
 
-def middle_kernel(cols, thr_ref, own_ref, edge_ref, s0, s1, s2, time_ref, shrunk_ref, timed_ref, first_out, last_out):
+def middle_kernel(thr_ref, own_ref, edge_ref, s0, s1, s2, time_ref, shrunk_ref, timed_ref):
     quarter = shrunk_ref.shape[0] // 4
     half = shrunk_ref.shape[1] // 2
     matrix = edge_ref[...]
@@ -371,18 +381,35 @@
     for b in range(len(coarse)):
         for base, piece in ((0, lows[b]), (half // 2, highs[b])):
             timed_ref[:, base + b * LANES : base + (b + 1) * LANES] = piece
-    starts = range(0, timed_ref.shape[0], cols)
-    first_out[...] = jnp.concatenate([timed_ref[at : at + SIDE] for at in starts], 0)
-    last_out[...] = jnp.concatenate([timed_ref[at + cols - SIDE : at + cols] for at in starts], 0)
-
-
-def join_kernel(left_ref, own_ref, right_ref, out_ref):
-    out_ref[...] = jnp.concatenate([left_ref[...], own_ref[...], right_ref[...]], 0)
+
+
+def sides_kernel(cols, before, own, after, stack_out, first_out, last_out):
+    stack_out[...] = jnp.concatenate([before[...], own[...], after[...]], 0)
+    starts = range(0, stack_out.shape[0], cols)
+    first_out[...] = jnp.concatenate([stack_out[at : at + SIDE] for at in starts], 0)
+    last_out[...] = jnp.concatenate([stack_out[at + cols - SIDE : at + cols] for at in starts], 0)
 
 
 def details_kernel(
-    thr_ref, low_in, high_in, edge_ref, s0, s1, s2, back_low, back_ref, low_out, high_out, low_states, high_states
+    thr_ref,
+    low_in,
+    high_in,
+    edge_ref,
+    s0,
+    s1,
+    s2,
+    back_low,
+    back_ref,
+    next_in,
+    time_t,
+    low_out,
+    high_out,
+    low_states,
+    high_states,
+    next_out,
 ):
+    for b, block in enumerate(time_pairs(next_in[...], time_t[...])):
+        next_out[:, b * BLOCK : (b + 1) * BLOCK] = block
     quarter = low_in.shape[0] // 4
     for where in steps(low_in):
         low, high = take_joint((s0, s1, s2), where)
@@ -418,7 +445,6 @@
     for q in range(1, 4):
         limit = jnp.where(row >= q * quarter, jnp.where(high, thr_ref[2, 2 * q], thr_ref[2, 2 * q - 1]), limit)
     rebuilt = left_dot(back_m[...], shrink(bands, limit))
-    details = time_pairs(next_in[...], time_t[...])
     lows = []
     for block in time_pairs(rebuilt, time_t[...]):
         lows += [block[:, b : b + LANES] for b in range(0, BLOCK, LANES)]
@@ -426,7 +452,7 @@
     count = low_states.shape[0]
     for b, block in enumerate(synthesis_from_low(lows, time_low[...])):
         where = slice(b * BLOCK, (b + 1) * BLOCK)
-        bands = jnp.concatenate([details[b][:rows] + block, details[b][rows:]], 0)
+        bands = jnp.concatenate([next_in[:rows, where] + block, next_in[rows:, where]], 0)
         next_out[:, where] = bands
         states = left_dot(back_ref[...], bands)
         low = jnp.concatenate([states[:count] + low_states[:, where], states[count:]], 0)
@@ -504,7 +530,9 @@
 
 
 def exchange(states, ahead):
-    return [shift(states[0], ahead, 0), shift(states[1], 0, ahead), shift(states[2], ahead, ahead)]
+    corner = shift(states[2], ahead, ahead)
+    column = shift(states[1], 0, ahead)
+    return [shift(states[0], ahead, 0), column, corner]
 
 
 def on_device(traces, dest_tile, bin_in_tile, fold, thresholds):
@@ -572,12 +600,12 @@
         time_matrix,
         triple(own0, 1),
         triple(own1, 1),
-        cost=8e9,
-    )
-    side_shape = ((rows2 * SIDE, samples // 4), f32)
-    shrunk1, timed, firsts, lasts = call(
-        functools.partial(middle_kernel, cols2),
-        [((quarter, half), f32), ((last, half // 2), f32), side_shape, side_shape],
+        cost=1e9,
+    )
+    rows_all = rows2 + 2 * SIDE
+    shrunk1, timed = call(
+        middle_kernel,
+        [((quarter, half), f32), ((last, half // 2), f32)],
         thresholds,
         own_next,
         triple(edge1, 1),
@@ -585,18 +613,12 @@
         time_matrix,
         smem=(0,),
     )
-    sides = shift(lasts, 0, -1), shift(firsts, 0, 1)
-    (wide,) = call(
-        join_kernel,
-        [((last + 2 * rows2 * SIDE, samples // 4), f32)],
-        sides[0],
-        timed,
-        sides[1],
-    )
-    before, behind = shift(wide, -1, 0), shift(wide, 1, 0)
-    low_details, high_details, low_states, high_states = call(
+    before, behind = shift(timed, -1, 0), shift(timed, 1, 0)
+    low_details, high_details, low_states, high_states, next_details = call(
         details_kernel,
-        [((bins - quarter, half), f32), ((bins, half), f32)] + [((count0, half), f32)] * 2,
+        [((bins - quarter, half), f32), ((bins, half), f32)]
+        + [((count0, half), f32)] * 2
+        + [((quarter, half), f32)],
         thresholds,
         own_low,
         own_high,
@@ -604,22 +626,33 @@
         *states,
         triple(edge0[quarter:].T, 1),
         triple(edge0.T, 1),
+        shrunk1,
+        time_back,
         smem=(0,),
-        after=(wide,),
-        cost=6e9,
-    )
+        after=(timed,),
+        cost=1e9,
+    )
+    stack, firsts, lasts = call(
+        functools.partial(sides_kernel, cols2),
+        [((rows_all * size, samples // 4), f32) for size in (cols2, SIDE, SIDE)],
+        before,
+        timed,
+        behind,
+        after=(low_details,),
+    )
+    left, right = shift(lasts, 0, -1), shift(firsts, 0, 1)
     bands1, *states = call(
         deepest_kernel,
         [((quarter, half), f32)] + joint_shapes,
         thresholds,
-        before,
-        wide,
-        behind,
+        left,
+        stack,
+        right,
         triple(bands2, 1),
         triple(back2, 1),
         time_back,
         time_back_low,
-        shrunk1,
+        next_details,
         low_states,
         high_states,
         triple(edge1.T, 1),
@@ -637,7 +670,7 @@
         triple(own1.T, 1),
         time_back,
         scale,
-        cost=6e9,
+        cost=1e9,
     )
     (denoised,) = call(
         final_kernel,

time: 128 us -> 126 us (0.984)
  waiting for transfers between devices: 71.7 us -> 70.4 us
    ppermute x4, waiting for transfers between devices: 19.8 us -> 3.68 us  [shift(): lax.ppermute(block, 'inl', [((i + inline_by) % inline_devs, i) for i in r...]
    ppermute x2, waiting for transfers between devices: 6.13 us -> 20.4 us  [shift(): return lax.ppermute(block, ('inl', 'xl'), route)]
  transfers between devices with their start and end apart: 11 -> 11, of which waited for: 7 -> 6; matrix products, arithmetic and copies ran while one was open for 0% -> 0% of each run, Pallas kernels for 10% -> 11%
where the time goes in v3:
time: 126 us
  waiting for transfers between devices  70.4 us (56%)
  Pallas kernels  33.5 us (27%)
  starting transfers between devices  21.2 us (17%)
    all_to_all x1, waiting for transfers between devices, on_device(): lax.all_to_all(outgoing.reshape(devices, GROUP, width), ('inl', 'xl'), sp...  44 us
    pallas_call x9, Pallas kernels, call(): pl.pallas_call(body, out_shape=[jax.ShapeDtypeStruct(shape, dtype) for sh...  33.5 us
    ppermute x2, waiting for transfers between devices, shift(): return lax.ppermute(block, ('inl', 'xl'), route)  20.4 us
    all_to_all x1, starting transfers between devices, on_device(): lax.all_to_all(outgoing.reshape(devices, GROUP, width), ('inl', 'xl'), sp...  11.6 us
    ppermute x4, starting transfers between devices, shift(): lax.ppermute(block, 'inl', [((i + inline_by) % inline_devs, i) for i in r...  5.76 us
    ppermute x4, waiting for transfers between devices, shift(): lax.ppermute(block, 'inl', [((i + inline_by) % inline_devs, i) for i in r...  3.68 us
    ppermute x4, starting transfers between devices, shift(): lax.ppermute(block, 'xl', [((j + cross_by) % cross_devs, j) for j in rang...  2.98 us
  transfers between devices with their start and end apart: 11, of which 6 were waited for; matrix products, arithmetic and copies ran while one was open for 0% of the time, Pallas kernels for 11%

profile of v3, /device:TPU:0, one launch (start us, length us, event | category | flops | bytes accessed | tf_op | source)
XLA Modules:
  0.0 125.9 jit_solution(4932966283363577219)
XLA Ops:
  0.0 6.5 %shard_map.208 = bf16[1024,1664]{1,0:T(8,128)(2,1)} custom-call(s32[1,512]{1,0:T(1,128)} %bitcast.6, s32[1,512]{1,0:T(1,128)} %bitcast.7, bf16[512,2048]{1,0:T(8,128)(2,1)} %refs_2_.4), custom_call_target="tpu_custom_call" | custom-call | tf_op jit(solution)/shard_map/pallas_call | solution.py:503
  6.5 0.0 copy-start.18
  6.5 0.0 copy-start.1
  6.5 0.0 copy-start.7
  6.5 11.6 %all-to-all-start = ((bf16[128,8,1664]{2,1,0:T(8,128)(2,1)}), bf16[128,8,1664]{2,1,0:T(8,128)(2,1)}, u32[]{:S(2)}, u32[]{:S(2)}) async-start(bf16[128,8,1664]{2,1,0:T(8,128)(2,1)} %bitcast.5), calls=%async_computation | async-start | bytes 6815744 | tf_op jit(solution)/shard_map/all_to_all | solution.py:562
  18.2 0.0 copy-done.18
  18.2 0.0 copy-start.4
  18.2 0.0 copy-start.11
  18.2 0.1 reshape.24.refs_1_.refs_7_
  18.3 44.0 %all-to-all-done = bf16[128,8,1664]{2,1,0:T(8,128)(2,1)} async-done(((bf16[128,8,1664]{2,1,0:T(8,128)(2,1)}), bf16[128,8,1664]{2,1,0:T(8,128)(2,1)}, u32[]{:S(2)}, u32[]{:S(2)}) %all-to-all-start) | async-done | bytes 3407904 | tf_op jit(solution)/shard_map/all_to_all | solution.py:562
  62.4 0.0 copy-done.1
  62.4 0.0 copy-done.7
  62.4 6.2 %shard_map.209 = (f32[384,2048]{1,0:T(8,128)S(1)}, f32[120,1024]{1,0:T(8,128)S(1)}, f32[80,1024]{1,0:T(8,128)S(1)}, f32[24,1024]{1,0:T(8,128)S(1)}) custom-call(bf16[1024,1664]{1,0:T(8,128)(2,1)} %bitcast.3.refs_0_, f32[384,1]{1,0:T(8,128)S(1)} %reshape.24.refs_1_.refs_7_, bf16[1152,256]{1,0:T(8,128)(2,1)S(1)} %copy-done.1, bf16[136,1152]{1,0:T(8,128)(2,1)S(1)} %copy-done.7), custom_call_target="tpu_custom_call" | custom-call | tf_op jit(solution)/shard_map/pallas_call | solution.py:503
  68.5 0.0 copy-start.14
  68.5 0.0 copy-start.16
  68.6 1.3 %collective-permute-start = (f32[120,1024]{1,0:T(8,128)S(1)}, f32[120,1024]{1,0:T(8,128)S(1)}, u32[]{:S(2)}, u32[]{:S(2)}) collective-permute-start(f32[120,1024]{1,0:T(8,128)S(1)} %get-tuple-element.29), channel_id=1, source_target_pairs={{8,0},{16,8},{24,16},{32,24},{40,32},{48,40},{56,48},{64,56},{72,6... | collective-permute-start | bytes 1474568 | tf_op jit(solution)/shard_map/ppermute | solution.py:521
  69.9 0.0 collective-permute-start.1
  69.9 0.5 collective-permute-start.2
  70.4 0.0 copy-done.4
  70.4 0.0 copy-done.11
  70.4 0.0 copy-start.10
  70.4 0.0 copy-start.12
  70.5 4.6 %shard_map.210 = (f32[384,1024]{1,0:T(8,128)S(1)}, f32[384,1024]{1,0:T(8,128)S(1)}, f32[96,1024]{1,0:T(8,128)S(1)}) custom-call(f32[384,2048]{1,0:T(8,128)S(1)} %get-tuple-element.26.refs_0_, bf16[1152,256]{1,0:T(8,128)(2,1)S(1)} %copy-done.1, bf16[384,1152]{1,0:T(8,128)(2,1)S(1)} %copy-done.4, bf16[96,1152]{1,0:T(8,128)(2,1)S(1)} %copy-done.11), custom_call_target="tpu_custom_call" | custom-call | flops 1000000000 | tf_op jit(solution)/shard_map/pallas_call | solution.py:503
  75.0 7.6 %collective-permute-done.2.refs_5_.refs_6_ = f32[24,1024]{1,0:T(8,128)S(1)} collective-permute-done((f32[24,1024]{1,0:T(8,128)S(1)}, f32[24,1024]{1,0:T(8,128)S(1)}, u32[]{:S(2)}, u32[]{:S(2)}) %collective-permute-start.2) | collective-permute-done | bytes 98336 | tf_op jit(solution)/shard_map/ppermute | solution.py:529
  82.6 0.0 collective-permute-done.1.refs_4_.refs_5_
  82.6 0.6 collective-permute-done.refs_3_.refs_4_
  83.2 0.0 copy-done.14
  83.2 0.0 copy-done.16
  83.2 1.5 %shard_map.211 = (f32[96,1024]{1,0:T(8,128)S(1)}, f32[24,512]{1,0:T(8,128)S(1)}) custom-call(f32[3,7]{1,0:T(4,128)S(1)} %copy-done.16, f32[96,1024]{1,0:T(8,128)S(1)} %get-tuple-element.32.refs_1_, bf16[96,408]{1,0:T(8,128)(2,1)S(1)} %copy-done.14, f32[120,1024]{1,0:T(8,128)S(1)} %collective-permute-done.refs_3_.refs_4_, ...), custom_call_target="tpu_custom_call" | custom-call | tf_op jit(solution)/shard_map/pallas_call | solution.py:503
  84.7 4.4 %collective-permute-start.4 = (f32[24,512]{1,0:T(8,128)S(1)}, f32[24,512]{1,0:T(8,128)S(1)}, u32[]{:S(2)}, u32[]{:S(2)}) collective-permute-start(f32[24,512]{1,0:T(8,128)S(1)} %get-tuple-element.34.refs_11_.refs_1_), channel_id=1, source_target_pairs={{8,0},{16,8},{24,16},{32,24},{40,32},{48,40},{56,48},{64,56},{72,6... | collective-permute-start | bytes 147464 | tf_op jit(solution)/shard_map/ppermute | solution.py:521
  89.1 0.0 collective-permute-start.3
  89.1 0.0 copy-done
  89.1 0.0 copy-done.9
  89.1 0.0 copy-done.10
  89.1 0.0 copy-done.12
  89.1 0.0 copy-start.2
  89.1 0.0 copy-start.13
  89.1 0.0 copy-start.15
  89.2 0.0 copy-start.17
  89.2 4.2 %shard_map.212 = (f32[288,1024]{1,0:T(8,128)S(1)}, f32[384,1024]{1,0:T(8,128)S(1)}, f32[96,1024]{1,0:T(8,128)S(1)}, f32[96,1024]{1,0:T(8,128)S(1)}, f32[96,1024]{1,0:T(8,128)S(1)}) custom-call(f32[3,7]{1,0:T(4,128)S(1)} %copy-done.16, f32[384,1024]{1,0:T(8,128)S(1)} %get-tuple-element.27.refs_1_, f32[384,1024]{1,0:T(8,128)S(1)} %get-tuple-element.28.refs_2_, ...), custom_call_target="tpu_custom_call" | custom-call | flops 1000000000 | tf_op jit(solution)/shard_map/pallas_call | solution.py:503
  93.4 0.0 copy-start.3
  93.4 0.0 copy-start.5
  93.4 0.0 copy-start.8
  93.4 0.0 collective-permute-done.4.refs_2_
  93.4 3.1 %collective-permute-done.3.refs_0_ = f32[24,512]{1,0:T(8,128)S(1)} collective-permute-done((f32[24,512]{1,0:T(8,128)S(1)}, f32[24,512]{1,0:T(8,128)S(1)}, u32[]{:S(2)}, u32[]{:S(2)}) %collective-permute-start.3) | collective-permute-done | bytes 49184 | tf_op jit(solution)/shard_map/ppermute | solution.py:521
  96.5 0.0 collective-permute-start.5
  96.6 2.9 %collective-permute-start.6 = (f32[48,512]{1,0:T(8,128)S(1)}, f32[48,512]{1,0:T(8,128)S(1)}, u32[]{:S(2)}, u32[]{:S(2)}) collective-permute-start(f32[48,512]{1,0:T(8,128)S(1)} %get-tuple-element.39), channel_id=1, source_target_pairs={{1,0},{2,1},{3,2},{4,3},{5,4},{6,5},{7,6},{0,7},{9,8},{10,9},{11,1... | collective-permute-start | bytes 294920 | tf_op jit(solution)/shard_map/ppermute | solution.py:523
  99.5 2.3 %collective-permute-done.5.refs_1_ = f32[48,512]{1,0:T(8,128)S(1)} collective-permute-done((f32[48,512]{1,0:T(8,128)S(1)}, f32[48,512]{1,0:T(8,128)S(1)}, u32[]{:S(2)}, u32[]{:S(2)}) %collective-permute-start.5) | collective-permute-done | bytes 98336 | tf_op jit(solution)/shard_map/ppermute | solution.py:523
  101.8 0.0 collective-permute-done.6.refs_3_
  101.8 0.0 copy-done.2
  101.8 0.0 copy-done.13
  101.8 0.0 copy-done.15
  101.8 0.0 copy-done.17
  101.8 1.9 %shard_map.214 = (f32[96,1024]{1,0:T(8,128)S(1)}, f32[120,1024]{1,0:T(8,128)S(1)}, f32[80,1024]{1,0:T(8,128)S(1)}, f32[24,1024]{1,0:T(8,128)S(1)}) custom-call(f32[3,7]{1,0:T(4,128)S(1)} %copy-done.16, f32[48,512]{1,0:T(8,128)S(1)} %collective-permute-done.5.refs_1_, f32[72,512]{1,0:T(8,128)S(1)} %get-tuple-element.38.refs_2_, ...), custom_call_target="tpu_custom_call" | custom-call | tf_op jit(solution)/shard_map/pallas_call | solution.py:503
  103.7 0.1 collective-permute-start.7
  103.8 0.0 collective-permute-start.8
  103.9 0.3 collective-permute-start.9
  104.2 0.0 copy-start.6
  104.2 4.9 %shard_map.215.refs_0_ = f32[384,2048]{1,0:T(8,128)S(1)} custom-call(f32[288,1024]{1,0:T(8,128)S(1)} %get-tuple-element.35.refs_3_.refs_0_, f32[384,1024]{1,0:T(8,128)S(1)} %get-tuple-element.36.refs_1_, f32[96,1024]{1,0:T(8,128)S(1)} %get-tuple-element.43.refs_2_, bf16[384,864]{1,0:T(8,128)(2,1)S(1)} %copy-done.5, bf16[384,1152]{1,0:T(8,128)(2,1)S(1)} %copy-done.3, ...), custom_call_target="tpu_custom_call" | custom-call | flops 1000000000 | tf_op jit(solution)/shard_map/pallas_call | solution.py:503
  109.1 12.8 %collective-permute-done.9.refs_3_ = f32[24,1024]{1,0:T(8,128)S(1)} collective-permute-done((f32[24,1024]{1,0:T(8,128)S(1)}, f32[24,1024]{1,0:T(8,128)S(1)}, u32[]{:S(2)}, u32[]{:S(2)}) %collective-permute-start.9) | collective-permute-done | bytes 98336 | tf_op jit(solution)/shard_map/ppermute | solution.py:529
  122.0 0.0 collective-permute-done.8.refs_2_
  122.0 0.0 collective-permute-done.7.refs_1_
  122.0 0.0 copy-done.6
  122.0 3.7 %shard_map.216 = f32[384,2048]{1,0:T(8,128)} custom-call(f32[384,2048]{1,0:T(8,128)S(1)} %shard_map.215.refs_0_, f32[120,1024]{1,0:T(8,128)S(1)} %collective-permute-done.7.refs_1_, f32[80,1024]{1,0:T(8,128)S(1)} %collective-permute-done.8.refs_2_, f32[24,1024]{1,0:T(8,128)S(1)} %collective-permute-done.9.refs_3_, bf16[1536,256]{1,0:T(8,128)(2,1)S(1)} %copy-done, ...), custom_call_target="tpu_custom_call" | custom-call | tf_op jit(solution)/shard_map/pallas_call | solution.py:503
  (7 shorter events, 0.1 us)
Async XLA Ops:
  6.5 11.7 %copy-start.18 = (s32[16,24]{1,0:T(8,128)S(1)}, s32[16,24]{1,0:T(8,128)}, u32[]{:S(2)}) copy-start(s32[16,24]{1,0:T(8,128)} %param.25) | copy-start | bytes 4612
  6.5 55.8 %copy-start.1 = (bf16[1152,256]{1,0:T(8,128)(2,1)S(1)}, bf16[1152,256]{1,0:T(8,128)(2,1)}, u32[]{:S(2)}) copy-start(bf16[1152,256]{1,0:T(8,128)(2,1)} %constant.17.clone.refs_2_.refs_1_.refs_6_) | copy-start | bytes 1769476
  6.5 55.8 %copy-start.7 = (bf16[136,1152]{1,0:T(8,128)(2,1)S(1)}, bf16[136,1152]{1,0:T(8,128)(2,1)}, u32[]{:S(2)}) copy-start(bf16[136,1152]{1,0:T(8,128)(2,1)} %constant.36.clone.refs_3_) | copy-start | bytes 940036
  6.5 55.8 %all-to-all-start = ((bf16[128,8,1664]{2,1,0:T(8,128)(2,1)}), bf16[128,8,1664]{2,1,0:T(8,128)(2,1)}, u32[]{:S(2)}, u32[]{:S(2)}) async-start(bf16[128,8,1664]{2,1,0:T(8,128)(2,1)} %bitcast.5), calls=%async_computation | async-start | bytes 6815744 | tf_op jit(solution)/shard_map/all_to_all | solution.py:562
  18.2 52.2 %copy-start.4 = (bf16[384,1152]{1,0:T(8,128)(2,1)S(1)}, bf16[384,1152]{1,0:T(8,128)(2,1)}, u32[]{:S(2)}) copy-start(bf16[384,1152]{1,0:T(8,128)(2,1)} %constant.37.clone.refs_2_) | copy-start | bytes 2654212
  18.2 52.2 %copy-start.11 = (bf16[96,1152]{1,0:T(8,128)(2,1)S(1)}, bf16[96,1152]{1,0:T(8,128)(2,1)}, u32[]{:S(2)}) copy-start(bf16[96,1152]{1,0:T(8,128)(2,1)} %constant.38.clone.refs_3_) | copy-start | bytes 663556
  68.5 14.7 %copy-start.14 = (bf16[96,408]{1,0:T(8,128)(2,1)S(1)}, bf16[96,408]{1,0:T(8,128)(2,1)}, u32[]{:S(2)}) copy-start(bf16[96,408]{1,0:T(8,128)(2,1)} %constant.39.clone.refs_2_) | copy-start | bytes 235012
  68.5 14.7 %copy-start.16 = (f32[3,7]{1,0:T(4,128)S(1)}, f32[3,7]{1,0:T(4,128)}, u32[]{:S(2)}) copy-start(f32[3,7]{1,0:T(4,128)} %refs_0_.5) | copy-start | bytes 256
  68.6 14.7 %collective-permute-start = (f32[120,1024]{1,0:T(8,128)S(1)}, f32[120,1024]{1,0:T(8,128)S(1)}, u32[]{:S(2)}, u32[]{:S(2)}) collective-permute-start(f32[120,1024]{1,0:T(8,128)S(1)} %get-tuple-element.29), channel_id=1, source_target_pairs={{8,0},{16,8},{24,16},{32,24},{40,32},{48,40},{56,48},{64,56},{72,6... | collective-permute-start | bytes 1474568 | tf_op jit(solution)/shard_map/ppermute | solution.py:521
  69.9 12.8 %collective-permute-start.1 = (f32[80,1024]{1,0:T(8,128)S(1)}, f32[80,1024]{1,0:T(8,128)S(1)}, u32[]{:S(2)}, u32[]{:S(2)}) collective-permute-start(f32[80,1024]{1,0:T(8,128)S(1)} %get-tuple-element.30), channel_id=1, source_target_pairs={{1,0},{2,1},{3,2},{4,3},{5,4},{6,5},{7,6},{0,7},{9,8},{10,9},{11,1... | collective-permute-start | bytes 983048 | tf_op jit(solution)/shard_map/ppermute | solution.py:523
  69.9 12.8 %collective-permute-start.2 = (f32[24,1024]{1,0:T(8,128)S(1)}, f32[24,1024]{1,0:T(8,128)S(1)}, u32[]{:S(2)}, u32[]{:S(2)}) collective-permute-start(f32[24,1024]{1,0:T(8,128)S(1)} %get-tuple-element.31), channel_id=1, source_target_pairs={{9,0},{10,1},{11,2},{12,3},{13,4},{14,5},{15,6},{8,7},{17,8},{18,9... | collective-permute-start | bytes 294920 | tf_op jit(solution)/shard_map/ppermute | solution.py:529
  70.4 18.7 %copy-start = (bf16[1536,256]{1,0:T(8,128)(2,1)S(1)}, bf16[1536,256]{1,0:T(8,128)(2,1)}, u32[]{:S(2)}) copy-start(bf16[1536,256]{1,0:T(8,128)(2,1)} %constant.43.clone.refs_10_.refs_6_.refs_4_) | copy-start | bytes 2359300
  70.4 18.7 %copy-start.9 = (bf16[384,288]{1,0:T(8,128)(2,1)S(1)}, bf16[384,288]{1,0:T(8,128)(2,1)}, u32[]{:S(2)}) copy-start(bf16[384,288]{1,0:T(8,128)(2,1)} %constant.40.clone.refs_3_) | copy-start | bytes 663556
  70.4 18.7 %copy-start.10 = (bf16[96,1152]{1,0:T(8,128)(2,1)S(1)}, bf16[96,1152]{1,0:T(8,128)(2,1)}, u32[]{:S(2)}) copy-start(bf16[96,1152]{1,0:T(8,128)(2,1)} %constant.42.clone.refs_8_) | copy-start | bytes 663556
  70.4 18.7 %copy-start.12 = (bf16[96,864]{1,0:T(8,128)(2,1)S(1)}, bf16[96,864]{1,0:T(8,128)(2,1)}, u32[]{:S(2)}) copy-start(bf16[96,864]{1,0:T(8,128)(2,1)} %constant.41.clone.refs_7_) | copy-start | bytes 497668
  84.7 8.7 %collective-permute-start.4 = (f32[24,512]{1,0:T(8,128)S(1)}, f32[24,512]{1,0:T(8,128)S(1)}, u32[]{:S(2)}, u32[]{:S(2)}) collective-permute-start(f32[24,512]{1,0:T(8,128)S(1)} %get-tuple-element.34.refs_11_.refs_1_), channel_id=1, source_target_pairs={{8,0},{16,8},{24,16},{32,24},{40,32},{48,40},{56,48},{64,56},{72,6... | collective-permute-start | bytes 147464 | tf_op jit(solution)/shard_map/ppermute | solution.py:521
  89.1 7.4 %collective-permute-start.3 = (f32[24,512]{1,0:T(8,128)S(1)}, f32[24,512]{1,0:T(8,128)S(1)}, u32[]{:S(2)}, u32[]{:S(2)}) collective-permute-start(f32[24,512]{1,0:T(8,128)S(1)} %get-tuple-element.34.refs_11_.refs_1_), channel_id=1, source_target_pairs={{120,0},{0,8},{8,16},{16,24},{24,32},{32,40},{40,48},{48,56},{56,6... | collective-permute-start | bytes 147464 | tf_op jit(solution)/shard_map/ppermute | solution.py:521
  89.1 12.7 %copy-start.2 = (bf16[768,256]{1,0:T(8,128)(2,1)S(1)}, bf16[768,256]{1,0:T(8,128)(2,1)}, u32[]{:S(2)}) copy-start(bf16[768,256]{1,0:T(8,128)(2,1)} %constant.46.clone.refs_7_.refs_5_) | copy-start | bytes 1179652
  89.1 12.7 %copy-start.13 = (bf16[136,288]{1,0:T(8,128)(2,1)S(1)}, bf16[136,288]{1,0:T(8,128)(2,1)}, u32[]{:S(2)}) copy-start(bf16[136,288]{1,0:T(8,128)(2,1)} %constant.47.clone.refs_11_) | copy-start | bytes 235012
  89.1 12.7 %copy-start.15 = (bf16[80,504]{1,0:T(8,128)(2,1)S(1)}, bf16[80,504]{1,0:T(8,128)(2,1)}, u32[]{:S(2)}) copy-start(bf16[80,504]{1,0:T(8,128)(2,1)} %constant.44.clone.refs_4_) | copy-start | bytes 241924
  89.2 12.7 %copy-start.17 = (bf16[24,240]{1,0:T(8,128)(2,1)S(1)}, bf16[24,240]{1,0:T(8,128)(2,1)}, u32[]{:S(2)}) copy-start(bf16[24,240]{1,0:T(8,128)(2,1)} %constant.45.clone.refs_5_) | copy-start | bytes 34564
  93.4 10.8 %copy-start.3 = (bf16[384,1152]{1,0:T(8,128)(2,1)S(1)}, bf16[384,1152]{1,0:T(8,128)(2,1)}, u32[]{:S(2)}) copy-start(bf16[384,1152]{1,0:T(8,128)(2,1)} %constant.49.clone.refs_4_) | copy-start | bytes 2654212
  93.4 10.8 %copy-start.5 = (bf16[384,864]{1,0:T(8,128)(2,1)S(1)}, bf16[384,864]{1,0:T(8,128)(2,1)}, u32[]{:S(2)}) copy-start(bf16[384,864]{1,0:T(8,128)(2,1)} %constant.48.clone.refs_3_) | copy-start | bytes 1990660
  93.4 10.8 %copy-start.8 = (bf16[384,288]{1,0:T(8,128)(2,1)S(1)}, bf16[384,288]{1,0:T(8,128)(2,1)}, u32[]{:S(2)}) copy-start(bf16[384,288]{1,0:T(8,128)(2,1)} %constant.50.clone.refs_5_) | copy-start | bytes 663556
  96.5 5.3 %collective-permute-start.5 = (f32[48,512]{1,0:T(8,128)S(1)}, f32[48,512]{1,0:T(8,128)S(1)}, u32[]{:S(2)}, u32[]{:S(2)}) collective-permute-start(f32[48,512]{1,0:T(8,128)S(1)} %get-tuple-element.37), channel_id=1, source_target_pairs={{7,0},{0,1},{1,2},{2,3},{3,4},{4,5},{5,6},{6,7},{15,8},{8,9},{9,10... | collective-permute-start | bytes 294920 | tf_op jit(solution)/shard_map/ppermute | solution.py:523
  96.6 5.2 %collective-permute-start.6 = (f32[48,512]{1,0:T(8,128)S(1)}, f32[48,512]{1,0:T(8,128)S(1)}, u32[]{:S(2)}, u32[]{:S(2)}) collective-permute-start(f32[48,512]{1,0:T(8,128)S(1)} %get-tuple-element.39), channel_id=1, source_target_pairs={{1,0},{2,1},{3,2},{4,3},{5,4},{6,5},{7,6},{0,7},{9,8},{10,9},{11,1... | collective-permute-start | bytes 294920 | tf_op jit(solution)/shard_map/ppermute | solution.py:523
  103.7 18.2 %collective-permute-start.7 = (f32[120,1024]{1,0:T(8,128)S(1)}, f32[120,1024]{1,0:T(8,128)S(1)}, u32[]{:S(2)}, u32[]{:S(2)}) collective-permute-start(f32[120,1024]{1,0:T(8,128)S(1)} %get-tuple-element.44), channel_id=1, source_target_pairs={{120,0},{0,8},{8,16},{16,24},{24,32},{32,40},{40,48},{48,56},{56,6... | collective-permute-start | bytes 1474568 | tf_op jit(solution)/shard_map/ppermute | solution.py:521
  103.8 18.1 %collective-permute-start.8 = (f32[80,1024]{1,0:T(8,128)S(1)}, f32[80,1024]{1,0:T(8,128)S(1)}, u32[]{:S(2)}, u32[]{:S(2)}) collective-permute-start(f32[80,1024]{1,0:T(8,128)S(1)} %get-tuple-element.45), channel_id=1, source_target_pairs={{7,0},{0,1},{1,2},{2,3},{3,4},{4,5},{5,6},{6,7},{15,8},{8,9},{9,10... | collective-permute-start | bytes 983048 | tf_op jit(solution)/shard_map/ppermute | solution.py:523
  103.9 18.1 %collective-permute-start.9 = (f32[24,1024]{1,0:T(8,128)S(1)}, f32[24,1024]{1,0:T(8,128)S(1)}, u32[]{:S(2)}, u32[]{:S(2)}) collective-permute-start(f32[24,1024]{1,0:T(8,128)S(1)} %get-tuple-element.46), channel_id=1, source_target_pairs={{127,0},{120,1},{121,2},{122,3},{123,4},{124,5},{125,6},{126,7},{7... | collective-permute-start | bytes 294920 | tf_op jit(solution)/shard_map/ppermute | solution.py:529
  104.2 17.8 %copy-start.6 = (bf16[384,408]{1,0:T(8,128)(2,1)S(1)}, bf16[384,408]{1,0:T(8,128)(2,1)}, u32[]{:S(2)}) copy-start(bf16[384,408]{1,0:T(8,128)(2,1)} %constant.51.clone.refs_6_) | copy-start | bytes 940036

commit v4 on v3

--- a/solution.py
+++ b/solution.py
@@ -17,6 +17,8 @@
 VMEM_LIMIT = 32 * 1024 * 1024
 LARGE_LIMIT = 62 * 1024 * 1024
 MIDDLE_LIMIT = 48 * 1024 * 1024
+TOP_CODE = 32767.0
+LAST_MARK = 880.0
 SIDE = 4
 
 low_taps = [
@@ -267,7 +269,7 @@
         copy.wait()
 
 
-def bin_kernel(arrived_far, scale_ref, time_ref, state_ref, summed_ref, s0, s1, s2, arrived_ref, sems):
+def bin_kernel(sizes, arrived_far, scale_ref, time_ref, state_ref, summed_ref, s0, s1, s2, arrived_ref, sems):
     outs = (s0, s1, s2)
     width = summed_ref.shape[1] // 4
     coming = []
@@ -311,32 +313,58 @@
         states = left_dot(matrix, piece)
         blocks += [states[:, b : b + BLOCK] for b in range(0, span, BLOCK)]
     lows, highs = time_analysis(blocks, time_ref[...])
-    for b in range(len(blocks)):
-        put_joint(outs, slice(b * LANES, (b + 1) * LANES), lows[b], highs[b])
-
-
-def put_joint(outs, where, low, high):
-    part = joint_parts(outs)
-    outs[0][:, where] = jnp.concatenate([low[part[0]], high[part[0]], low[part[3]]], 0)
-    outs[1][:, where] = jnp.concatenate([low[part[1]], high[part[1]], low[part[4]]], 0)
-    outs[2][:, where] = jnp.concatenate([low[part[2]], high[part[2]][:8]], 0)
-
-
-def joint_parts(refs):
-    rows, cols, corner = [ref.shape[0] for ref in refs]
-    ends = [0]
-    for size in (rows * 2 // 5, cols * 2 // 5, corner - 8, rows // 5, cols // 5):
-        ends.append(ends[-1] + size)
-    return [slice(ends[k], ends[k + 1]) for k in range(5)]
-
-
-def take_joint(refs, where):
-    rows, cols, corner = [ref.shape[0] for ref in refs]
-    r, c, d = rows * 2 // 5, cols * 2 // 5, corner - 8
-    m0, m1, m2 = [ref[:, where] for ref in refs]
-    low = jnp.concatenate([m0[:r], m1[:c], m2[:d], m0[2 * r :], m1[2 * c :]], 0)
-    high = jnp.concatenate([m0[r : 2 * r], m1[c : 2 * c], m2[d:], jnp.zeros((d - 8, m2.shape[1]), f32)], 0)
-    return low, high
+    put_joint(sizes, outs, lows, highs)
+
+
+def encode(pieces, out):
+    lane = lax.broadcasted_iota(jnp.int32, (out.shape[0], LANES), 1)
+    marks = jnp.zeros((out.shape[0], LANES), f32)
+    for b, piece in enumerate(pieces):
+        largest = jnp.max(jnp.abs(piece), 1, keepdims=True)
+        mark = jnp.clip(jnp.ceil(jnp.log2(largest) * 8.0), -LAST_MARK, LAST_MARK)
+        code = jnp.clip(jnp.round(piece * (jnp.exp2(mark * -0.125) * TOP_CODE)), -TOP_CODE, TOP_CODE)
+        out[:, b * LANES : (b + 1) * LANES] = code.astype(jnp.int32).astype(jnp.int16)
+        marks = jnp.where(lane == b, mark, marks)
+    out[:, len(pieces) * LANES :] = marks.astype(jnp.int32).astype(jnp.int16)
+
+
+def scales_of(refs):
+    marks = [ref[:, ref.shape[1] - LANES :].astype(jnp.int32).astype(f32) for ref in refs]
+    return [jnp.exp2(mark * 0.125) * (1.0 / TOP_CODE) for mark in marks]
+
+
+def decode(ref, scale, where):
+    pieces = []
+    for start in range(where.start, where.stop, LANES):
+        b = start // LANES
+        code = ref[:, start : start + LANES].astype(jnp.int32).astype(f32)
+        pieces.append(code * scale[:, b : b + 1])
+    return jnp.concatenate(pieces, 1)
+
+
+def put_joint(sizes, outs, lows, highs):
+    ends = np.cumsum([0] + sizes)
+    part = [slice(int(ends[k]), int(ends[k + 1])) for k in range(5)]
+
+    def message(rows, *pieces):
+        spare = rows - sum(piece.shape[0] for piece in pieces)
+        if spare:
+            pieces += (jnp.zeros((spare, LANES), f32),)
+        return jnp.concatenate(pieces, 0)
+
+    rows = [out.shape[0] for out in outs]
+    pairs = list(zip(lows, highs))
+    encode([message(rows[0], low[part[0]], high[part[0]], low[part[3]]) for low, high in pairs], outs[0])
+    encode([message(rows[1], low[part[1]], high[part[1]], low[part[4]]) for low, high in pairs], outs[1])
+    encode([message(rows[2], low[part[2]], high[part[2]][:8]) for low, high in pairs], outs[2])
+
+
+def take_joint(sizes, refs, scales, where):
+    r, c, d, further_r, further_c = sizes
+    m0, m1, m2 = [decode(ref, scale, where) for ref, scale in zip(refs, scales)]
+    low = [m0[:r], m1[:c], m2[:d], m0[2 * r : 2 * r + further_r], m1[2 * c : 2 * c + further_c]]
+    high = [m0[r : 2 * r], m1[c : 2 * c], m2[d : d + 8], jnp.zeros((d - 8, m2.shape[1]), f32)]
+    return jnp.concatenate(low, 0), jnp.concatenate(high, 0)
 
 
 def join_rows(refs, where):
@@ -358,13 +386,15 @@
         high_ref[:, where] = left_dot(own_ref[...], jnp.concatenate([highs[b], highs[b + 1]], 1))
 
 
-def middle_kernel(thr_ref, own_ref, edge_ref, s0, s1, s2, time_ref, shrunk_ref, timed_ref):
+def middle_kernel(sizes, thr_ref, own_ref, edge_ref, s0, s1, s2, time_ref, shrunk_ref, timed_ref):
     quarter = shrunk_ref.shape[0] // 4
     half = shrunk_ref.shape[1] // 2
     matrix = edge_ref[...]
     blocks = []
+    refs = (s0, s1, s2)
+    scales = scales_of(refs)
     for where in steps(own_ref):
-        low, _ = take_joint((s0, s1, s2), where)
+        low, _ = take_joint(sizes, refs, scales, where)
         blocks.append(own_ref[:, where] + left_dot(matrix, low))
     lows, highs = time_analysis(blocks, time_ref[...])
     for b in range(len(blocks)):
@@ -391,6 +421,7 @@
 
 
 def details_kernel(
+    sizes,
     thr_ref,
     low_in,
     high_in,
@@ -411,8 +442,10 @@
     for b, block in enumerate(time_pairs(next_in[...], time_t[...])):
         next_out[:, b * BLOCK : (b + 1) * BLOCK] = block
     quarter = low_in.shape[0] // 4
+    refs = (s0, s1, s2)
+    scales = scales_of(refs)
     for where in steps(low_in):
-        low, high = take_joint((s0, s1, s2), where)
+        low, high = take_joint(sizes, refs, scales, where)
         bands = low_in[quarter:, where] + left_dot(edge_ref[quarter:], low[: high.shape[0]])
         bands = [shrink(bands[(q - 1) * quarter : q * quarter], thr_ref[0, 2 * q - 1]) for q in range(1, 4)]
         bands = jnp.concatenate(bands, 0)
@@ -434,7 +467,7 @@
 
 
 def deepest_kernel(
-    thr_ref, before, own, after, bands_m, back_m, time_t, time_low, next_in, low_states, high_states, back_ref, next_out, *outs
+    sizes, thr_ref, before, own, after, bands_m, back_m, time_t, time_low, next_in, low_states, high_states, back_ref, next_out, *outs
 ):
     stack = jnp.concatenate([before[...], own[...], after[...]], 0)
     bands = left_dot(bands_m[...], stack)
@@ -450,13 +483,17 @@
         lows += [block[:, b : b + LANES] for b in range(0, BLOCK, LANES)]
     rows = rebuilt.shape[0]
     count = low_states.shape[0]
+    state_lows, state_highs = [], []
     for b, block in enumerate(synthesis_from_low(lows, time_low[...])):
         where = slice(b * BLOCK, (b + 1) * BLOCK)
         bands = jnp.concatenate([next_in[:rows, where] + block, next_in[rows:, where]], 0)
         next_out[:, where] = bands
         states = left_dot(back_ref[...], bands)
         low = jnp.concatenate([states[:count] + low_states[:, where], states[count:]], 0)
-        put_joint(outs, where, low, high_states[:, where])
+        for at in range(0, BLOCK, LANES):
+            state_lows.append(low[:, at : at + LANES])
+            state_highs.append(high_states[:, where.start + at : where.start + at + LANES])
+    put_joint(sizes, outs, state_lows, state_highs)
 
 
 def own_back_kernel(low_in, high_in, next_in, low_t, high_t, next_t, time_t, scale_ref, out_ref):
@@ -471,10 +508,12 @@
         out_ref[:, b * BLOCK : (b + 1) * BLOCK] = block * scale
 
 
-def final_kernel(own_ref, s0, s1, s2, time_t, time_low, state_t, scale_ref, out_far, out_ref, sems):
+def final_kernel(sizes, own_ref, s0, s1, s2, time_t, time_low, state_t, scale_ref, out_far, out_ref, sems):
     pairs, lows = [], []
-    for start in range(0, s0.shape[1], LANES):
-        low, high = take_joint((s0, s1, s2), slice(start, start + LANES))
+    refs = (s0, s1, s2)
+    scales = scales_of(refs)
+    for start in range(0, own_ref.shape[1] // 2, LANES):
+        low, high = take_joint(sizes, refs, scales, slice(start, start + LANES))
         count = high.shape[0]
         pairs.append(jnp.concatenate([low[:count], high], 1))
         lows.append(low[count:])
@@ -575,14 +614,11 @@
     assert rows2 == SIDE and cols2 >= SIDE
     bands2, back2 = side_matrices(rows2, cols2)
     count0 = sum(sizes[:3])
-    joint_shapes = [
-        ((2 * sizes[0] + sizes[3], half), f32),
-        ((2 * sizes[1] + sizes[4], half), f32),
-        ((sizes[2] + 8, half), f32),
-    ]
+    joint_rows = [2 * sizes[0] + sizes[3], 2 * sizes[1] + sizes[4], sizes[2] + 8]
+    joint_shapes = [((-(-rows // 16) * 16, half + LANES), jnp.int16) for rows in joint_rows]
 
     summed, *states = call(
-        bin_kernel,
+        functools.partial(bin_kernel, sizes),
         [((bins, samples), f32)] + joint_shapes,
         arrived,
         scale,
@@ -604,7 +640,7 @@
     )
     rows_all = rows2 + 2 * SIDE
     shrunk1, timed = call(
-        middle_kernel,
+        functools.partial(middle_kernel, sizes),
         [((quarter, half), f32), ((last, half // 2), f32)],
         thresholds,
         own_next,
@@ -615,7 +651,7 @@
     )
     before, behind = shift(timed, -1, 0), shift(timed, 1, 0)
     low_details, high_details, low_states, high_states, next_details = call(
-        details_kernel,
+        functools.partial(details_kernel, sizes),
         [((bins - quarter, half), f32), ((bins, half), f32)]
         + [((count0, half), f32)] * 2
         + [((quarter, half), f32)],
@@ -642,7 +678,7 @@
     )
     left, right = shift(lasts, 0, -1), shift(firsts, 0, 1)
     bands1, *states = call(
-        deepest_kernel,
+        functools.partial(deepest_kernel, sizes),
         [((quarter, half), f32)] + joint_shapes,
         thresholds,
         left,
@@ -673,7 +709,7 @@
         cost=1e9,
     )
     (denoised,) = call(
-        final_kernel,
+        functools.partial(final_kernel, sizes),
         [((bins, samples), f32)],
         own_back,
         *states,

time: 126 us -> 118 us (0.937)
  waiting for transfers between devices: 70.4 us -> 60.9 us
    ppermute x2, waiting for transfers between devices: 20.4 us -> 10.6 us  [shift(): return lax.ppermute(block, ('inl', 'xl'), route)]
  transfers between devices with their start and end apart: 11 -> 11, of which waited for: 6 -> 6; matrix products, arithmetic and copies ran while one was open for 0% -> 0% of each run, Pallas kernels for 11% -> 12%
where the time goes in v4:
time: 118 us; the launch traced here: 117 us
  waiting for transfers between devices  60.9 us (52%)
  Pallas kernels  34.2 us (29%)
  starting transfers between devices  21.5 us (18%)
    all_to_all x1, waiting for transfers between devices, on_device(): lax.all_to_all(outgoing.reshape(devices, GROUP, width), ('inl', 'xl'), sp...  44 us
    pallas_call x9, Pallas kernels, call(): pl.pallas_call(body, out_shape=[jax.ShapeDtypeStruct(shape, dtype) for sh...  34.2 us
    all_to_all x1, starting transfers between devices, on_device(): lax.all_to_all(outgoing.reshape(devices, GROUP, width), ('inl', 'xl'), sp...  11.6 us
    ppermute x2, waiting for transfers between devices, shift(): return lax.ppermute(block, ('inl', 'xl'), route)  10.6 us
    ppermute x4, starting transfers between devices, shift(): lax.ppermute(block, 'inl', [((i + inline_by) % inline_devs, i) for i in r...  6 us
    ppermute x4, waiting for transfers between devices, shift(): lax.ppermute(block, 'inl', [((i + inline_by) % inline_devs, i) for i in r...  3.97 us
    ppermute x4, starting transfers between devices, shift(): lax.ppermute(block, 'xl', [((j + cross_by) % cross_devs, j) for j in rang...  2.98 us
  transfers between devices with their start and end apart: 11, of which 6 were waited for; matrix products, arithmetic and copies ran while one was open for 0% of the time, Pallas kernels for 12%

profile of v4, /device:TPU:0, one launch (start us, length us, event | category | flops | bytes accessed | tf_op | source)
XLA Modules:
  0.0 117.3 jit_solution(7617770451030088176)
XLA Ops:
  0.0 6.5 %shard_map.208 = bf16[1024,1664]{1,0:T(8,128)(2,1)} custom-call(s32[1,512]{1,0:T(1,128)} %bitcast.6, s32[1,512]{1,0:T(1,128)} %bitcast.7, bf16[512,2048]{1,0:T(8,128)(2,1)} %refs_2_.4), custom_call_target="tpu_custom_call" | custom-call | tf_op jit(solution)/shard_map/pallas_call | solution.py:542
  6.5 0.0 copy-start.18
  6.5 0.0 copy-start.1
  6.5 0.0 copy-start.7
  6.5 11.6 %all-to-all-start = ((bf16[128,8,1664]{2,1,0:T(8,128)(2,1)}), bf16[128,8,1664]{2,1,0:T(8,128)(2,1)}, u32[]{:S(2)}, u32[]{:S(2)}) async-start(bf16[128,8,1664]{2,1,0:T(8,128)(2,1)} %bitcast.5), calls=%async_computation | async-start | bytes 6815744 | tf_op jit(solution)/shard_map/all_to_all | solution.py:601
  18.2 0.0 copy-done.18
  18.2 0.0 copy-start.4
  18.2 0.0 copy-start.11
  18.2 0.1 reshape.24.refs_1_.refs_7_
  18.3 44.0 %all-to-all-done = bf16[128,8,1664]{2,1,0:T(8,128)(2,1)} async-done(((bf16[128,8,1664]{2,1,0:T(8,128)(2,1)}), bf16[128,8,1664]{2,1,0:T(8,128)(2,1)}, u32[]{:S(2)}, u32[]{:S(2)}) %all-to-all-start) | async-done | bytes 3407904 | tf_op jit(solution)/shard_map/all_to_all | solution.py:601
  62.4 0.0 copy-done.1
  62.4 0.0 copy-done.7
  62.4 6.4 %shard_map.209 = (f32[384,2048]{1,0:T(8,128)S(1)}, s16[128,1152]{1,0:T(8,128)(2,1)S(1)}, s16[80,1152]{1,0:T(8,128)(2,1)S(1)}, s16[32,1152]{1,0:T(8,128)(2,1)S(1)}) custom-call(bf16[1024,1664]{1,0:T(8,128)(2,1)} %bitcast.3.refs_0_, f32[384,1]{1,0:T(8,128)S(1)} %reshape.24.refs_1_.refs_7_, bf16[1152,256]{1,0:T(8,128)(2,1)S(1)} %copy-done.1, ...), custom_call_target="tpu_custom_call" | custom-call | tf_op jit(solution)/shard_map/pallas_call | solution.py:542
  68.8 0.0 copy-start.14
  68.8 0.0 copy-start.16
  68.8 1.3 %collective-permute-start = (s16[128,1152]{1,0:T(8,128)(2,1)S(1)}, s16[128,1152]{1,0:T(8,128)(2,1)S(1)}, u32[]{:S(2)}, u32[]{:S(2)}) collective-permute-start(s16[128,1152]{1,0:T(8,128)(2,1)S(1)} %get-tuple-element.29), channel_id=1, source_target_pairs={{8,0},{16,8},{24,16},{32,24},{40,32},{48,40},{56,48},{64,56},{72,6... | collective-permute-start | bytes 884744 | tf_op jit(solution)/shard_map/ppermute | solution.py:560
  70.1 0.0 collective-permute-start.1
  70.1 0.5 collective-permute-start.2
  70.6 0.0 copy-done.4
  70.6 0.0 copy-done.11
  70.7 0.0 copy-start.10
  70.7 0.0 copy-start.12
  70.7 4.6 %shard_map.210 = (f32[384,1024]{1,0:T(8,128)S(1)}, f32[384,1024]{1,0:T(8,128)S(1)}, f32[96,1024]{1,0:T(8,128)S(1)}) custom-call(f32[384,2048]{1,0:T(8,128)S(1)} %get-tuple-element.26.refs_0_, bf16[1152,256]{1,0:T(8,128)(2,1)S(1)} %copy-done.1, bf16[384,1152]{1,0:T(8,128)(2,1)S(1)} %copy-done.4, bf16[96,1152]{1,0:T(8,128)(2,1)S(1)} %copy-done.11), custom_call_target="tpu_custom_call" | custom-call | flops 1000000000 | tf_op jit(solution)/shard_map/pallas_call | solution.py:542
  75.3 2.5 %collective-permute-done.2.refs_5_.refs_6_ = s16[32,1152]{1,0:T(8,128)(2,1)S(1)} collective-permute-done((s16[32,1152]{1,0:T(8,128)(2,1)S(1)}, s16[32,1152]{1,0:T(8,128)(2,1)S(1)}, u32[]{:S(2)}, u32[]{:S(2)}) %collective-permute-start.2) | collective-permute-done | bytes 73760 | tf_op jit(solution)/shard_map/ppermute | solution.py:568
  77.9 0.0 collective-permute-done.1.refs_4_.refs_5_
  77.9 0.9 collective-permute-done.refs_3_.refs_4_
  78.7 0.0 copy-done.14
  78.7 0.0 copy-done.16
  78.7 1.7 %shard_map.211 = (f32[96,1024]{1,0:T(8,128)S(1)}, f32[24,512]{1,0:T(8,128)S(1)}) custom-call(f32[3,7]{1,0:T(4,128)S(1)} %copy-done.16, f32[96,1024]{1,0:T(8,128)S(1)} %get-tuple-element.32.refs_1_, bf16[96,408]{1,0:T(8,128)(2,1)S(1)} %copy-done.14, s16[128,1152]{1,0:T(8,128)(2,1)S(1)} %collective-permute-done.refs_3_.refs_4_, ...), custom_call_target="tpu_custom_call" | custom-call | tf_op jit(solution)/shard_map/pallas_call | solution.py:542
  80.4 4.6 %collective-permute-start.4 = (f32[24,512]{1,0:T(8,128)S(1)}, f32[24,512]{1,0:T(8,128)S(1)}, u32[]{:S(2)}, u32[]{:S(2)}) collective-permute-start(f32[24,512]{1,0:T(8,128)S(1)} %get-tuple-element.34.refs_11_.refs_1_), channel_id=1, source_target_pairs={{8,0},{16,8},{24,16},{32,24},{40,32},{48,40},{56,48},{64,56},{72,6... | collective-permute-start | bytes 147464 | tf_op jit(solution)/shard_map/ppermute | solution.py:560
  85.0 0.0 collective-permute-start.3
  85.0 0.0 copy-done
  85.0 0.0 copy-done.9
  85.0 0.0 copy-done.10
  85.1 0.0 copy-done.12
  85.1 0.0 copy-start.2
  85.1 0.0 copy-start.13
  85.1 0.0 copy-start.15
  85.1 0.0 copy-start.17
  85.1 4.2 %shard_map.212 = (f32[288,1024]{1,0:T(8,128)S(1)}, f32[384,1024]{1,0:T(8,128)S(1)}, f32[96,1024]{1,0:T(8,128)S(1)}, f32[96,1024]{1,0:T(8,128)S(1)}, f32[96,1024]{1,0:T(8,128)S(1)}) custom-call(f32[3,7]{1,0:T(4,128)S(1)} %copy-done.16, f32[384,1024]{1,0:T(8,128)S(1)} %get-tuple-element.27.refs_1_, f32[384,1024]{1,0:T(8,128)S(1)} %get-tuple-element.28.refs_2_, ...), custom_call_target="tpu_custom_call" | custom-call | flops 1000000000 | tf_op jit(solution)/shard_map/pallas_call | solution.py:542
  89.3 0.0 copy-start.3
  89.3 0.0 copy-start.5
  89.3 0.0 copy-start.8
  89.3 0.0 collective-permute-done.4.refs_2_
  89.3 3.1 %collective-permute-done.3.refs_0_ = f32[24,512]{1,0:T(8,128)S(1)} collective-permute-done((f32[24,512]{1,0:T(8,128)S(1)}, f32[24,512]{1,0:T(8,128)S(1)}, u32[]{:S(2)}, u32[]{:S(2)}) %collective-permute-start.3) | collective-permute-done | bytes 49184 | tf_op jit(solution)/shard_map/ppermute | solution.py:560
  92.5 0.0 collective-permute-start.5
  92.5 2.9 %collective-permute-start.6 = (f32[48,512]{1,0:T(8,128)S(1)}, f32[48,512]{1,0:T(8,128)S(1)}, u32[]{:S(2)}, u32[]{:S(2)}) collective-permute-start(f32[48,512]{1,0:T(8,128)S(1)} %get-tuple-element.39), channel_id=1, source_target_pairs={{1,0},{2,1},{3,2},{4,3},{5,4},{6,5},{7,6},{0,7},{9,8},{10,9},{11,1... | collective-permute-start | bytes 294920 | tf_op jit(solution)/shard_map/ppermute | solution.py:562
  95.5 2.3 %collective-permute-done.5.refs_1_ = f32[48,512]{1,0:T(8,128)S(1)} collective-permute-done((f32[48,512]{1,0:T(8,128)S(1)}, f32[48,512]{1,0:T(8,128)S(1)}, u32[]{:S(2)}, u32[]{:S(2)}) %collective-permute-start.5) | collective-permute-done | bytes 98336 | tf_op jit(solution)/shard_map/ppermute | solution.py:562
  97.8 0.0 collective-permute-done.6.refs_3_
  97.8 0.0 copy-done.2
  97.8 0.0 copy-done.13
  97.8 0.0 copy-done.15
  97.8 0.0 copy-done.17
  97.8 2.1 %shard_map.214 = (f32[96,1024]{1,0:T(8,128)S(1)}, s16[128,1152]{1,0:T(8,128)(2,1)S(1)}, s16[80,1152]{1,0:T(8,128)(2,1)S(1)}, s16[32,1152]{1,0:T(8,128)(2,1)S(1)}) custom-call(f32[3,7]{1,0:T(4,128)S(1)} %copy-done.16, f32[48,512]{1,0:T(8,128)S(1)} %collective-permute-done.5.refs_1_, f32[72,512]{1,0:T(8,128)S(1)} %get-tuple-element.38.refs_2_, ...), custom_call_target="tpu_custom_call" | custom-call | tf_op jit(solution)/shard_map/pallas_call | solution.py:542
  99.9 0.1 collective-permute-start.7
  100.0 0.0 collective-permute-start.8
  100.0 0.3 collective-permute-start.9
  100.3 0.0 copy-done.3
  100.4 0.0 copy-start.6
  100.4 4.9 %shard_map.215.refs_0_ = f32[384,2048]{1,0:T(8,128)S(1)} custom-call(f32[288,1024]{1,0:T(8,128)S(1)} %get-tuple-element.35.refs_3_.refs_0_, f32[384,1024]{1,0:T(8,128)S(1)} %get-tuple-element.36.refs_1_, f32[96,1024]{1,0:T(8,128)S(1)} %get-tuple-element.43.refs_2_, bf16[384,864]{1,0:T(8,128)(2,1)S(1)} %copy-done.5, bf16[384,1152]{1,0:T(8,128)(2,1)S(1)} %copy-done.3, ...), custom_call_target="tpu_custom_call" | custom-call | flops 1000000000 | tf_op jit(solution)/shard_map/pallas_call | solution.py:542
  105.3 8.1 %collective-permute-done.9.refs_3_ = s16[32,1152]{1,0:T(8,128)(2,1)S(1)} collective-permute-done((s16[32,1152]{1,0:T(8,128)(2,1)S(1)}, s16[32,1152]{1,0:T(8,128)(2,1)S(1)}, u32[]{:S(2)}, u32[]{:S(2)}) %collective-permute-start.9) | collective-permute-done | bytes 73760 | tf_op jit(solution)/shard_map/ppermute | solution.py:568
  113.4 0.0 collective-permute-done.8.refs_2_
  113.4 0.0 collective-permute-done.7.refs_1_
  113.4 3.7 %shard_map.216 = f32[384,2048]{1,0:T(8,128)} custom-call(f32[384,2048]{1,0:T(8,128)S(1)} %shard_map.215.refs_0_, s16[128,1152]{1,0:T(8,128)(2,1)S(1)} %collective-permute-done.7.refs_1_, s16[80,1152]{1,0:T(8,128)(2,1)S(1)} %collective-permute-done.8.refs_2_, s16[32,1152]{1,0:T(8,128)(2,1)S(1)} %collective-permute-done.9.refs_3_, ...), custom_call_target="tpu_custom_call" | custom-call | tf_op jit(solution)/shard_map/pallas_call | solution.py:542
  (7 shorter events, 0.1 us)
Async XLA Ops:
  6.5 11.7 %copy-start.18 = (s32[16,24]{1,0:T(8,128)S(1)}, s32[16,24]{1,0:T(8,128)}, u32[]{:S(2)}) copy-start(s32[16,24]{1,0:T(8,128)} %param.25) | copy-start | bytes 4612
  6.5 55.8 %copy-start.1 = (bf16[1152,256]{1,0:T(8,128)(2,1)S(1)}, bf16[1152,256]{1,0:T(8,128)(2,1)}, u32[]{:S(2)}) copy-start(bf16[1152,256]{1,0:T(8,128)(2,1)} %constant.17.clone.refs_2_.refs_1_.refs_6_) | copy-start | bytes 1769476
  6.5 55.8 %copy-start.7 = (bf16[136,1152]{1,0:T(8,128)(2,1)S(1)}, bf16[136,1152]{1,0:T(8,128)(2,1)}, u32[]{:S(2)}) copy-start(bf16[136,1152]{1,0:T(8,128)(2,1)} %constant.36.clone.refs_3_) | copy-start | bytes 940036
  6.5 55.8 %all-to-all-start = ((bf16[128,8,1664]{2,1,0:T(8,128)(2,1)}), bf16[128,8,1664]{2,1,0:T(8,128)(2,1)}, u32[]{:S(2)}, u32[]{:S(2)}) async-start(bf16[128,8,1664]{2,1,0:T(8,128)(2,1)} %bitcast.5), calls=%async_computation | async-start | bytes 6815744 | tf_op jit(solution)/shard_map/all_to_all | solution.py:601
  18.2 52.5 %copy-start.4 = (bf16[384,1152]{1,0:T(8,128)(2,1)S(1)}, bf16[384,1152]{1,0:T(8,128)(2,1)}, u32[]{:S(2)}) copy-start(bf16[384,1152]{1,0:T(8,128)(2,1)} %constant.37.clone.refs_2_) | copy-start | bytes 2654212
  18.2 52.5 %copy-start.11 = (bf16[96,1152]{1,0:T(8,128)(2,1)S(1)}, bf16[96,1152]{1,0:T(8,128)(2,1)}, u32[]{:S(2)}) copy-start(bf16[96,1152]{1,0:T(8,128)(2,1)} %constant.38.clone.refs_3_) | copy-start | bytes 663556
  68.8 10.0 %copy-start.14 = (bf16[96,408]{1,0:T(8,128)(2,1)S(1)}, bf16[96,408]{1,0:T(8,128)(2,1)}, u32[]{:S(2)}) copy-start(bf16[96,408]{1,0:T(8,128)(2,1)} %constant.39.clone.refs_2_) | copy-start | bytes 235012
  68.8 10.0 %copy-start.16 = (f32[3,7]{1,0:T(4,128)S(1)}, f32[3,7]{1,0:T(4,128)}, u32[]{:S(2)}) copy-start(f32[3,7]{1,0:T(4,128)} %refs_0_.5) | copy-start | bytes 256
  68.8 9.9 %collective-permute-start = (s16[128,1152]{1,0:T(8,128)(2,1)S(1)}, s16[128,1152]{1,0:T(8,128)(2,1)S(1)}, u32[]{:S(2)}, u32[]{:S(2)}) collective-permute-start(s16[128,1152]{1,0:T(8,128)(2,1)S(1)} %get-tuple-element.29), channel_id=1, source_target_pairs={{8,0},{16,8},{24,16},{32,24},{40,32},{48,40},{56,48},{64,56},{72,6... | collective-permute-start | bytes 884744 | tf_op jit(solution)/shard_map/ppermute | solution.py:560
  70.1 7.8 %collective-permute-start.1 = (s16[80,1152]{1,0:T(8,128)(2,1)S(1)}, s16[80,1152]{1,0:T(8,128)(2,1)S(1)}, u32[]{:S(2)}, u32[]{:S(2)}) collective-permute-start(s16[80,1152]{1,0:T(8,128)(2,1)S(1)} %get-tuple-element.30), channel_id=1, source_target_pairs={{1,0},{2,1},{3,2},{4,3},{5,4},{6,5},{7,6},{0,7},{9,8},{10,9},{11,1... | collective-permute-start | bytes 552968 | tf_op jit(solution)/shard_map/ppermute | solution.py:562
  70.1 7.8 %collective-permute-start.2 = (s16[32,1152]{1,0:T(8,128)(2,1)S(1)}, s16[32,1152]{1,0:T(8,128)(2,1)S(1)}, u32[]{:S(2)}, u32[]{:S(2)}) collective-permute-start(s16[32,1152]{1,0:T(8,128)(2,1)S(1)} %get-tuple-element.31), channel_id=1, source_target_pairs={{9,0},{10,1},{11,2},{12,3},{13,4},{14,5},{15,6},{8,7},{17,8},{18,9... | collective-permute-start | bytes 221192 | tf_op jit(solution)/shard_map/ppermute | solution.py:568
  70.6 14.4 %copy-start = (bf16[1536,256]{1,0:T(8,128)(2,1)S(1)}, bf16[1536,256]{1,0:T(8,128)(2,1)}, u32[]{:S(2)}) copy-start(bf16[1536,256]{1,0:T(8,128)(2,1)} %constant.43.clone.refs_10_.refs_6_.refs_4_) | copy-start | bytes 2359300
  70.6 14.4 %copy-start.9 = (bf16[384,288]{1,0:T(8,128)(2,1)S(1)}, bf16[384,288]{1,0:T(8,128)(2,1)}, u32[]{:S(2)}) copy-start(bf16[384,288]{1,0:T(8,128)(2,1)} %constant.40.clone.refs_3_) | copy-start | bytes 663556
  70.7 14.4 %copy-start.10 = (bf16[96,1152]{1,0:T(8,128)(2,1)S(1)}, bf16[96,1152]{1,0:T(8,128)(2,1)}, u32[]{:S(2)}) copy-start(bf16[96,1152]{1,0:T(8,128)(2,1)} %constant.42.clone.refs_8_) | copy-start | bytes 663556
  70.7 14.4 %copy-start.12 = (bf16[96,864]{1,0:T(8,128)(2,1)S(1)}, bf16[96,864]{1,0:T(8,128)(2,1)}, u32[]{:S(2)}) copy-start(bf16[96,864]{1,0:T(8,128)(2,1)} %constant.41.clone.refs_7_) | copy-start | bytes 497668
  80.4 8.9 %collective-permute-start.4 = (f32[24,512]{1,0:T(8,128)S(1)}, f32[24,512]{1,0:T(8,128)S(1)}, u32[]{:S(2)}, u32[]{:S(2)}) collective-permute-start(f32[24,512]{1,0:T(8,128)S(1)} %get-tuple-element.34.refs_11_.refs_1_), channel_id=1, source_target_pairs={{8,0},{16,8},{24,16},{32,24},{40,32},{48,40},{56,48},{64,56},{72,6... | collective-permute-start | bytes 147464 | tf_op jit(solution)/shard_map/ppermute | solution.py:560
  85.0 7.4 %collective-permute-start.3 = (f32[24,512]{1,0:T(8,128)S(1)}, f32[24,512]{1,0:T(8,128)S(1)}, u32[]{:S(2)}, u32[]{:S(2)}) collective-permute-start(f32[24,512]{1,0:T(8,128)S(1)} %get-tuple-element.34.refs_11_.refs_1_), channel_id=1, source_target_pairs={{120,0},{0,8},{8,16},{16,24},{24,32},{32,40},{40,48},{48,56},{56,6... | collective-permute-start | bytes 147464 | tf_op jit(solution)/shard_map/ppermute | solution.py:560
  85.1 12.7 %copy-start.2 = (bf16[768,256]{1,0:T(8,128)(2,1)S(1)}, bf16[768,256]{1,0:T(8,128)(2,1)}, u32[]{:S(2)}) copy-start(bf16[768,256]{1,0:T(8,128)(2,1)} %constant.46.clone.refs_7_.refs_5_) | copy-start | bytes 1179652
  85.1 12.7 %copy-start.13 = (bf16[136,288]{1,0:T(8,128)(2,1)S(1)}, bf16[136,288]{1,0:T(8,128)(2,1)}, u32[]{:S(2)}) copy-start(bf16[136,288]{1,0:T(8,128)(2,1)} %constant.47.clone.refs_11_) | copy-start | bytes 235012
  85.1 12.7 %copy-start.15 = (bf16[80,504]{1,0:T(8,128)(2,1)S(1)}, bf16[80,504]{1,0:T(8,128)(2,1)}, u32[]{:S(2)}) copy-start(bf16[80,504]{1,0:T(8,128)(2,1)} %constant.44.clone.refs_4_) | copy-start | bytes 241924
  85.1 12.7 %copy-start.17 = (bf16[24,240]{1,0:T(8,128)(2,1)S(1)}, bf16[24,240]{1,0:T(8,128)(2,1)}, u32[]{:S(2)}) copy-start(bf16[24,240]{1,0:T(8,128)(2,1)} %constant.45.clone.refs_5_) | copy-start | bytes 34564
  89.3 11.1 %copy-start.3 = (bf16[384,1152]{1,0:T(8,128)(2,1)S(1)}, bf16[384,1152]{1,0:T(8,128)(2,1)}, u32[]{:S(2)}) copy-start(bf16[384,1152]{1,0:T(8,128)(2,1)} %constant.49.clone.refs_4_) | copy-start | bytes 2654212
  89.3 11.1 %copy-start.5 = (bf16[384,864]{1,0:T(8,128)(2,1)S(1)}, bf16[384,864]{1,0:T(8,128)(2,1)}, u32[]{:S(2)}) copy-start(bf16[384,864]{1,0:T(8,128)(2,1)} %constant.48.clone.refs_3_) | copy-start | bytes 1990660
  89.3 11.0 %copy-start.8 = (bf16[384,288]{1,0:T(8,128)(2,1)S(1)}, bf16[384,288]{1,0:T(8,128)(2,1)}, u32[]{:S(2)}) copy-start(bf16[384,288]{1,0:T(8,128)(2,1)} %constant.50.clone.refs_5_) | copy-start | bytes 663556
  92.5 5.3 %collective-permute-start.5 = (f32[48,512]{1,0:T(8,128)S(1)}, f32[48,512]{1,0:T(8,128)S(1)}, u32[]{:S(2)}, u32[]{:S(2)}) collective-permute-start(f32[48,512]{1,0:T(8,128)S(1)} %get-tuple-element.37), channel_id=1, source_target_pairs={{7,0},{0,1},{1,2},{2,3},{3,4},{4,5},{5,6},{6,7},{15,8},{8,9},{9,10... | collective-permute-start | bytes 294920 | tf_op jit(solution)/shard_map/ppermute | solution.py:562
  92.5 5.2 %collective-permute-start.6 = (f32[48,512]{1,0:T(8,128)S(1)}, f32[48,512]{1,0:T(8,128)S(1)}, u32[]{:S(2)}, u32[]{:S(2)}) collective-permute-start(f32[48,512]{1,0:T(8,128)S(1)} %get-tuple-element.39), channel_id=1, source_target_pairs={{1,0},{2,1},{3,2},{4,3},{5,4},{6,5},{7,6},{0,7},{9,8},{10,9},{11,1... | collective-permute-start | bytes 294920 | tf_op jit(solution)/shard_map/ppermute | solution.py:562
  99.9 13.5 %collective-permute-start.7 = (s16[128,1152]{1,0:T(8,128)(2,1)S(1)}, s16[128,1152]{1,0:T(8,128)(2,1)S(1)}, u32[]{:S(2)}, u32[]{:S(2)}) collective-permute-start(s16[128,1152]{1,0:T(8,128)(2,1)S(1)} %get-tuple-element.44), channel_id=1, source_target_pairs={{120,0},{0,8},{8,16},{16,24},{24,32},{32,40},{40,48},{48,56},{56,6... | collective-permute-start | bytes 884744 | tf_op jit(solution)/shard_map/ppermute | solution.py:560
  100.0 13.4 %collective-permute-start.8 = (s16[80,1152]{1,0:T(8,128)(2,1)S(1)}, s16[80,1152]{1,0:T(8,128)(2,1)S(1)}, u32[]{:S(2)}, u32[]{:S(2)}) collective-permute-start(s16[80,1152]{1,0:T(8,128)(2,1)S(1)} %get-tuple-element.45), channel_id=1, source_target_pairs={{7,0},{0,1},{1,2},{2,3},{3,4},{4,5},{5,6},{6,7},{15,8},{8,9},{9,10... | collective-permute-start | bytes 552968 | tf_op jit(solution)/shard_map/ppermute | solution.py:562
  100.0 13.4 %collective-permute-start.9 = (s16[32,1152]{1,0:T(8,128)(2,1)S(1)}, s16[32,1152]{1,0:T(8,128)(2,1)S(1)}, u32[]{:S(2)}, u32[]{:S(2)}) collective-permute-start(s16[32,1152]{1,0:T(8,128)(2,1)S(1)} %get-tuple-element.46), channel_id=1, source_target_pairs={{127,0},{120,1},{121,2},{122,3},{123,4},{124,5},{125,6},{126,7},{7... | collective-permute-start | bytes 221192 | tf_op jit(solution)/shard_map/ppermute | solution.py:568
  100.4 13.1 %copy-start.6 = (bf16[384,408]{1,0:T(8,128)(2,1)S(1)}, bf16[384,408]{1,0:T(8,128)(2,1)}, u32[]{:S(2)}) copy-start(bf16[384,408]{1,0:T(8,128)(2,1)} %constant.51.clone.refs_6_) | copy-start | bytes 940036

commit v5 on v4

--- a/solution.py
+++ b/solution.py
@@ -386,31 +386,36 @@
         high_ref[:, where] = left_dot(own_ref[...], jnp.concatenate([highs[b], highs[b + 1]], 1))
 
 
-def middle_kernel(sizes, thr_ref, own_ref, edge_ref, s0, s1, s2, time_ref, shrunk_ref, timed_ref):
-    quarter = shrunk_ref.shape[0] // 4
-    half = shrunk_ref.shape[1] // 2
-    matrix = edge_ref[...]
-    blocks = []
+def middle_kernel(sizes, own_ref, edge_ref, s0, s1, s2, time_ref, timed_ref):
+    rows, length = timed_ref.shape
+    matrix = edge_ref[:rows]
     refs = (s0, s1, s2)
     scales = scales_of(refs)
+    blocks = []
     for where in steps(own_ref):
         low, _ = take_joint(sizes, refs, scales, where)
-        blocks.append(own_ref[:, where] + left_dot(matrix, low))
-    lows, highs = time_analysis(blocks, time_ref[...])
-    for b in range(len(blocks)):
-        for base, piece, high in ((0, lows[b], 0), (half, highs[b], 1)):
-            where = slice(base + b * LANES, base + (b + 1) * LANES)
-            for q in range(4):
-                at = slice(q * quarter, (q + 1) * quarter)
-                if q or high:
-                    shrunk_ref[at, where] = shrink(piece[at], thr_ref[1, 2 * q + high - 1])
-                else:
-                    shrunk_ref[at, where] = jnp.zeros_like(piece[at])
-    coarse = [jnp.concatenate([lows[b][:quarter], lows[b + 1][:quarter]], 1) for b in range(0, len(lows), 2)]
+        blocks.append(own_ref[:rows, where] + left_dot(matrix, low))
+    lows, _ = time_analysis(blocks, time_ref[...])
+    coarse = [jnp.concatenate([lows[b], lows[b + 1]], 1) for b in range(0, len(lows), 2)]
     lows, highs = time_analysis(coarse, time_ref[...])
     for b in range(len(coarse)):
-        for base, piece in ((0, lows[b]), (half // 2, highs[b])):
+        for base, piece in ((0, lows[b]), (length // 2, highs[b])):
             timed_ref[:, base + b * LANES : base + (b + 1) * LANES] = piece
+
+
+def middle_details(thr_ref, blocks, time_matrix, time_t):
+    lows, highs = time_analysis(blocks, time_matrix)
+    quarter = blocks[0].shape[0] // 4
+    pairs = []
+    for b in range(len(blocks)):
+        sides = []
+        for piece, high in ((lows[b], 0), (highs[b], 1)):
+            bands = [piece[q * quarter : (q + 1) * quarter] for q in range(4)]
+            for q in range(4):
+                bands[q] = shrink(bands[q], thr_ref[1, 2 * q + high - 1]) if q or high else jnp.zeros_like(bands[q])
+            sides.append(jnp.concatenate(bands, 0))
+        pairs.append(jnp.concatenate(sides, 1))
+    return time_synthesis(pairs, time_t)
 
 
 def sides_kernel(cols, before, own, after, stack_out, first_out, last_out):
@@ -432,25 +437,37 @@
     back_low,
     back_ref,
     next_in,
+    next_edge,
+    time_ref,
     time_t,
+    next_back,
     low_out,
     high_out,
     low_states,
     high_states,
     next_out,
 ):
-    for b, block in enumerate(time_pairs(next_in[...], time_t[...])):
-        next_out[:, b * BLOCK : (b + 1) * BLOCK] = block
     quarter = low_in.shape[0] // 4
     refs = (s0, s1, s2)
     scales = scales_of(refs)
+    blocks = []
+    for where in steps(next_in):
+        low, _ = take_joint(sizes, refs, scales, where)
+        blocks.append(next_in[:, where] + left_dot(next_edge[...], low))
+    next_states = []
+    for b, block in enumerate(middle_details(thr_ref, blocks, time_ref[...], time_t[...])):
+        next_out[:, b * BLOCK : (b + 1) * BLOCK] = block
+        next_states.append(left_dot(next_back[...], block))
     for where in steps(low_in):
         low, high = take_joint(sizes, refs, scales, where)
         bands = low_in[quarter:, where] + left_dot(edge_ref[quarter:], low[: high.shape[0]])
         bands = [shrink(bands[(q - 1) * quarter : q * quarter], thr_ref[0, 2 * q - 1]) for q in range(1, 4)]
         bands = jnp.concatenate(bands, 0)
         low_out[:, where] = bands
-        low_states[:, where] = left_dot(back_low[...], bands)
+        states = left_dot(back_low[...], bands)
+        count = states.shape[0]
+        more = next_states[where.start // BLOCK]
+        low_states[:, where] = jnp.concatenate([states + more[:count], more[count:]], 0)
         bands = high_in[:, where] + left_dot(edge_ref[...], high)
         bands = [shrink(bands[q * quarter : (q + 1) * quarter], thr_ref[0, 2 * q]) for q in range(4)]
         bands = jnp.concatenate(bands, 0)
@@ -467,7 +484,7 @@
 
 
 def deepest_kernel(
-    sizes, thr_ref, before, own, after, bands_m, back_m, time_t, time_low, next_in, low_states, high_states, back_ref, next_out, *outs
+    sizes, thr_ref, before, own, after, bands_m, both_m, time_two, low_states, high_states, coarse_out, *outs
 ):
     stack = jnp.concatenate([before[...], own[...], after[...]], 0)
     bands = left_dot(bands_m[...], stack)
@@ -477,29 +494,25 @@
     quarter = bands.shape[0] // 4
     for q in range(1, 4):
         limit = jnp.where(row >= q * quarter, jnp.where(high, thr_ref[2, 2 * q], thr_ref[2, 2 * q - 1]), limit)
-    rebuilt = left_dot(back_m[...], shrink(bands, limit))
-    lows = []
-    for block in time_pairs(rebuilt, time_t[...]):
-        lows += [block[:, b : b + LANES] for b in range(0, BLOCK, LANES)]
-    rows = rebuilt.shape[0]
-    count = low_states.shape[0]
     state_lows, state_highs = [], []
-    for b, block in enumerate(synthesis_from_low(lows, time_low[...])):
-        where = slice(b * BLOCK, (b + 1) * BLOCK)
-        bands = jnp.concatenate([next_in[:rows, where] + block, next_in[rows:, where]], 0)
-        next_out[:, where] = bands
-        states = left_dot(back_ref[...], bands)
-        low = jnp.concatenate([states[:count] + low_states[:, where], states[count:]], 0)
-        for at in range(0, BLOCK, LANES):
+    rows = coarse_out.shape[0]
+    for b, block in enumerate(time_pairs(shrink(bands, limit), time_two[...])):
+        where = slice(b * block.shape[1], (b + 1) * block.shape[1])
+        both = left_dot(both_m[...], block)
+        coarse_out[:, where] = both[:rows]
+        low = both[rows:] + low_states[:, where]
+        for at in range(0, block.shape[1], LANES):
             state_lows.append(low[:, at : at + LANES])
             state_highs.append(high_states[:, where.start + at : where.start + at + LANES])
     put_joint(sizes, outs, state_lows, state_highs)
 
 
-def own_back_kernel(low_in, high_in, next_in, low_t, high_t, next_t, time_t, scale_ref, out_ref):
+def own_back_kernel(low_in, high_in, next_in, coarse_in, low_t, high_t, next_t, time_t, scale_ref, out_ref):
     blocks = []
     for where in steps(low_in):
-        low = left_dot(low_t[...], low_in[:, where]) + left_dot(next_t[...], next_in[:, where])
+        rows = coarse_in.shape[0]
+        bands = jnp.concatenate([next_in[:rows, where] + coarse_in[:, where], next_in[rows:, where]], 0)
+        low = left_dot(low_t[...], low_in[:, where]) + left_dot(next_t[...], bands)
         high = left_dot(high_t[...], high_in[:, where])
         for b in range(0, BLOCK, LANES):
             blocks.append(jnp.concatenate([low[:, b : b + LANES], high[:, b : b + LANES]], 1))
@@ -607,6 +620,12 @@
     time_matrix = np.concatenate([triple(main, 0), triple(following, 0)], 0)
     back_main, back_last = main.T, np.pad(following.T, ((0, 0), (0, BLOCK - LANES)))
     time_back = np.concatenate([triple(back_main, 0), triple(back_last, 0)], 0)
+    twice, onward = np.zeros((2, BLOCK, 2 * BLOCK))
+    twice[:LANES, :BLOCK] = twice[LANES:, BLOCK:] = back_main[:LANES]
+    twice[:LANES, BLOCK:] = onward[LANES:, :BLOCK] = back_last[:LANES]
+    last_two = back_last @ twice + back_main @ onward
+    assert np.abs(back_last @ onward).max() == 0.0
+    time_back_two = np.concatenate([triple(back_main @ twice, 0), triple(last_two, 0)], 0)
     time_back_low = np.concatenate([triple(back_main[:LANES], 0), triple(back_last[:LANES], 0)], 0)
     half, rows2, cols2 = samples // 2, tile_rows // 4, tile_cols // 4
     quarter, last = bins // 4, bins // 16
@@ -639,21 +658,19 @@
         cost=1e9,
     )
     rows_all = rows2 + 2 * SIDE
-    shrunk1, timed = call(
+    (timed,) = call(
         functools.partial(middle_kernel, sizes),
-        [((quarter, half), f32), ((last, half // 2), f32)],
-        thresholds,
+        [((last, half // 2), f32)],
         own_next,
         triple(edge1, 1),
         *states,
         time_matrix,
-        smem=(0,),
     )
     before, behind = shift(timed, -1, 0), shift(timed, 1, 0)
     low_details, high_details, low_states, high_states, next_details = call(
         functools.partial(details_kernel, sizes),
         [((bins - quarter, half), f32), ((bins, half), f32)]
-        + [((count0, half), f32)] * 2
+        + [((sum(sizes), half), f32), ((count0, half), f32)]
         + [((quarter, half), f32)],
         thresholds,
         own_low,
@@ -662,8 +679,11 @@
         *states,
         triple(edge0[quarter:].T, 1),
         triple(edge0.T, 1),
-        shrunk1,
+        own_next,
+        triple(edge1, 1),
+        time_matrix,
         time_back,
+        triple(edge1.T, 1),
         smem=(0,),
         after=(timed,),
         cost=1e9,
@@ -677,21 +697,18 @@
         after=(low_details,),
     )
     left, right = shift(lasts, 0, -1), shift(firsts, 0, 1)
-    bands1, *states = call(
+    coarse1, *states = call(
         functools.partial(deepest_kernel, sizes),
-        [((quarter, half), f32)] + joint_shapes,
+        [((last, half), f32)] + joint_shapes,
         thresholds,
         left,
         stack,
         right,
         triple(bands2, 1),
-        triple(back2, 1),
-        time_back,
-        time_back_low,
-        next_details,
+        triple(np.concatenate([back2, edge1[:last].T @ back2], 0), 1),
+        time_back_two,
         low_states,
         high_states,
-        triple(edge1.T, 1),
         smem=(0,),
     )
     states = exchange(states, -1)
@@ -700,7 +717,8 @@
         [((bins, samples), f32)],
         low_details,
         high_details,
-        bands1,
+        next_details,
+        coarse1,
         triple(own0[quarter:].T, 1),
         triple(own0.T, 1),
         triple(own1.T, 1),

time: 118 us -> 117 us (level)
  no operation moved by 1% of the time
where the time goes in v5:
time: 117 us
  waiting for transfers between devices  61.1 us (52%)
  Pallas kernels  33.2 us (28%)
  starting transfers between devices  21.5 us (18%)
    all_to_all x1, waiting for transfers between devices, on_device(): lax.all_to_all(outgoing.reshape(devices, GROUP, width), ('inl', 'xl'), sp...  44 us
    pallas_call x9, Pallas kernels, call(): pl.pallas_call(body, out_shape=[jax.ShapeDtypeStruct(shape, dtype) for sh...  33.2 us
    all_to_all x1, starting transfers between devices, on_device(): lax.all_to_all(outgoing.reshape(devices, GROUP, width), ('inl', 'xl'), sp...  11.6 us
    ppermute x2, waiting for transfers between devices, shift(): return lax.ppermute(block, ('inl', 'xl'), route)  10.5 us
    ppermute x4, starting transfers between devices, shift(): lax.ppermute(block, 'inl', [((i + inline_by) % inline_devs, i) for i in r...  6.04 us
    ppermute x4, waiting for transfers between devices, shift(): lax.ppermute(block, 'inl', [((i + inline_by) % inline_devs, i) for i in r...  4.27 us
    ppermute x4, starting transfers between devices, shift(): lax.ppermute(block, 'xl', [((j + cross_by) % cross_devs, j) for j in rang...  2.98 us
  transfers between devices with their start and end apart: 11, of which 6 were waited for; matrix products, arithmetic and copies ran while one was open for 0% of the time, Pallas kernels for 12%

profile of v5, /device:TPU:0, one launch (start us, length us, event | category | flops | bytes accessed | tf_op | source)
XLA Modules:
  0.0 116.5 jit_solution(1928650747297573394)
XLA Ops:
  0.0 6.5 %shard_map.226 = bf16[1024,1664]{1,0:T(8,128)(2,1)} custom-call(s32[1,512]{1,0:T(1,128)} %bitcast.6, s32[1,512]{1,0:T(1,128)} %bitcast.7, bf16[512,2048]{1,0:T(8,128)(2,1)} %refs_2_.3), custom_call_target="tpu_custom_call" | custom-call | tf_op jit(solution)/shard_map/pallas_call | solution.py:555
  6.5 0.0 copy-start.19
  6.5 0.0 copy-start
  6.5 0.0 copy-start.9
  6.5 11.6 %all-to-all-start = ((bf16[128,8,1664]{2,1,0:T(8,128)(2,1)}), bf16[128,8,1664]{2,1,0:T(8,128)(2,1)}, u32[]{:S(2)}, u32[]{:S(2)}) async-start(bf16[128,8,1664]{2,1,0:T(8,128)(2,1)} %bitcast.5), calls=%async_computation | async-start | bytes 6815744 | tf_op jit(solution)/shard_map/all_to_all | solution.py:614
  18.2 0.0 copy-done.19
  18.2 0.1 reshape.24.refs_1_.refs_8_.refs_7_
  18.3 44.0 %all-to-all-done = bf16[128,8,1664]{2,1,0:T(8,128)(2,1)} async-done(((bf16[128,8,1664]{2,1,0:T(8,128)(2,1)}), bf16[128,8,1664]{2,1,0:T(8,128)(2,1)}, u32[]{:S(2)}, u32[]{:S(2)}) %all-to-all-start) | async-done | bytes 3407904 | tf_op jit(solution)/shard_map/all_to_all | solution.py:614
  62.4 0.0 copy-done
  62.4 0.0 copy-done.9
  62.4 6.5 %shard_map.227 = (f32[384,2048]{1,0:T(8,128)S(1)}, s16[128,1152]{1,0:T(8,128)(2,1)S(1)}, s16[80,1152]{1,0:T(8,128)(2,1)S(1)}, s16[32,1152]{1,0:T(8,128)(2,1)S(1)}) custom-call(bf16[1024,1664]{1,0:T(8,128)(2,1)} %bitcast.3.refs_0_, f32[384,1]{1,0:T(8,128)S(1)} %reshape.24.refs_1_.refs_8_.refs_7_, bf16[1152,256]{1,0:T(8,128)(2,1)S(1)} %copy-done, ...), custom_call_target="tpu_custom_call" | custom-call | tf_op jit(solution)/shard_map/pallas_call | solution.py:555
  68.8 1.3 %collective-permute-start = (s16[128,1152]{1,0:T(8,128)(2,1)S(1)}, s16[128,1152]{1,0:T(8,128)(2,1)S(1)}, u32[]{:S(2)}, u32[]{:S(2)}) collective-permute-start(s16[128,1152]{1,0:T(8,128)(2,1)S(1)} %get-tuple-element.27), channel_id=1, source_target_pairs={{8,0},{16,8},{24,16},{32,24},{40,32},{48,40},{56,48},{64,56},{72,6... | collective-permute-start | bytes 884744 | tf_op jit(solution)/shard_map/ppermute | solution.py:573
  70.1 0.0 collective-permute-start.1
  70.1 0.5 collective-permute-start.2
  70.7 0.0 copy-done.4
  70.7 0.0 copy-done.13
  70.7 0.0 copy-start.11
  70.7 0.0 copy-start.12
  70.7 0.0 copy-start.14
  70.7 0.0 copy-start.15
  70.7 0.0 copy-start.18
  70.8 4.6 %shard_map.228 = (f32[384,1024]{1,0:T(8,128)S(1)}, f32[384,1024]{1,0:T(8,128)S(1)}, f32[96,1024]{1,0:T(8,128)S(1)}) custom-call(f32[384,2048]{1,0:T(8,128)S(1)} %get-tuple-element.24.refs_0_, bf16[1152,256]{1,0:T(8,128)(2,1)S(1)} %copy-done, bf16[384,1152]{1,0:T(8,128)(2,1)S(1)} %copy-done.4, bf16[96,1152]{1,0:T(8,128)(2,1)S(1)} %copy-done.13), custom_call_target="tpu_custom_call" | custom-call | flops 1000000000 | tf_op jit(solution)/shard_map/pallas_call | solution.py:555
  75.4 2.5 %collective-permute-done.2.refs_4_.refs_6_ = s16[32,1152]{1,0:T(8,128)(2,1)S(1)} collective-permute-done((s16[32,1152]{1,0:T(8,128)(2,1)S(1)}, s16[32,1152]{1,0:T(8,128)(2,1)S(1)}, u32[]{:S(2)}, u32[]{:S(2)}) %collective-permute-start.2) | collective-permute-done | bytes 73760 | tf_op jit(solution)/shard_map/ppermute | solution.py:581
  77.9 0.0 collective-permute-done.1.refs_3_.refs_5_
  77.9 0.9 collective-permute-done.refs_2_.refs_4_
  78.8 0.0 copy-done.8
  78.8 1.1 shard_map.229.refs_14_.refs_1_
  79.9 4.7 %collective-permute-start.4 = (f32[24,512]{1,0:T(8,128)S(1)}, f32[24,512]{1,0:T(8,128)S(1)}, u32[]{:S(2)}, u32[]{:S(2)}) collective-permute-start(f32[24,512]{1,0:T(8,128)S(1)} %shard_map.229.refs_14_.refs_1_), channel_id=1, source_target_pairs={{8,0},{16,8},{24,16},{32,24},{40,32},{48,40},{56,48},{64,56},{72,6... | collective-permute-start | bytes 147464 | tf_op jit(solution)/shard_map/ppermute | solution.py:573
  84.5 0.0 collective-permute-start.3
  84.5 0.0 copy-done.1
  84.5 0.0 copy-done.11
  84.5 0.0 copy-done.12
  84.5 0.0 copy-done.14
  84.5 0.0 copy-done.15
  84.6 0.0 copy-done.18
  84.6 0.0 copy-start.2
  84.6 0.0 copy-start.16
  84.6 0.0 copy-start.17
  84.6 3.9 %shard_map.230 = (f32[288,1024]{1,0:T(8,128)S(1)}, f32[384,1024]{1,0:T(8,128)S(1)}, f32[136,1024]{1,0:T(8,128)S(1)}, f32[96,1024]{1,0:T(8,128)S(1)}, f32[96,1024]{1,0:T(8,128)S(1)}) custom-call(f32[3,7]{1,0:T(4,128)S(1)} %copy-done.18, f32[384,1024]{1,0:T(8,128)S(1)} %get-tuple-element.25.refs_1_, f32[384,1024]{1,0:T(8,128)S(1)} %get-tuple-element.26.refs_2_, ...), custom_call_target="tpu_custom_call" | custom-call | flops 1000000000 | tf_op jit(solution)/shard_map/pallas_call | solution.py:555
  88.5 0.0 collective-permute-done.4.refs_2_
  88.5 3.4 %collective-permute-done.3.refs_0_ = f32[24,512]{1,0:T(8,128)S(1)} collective-permute-done((f32[24,512]{1,0:T(8,128)S(1)}, f32[24,512]{1,0:T(8,128)S(1)}, u32[]{:S(2)}, u32[]{:S(2)}) %collective-permute-start.3) | collective-permute-done | bytes 49184 | tf_op jit(solution)/shard_map/ppermute | solution.py:573
  92.0 0.0 collective-permute-start.5
  92.0 2.9 %collective-permute-start.6 = (f32[48,512]{1,0:T(8,128)S(1)}, f32[48,512]{1,0:T(8,128)S(1)}, u32[]{:S(2)}, u32[]{:S(2)}) collective-permute-start(f32[48,512]{1,0:T(8,128)S(1)} %get-tuple-element.36), channel_id=1, source_target_pairs={{1,0},{2,1},{3,2},{4,3},{5,4},{6,5},{7,6},{0,7},{9,8},{10,9},{11,1... | collective-permute-start | bytes 294920 | tf_op jit(solution)/shard_map/ppermute | solution.py:575
  94.9 2.3 %collective-permute-done.5.refs_1_ = f32[48,512]{1,0:T(8,128)S(1)} collective-permute-done((f32[48,512]{1,0:T(8,128)S(1)}, f32[48,512]{1,0:T(8,128)S(1)}, u32[]{:S(2)}, u32[]{:S(2)}) %collective-permute-start.5) | collective-permute-done | bytes 98336 | tf_op jit(solution)/shard_map/ppermute | solution.py:575
  97.2 0.0 collective-permute-done.6.refs_3_
  97.2 0.0 copy-done.2
  97.3 0.0 copy-done.16
  97.3 0.0 copy-done.17
  97.3 1.9 %shard_map.232 = (f32[24,1024]{1,0:T(8,128)S(1)}, s16[128,1152]{1,0:T(8,128)(2,1)S(1)}, s16[80,1152]{1,0:T(8,128)(2,1)S(1)}, s16[32,1152]{1,0:T(8,128)(2,1)S(1)}) custom-call(f32[3,7]{1,0:T(4,128)S(1)} %copy-done.18, f32[48,512]{1,0:T(8,128)S(1)} %collective-permute-done.5.refs_1_, f32[72,512]{1,0:T(8,128)S(1)} %get-tuple-element.35.refs_2_, ...), custom_call_target="tpu_custom_call" | custom-call | tf_op jit(solution)/shard_map/pallas_call | solution.py:555
  99.1 0.1 collective-permute-start.7
  99.2 0.0 collective-permute-start.8
  99.2 0.3 collective-permute-start.9
  99.6 0.0 copy-done.3
  99.6 0.0 copy-done.5
  99.6 0.0 copy-done.10
  99.6 0.0 copy-start.6
  99.6 0.0 copy-start.7
  99.6 5.0 %shard_map.233.refs_0_ = f32[384,2048]{1,0:T(8,128)S(1)} custom-call(f32[288,1024]{1,0:T(8,128)S(1)} %get-tuple-element.31.refs_3_.refs_0_, f32[384,1024]{1,0:T(8,128)S(1)} %get-tuple-element.32.refs_1_, f32[96,1024]{1,0:T(8,128)S(1)} %get-tuple-element.33.refs_2_, f32[24,1024]{1,0:T(8,128)S(1)} %get-tuple-element.39.refs_3_, ...), custom_call_target="tpu_custom_call" | custom-call | flops 1000000000 | tf_op jit(solution)/shard_map/pallas_call | solution.py:555
  104.6 8.0 %collective-permute-done.9.refs_3_ = s16[32,1152]{1,0:T(8,128)(2,1)S(1)} collective-permute-done((s16[32,1152]{1,0:T(8,128)(2,1)S(1)}, s16[32,1152]{1,0:T(8,128)(2,1)S(1)}, u32[]{:S(2)}, u32[]{:S(2)}) %collective-permute-start.9) | collective-permute-done | bytes 73760 | tf_op jit(solution)/shard_map/ppermute | solution.py:581
  112.6 0.0 collective-permute-done.8.refs_2_
  112.6 0.0 collective-permute-done.7.refs_1_
  112.6 0.0 copy-done.6
  112.7 0.0 copy-done.7
  112.7 3.7 %shard_map.234 = f32[384,2048]{1,0:T(8,128)} custom-call(f32[384,2048]{1,0:T(8,128)S(1)} %shard_map.233.refs_0_, s16[128,1152]{1,0:T(8,128)(2,1)S(1)} %collective-permute-done.7.refs_1_, s16[80,1152]{1,0:T(8,128)(2,1)S(1)} %collective-permute-done.8.refs_2_, s16[32,1152]{1,0:T(8,128)(2,1)S(1)} %collective-permute-done.9.refs_3_, ...), custom_call_target="tpu_custom_call" | custom-call | tf_op jit(solution)/shard_map/pallas_call | solution.py:555
  (9 shorter events, 0.1 us)
Async XLA Ops:
  6.5 11.7 %copy-start.19 = (s32[16,24]{1,0:T(8,128)S(1)}, s32[16,24]{1,0:T(8,128)}, u32[]{:S(2)}) copy-start(s32[16,24]{1,0:T(8,128)} %param.27) | copy-start | bytes 4612
  6.5 55.8 %copy-start = (bf16[1152,256]{1,0:T(8,128)(2,1)S(1)}, bf16[1152,256]{1,0:T(8,128)(2,1)}, u32[]{:S(2)}) copy-start(bf16[1152,256]{1,0:T(8,128)(2,1)} %constant.18.clone.refs_2_.refs_1_.refs_5_.refs_11_) | copy-start | bytes 1769476
  6.5 55.8 %copy-start.9 = (bf16[136,1152]{1,0:T(8,128)(2,1)S(1)}, bf16[136,1152]{1,0:T(8,128)(2,1)}, u32[]{:S(2)}) copy-start(bf16[136,1152]{1,0:T(8,128)(2,1)} %constant.38.clone.refs_3_) | copy-start | bytes 940036
  6.5 55.8 %all-to-all-start = ((bf16[128,8,1664]{2,1,0:T(8,128)(2,1)}), bf16[128,8,1664]{2,1,0:T(8,128)(2,1)}, u32[]{:S(2)}, u32[]{:S(2)}) async-start(bf16[128,8,1664]{2,1,0:T(8,128)(2,1)} %bitcast.5), calls=%async_computation | async-start | bytes 6815744 | tf_op jit(solution)/shard_map/all_to_all | solution.py:614
  62.4 8.3 %copy-start.4 = (bf16[384,1152]{1,0:T(8,128)(2,1)S(1)}, bf16[384,1152]{1,0:T(8,128)(2,1)}, u32[]{:S(2)}) copy-start(bf16[384,1152]{1,0:T(8,128)(2,1)} %constant.39.clone.refs_2_) | copy-start | bytes 2654212
  62.4 8.3 %copy-start.13 = (bf16[96,1152]{1,0:T(8,128)(2,1)S(1)}, bf16[96,1152]{1,0:T(8,128)(2,1)}, u32[]{:S(2)}) copy-start(bf16[96,1152]{1,0:T(8,128)(2,1)} %constant.40.clone.refs_3_) | copy-start | bytes 663556
  68.8 9.9 %collective-permute-start = (s16[128,1152]{1,0:T(8,128)(2,1)S(1)}, s16[128,1152]{1,0:T(8,128)(2,1)S(1)}, u32[]{:S(2)}, u32[]{:S(2)}) collective-permute-start(s16[128,1152]{1,0:T(8,128)(2,1)S(1)} %get-tuple-element.27), channel_id=1, source_target_pairs={{8,0},{16,8},{24,16},{32,24},{40,32},{48,40},{56,48},{64,56},{72,6... | collective-permute-start | bytes 884744 | tf_op jit(solution)/shard_map/ppermute | solution.py:573
  70.1 7.8 %collective-permute-start.1 = (s16[80,1152]{1,0:T(8,128)(2,1)S(1)}, s16[80,1152]{1,0:T(8,128)(2,1)S(1)}, u32[]{:S(2)}, u32[]{:S(2)}) collective-permute-start(s16[80,1152]{1,0:T(8,128)(2,1)S(1)} %get-tuple-element.28), channel_id=1, source_target_pairs={{1,0},{2,1},{3,2},{4,3},{5,4},{6,5},{7,6},{0,7},{9,8},{10,9},{11,1... | collective-permute-start | bytes 552968 | tf_op jit(solution)/shard_map/ppermute | solution.py:575
  70.1 7.8 %collective-permute-start.2 = (s16[32,1152]{1,0:T(8,128)(2,1)S(1)}, s16[32,1152]{1,0:T(8,128)(2,1)S(1)}, u32[]{:S(2)}, u32[]{:S(2)}) collective-permute-start(s16[32,1152]{1,0:T(8,128)(2,1)S(1)} %get-tuple-element.29), channel_id=1, source_target_pairs={{9,0},{10,1},{11,2},{12,3},{13,4},{14,5},{15,6},{8,7},{17,8},{18,9... | collective-permute-start | bytes 221192 | tf_op jit(solution)/shard_map/ppermute | solution.py:581
  70.7 8.1 %copy-start.8 = (bf16[96,408]{1,0:T(8,128)(2,1)S(1)}, bf16[96,408]{1,0:T(8,128)(2,1)}, u32[]{:S(2)}) copy-start(bf16[96,408]{1,0:T(8,128)(2,1)} %constant.41.clone.refs_1_.refs_10_) | copy-start | bytes 235012
  70.7 13.8 %copy-start.1 = (bf16[1536,256]{1,0:T(8,128)(2,1)S(1)}, bf16[1536,256]{1,0:T(8,128)(2,1)}, u32[]{:S(2)}) copy-start(bf16[1536,256]{1,0:T(8,128)(2,1)} %constant.45.clone.refs_12_.refs_7_.refs_4_) | copy-start | bytes 2359300
  70.7 13.8 %copy-start.11 = (bf16[384,288]{1,0:T(8,128)(2,1)S(1)}, bf16[384,288]{1,0:T(8,128)(2,1)}, u32[]{:S(2)}) copy-start(bf16[384,288]{1,0:T(8,128)(2,1)} %constant.42.clone.refs_3_) | copy-start | bytes 663556
  70.7 13.8 %copy-start.12 = (bf16[96,1152]{1,0:T(8,128)(2,1)S(1)}, bf16[96,1152]{1,0:T(8,128)(2,1)}, u32[]{:S(2)}) copy-start(bf16[96,1152]{1,0:T(8,128)(2,1)} %constant.44.clone.refs_8_) | copy-start | bytes 663556
  70.7 13.8 %copy-start.14 = (bf16[96,864]{1,0:T(8,128)(2,1)S(1)}, bf16[96,864]{1,0:T(8,128)(2,1)}, u32[]{:S(2)}) copy-start(bf16[96,864]{1,0:T(8,128)(2,1)} %constant.43.clone.refs_7_) | copy-start | bytes 497668
  70.7 13.8 %copy-start.15 = (bf16[136,288]{1,0:T(8,128)(2,1)S(1)}, bf16[136,288]{1,0:T(8,128)(2,1)}, u32[]{:S(2)}) copy-start(bf16[136,288]{1,0:T(8,128)(2,1)} %constant.46.clone.refs_13_) | copy-start | bytes 235012
  70.7 13.8 %copy-start.18 = (f32[3,7]{1,0:T(4,128)S(1)}, f32[3,7]{1,0:T(4,128)}, u32[]{:S(2)}) copy-start(f32[3,7]{1,0:T(4,128)} %refs_0_.3) | copy-start | bytes 256
  79.9 8.7 %collective-permute-start.4 = (f32[24,512]{1,0:T(8,128)S(1)}, f32[24,512]{1,0:T(8,128)S(1)}, u32[]{:S(2)}, u32[]{:S(2)}) collective-permute-start(f32[24,512]{1,0:T(8,128)S(1)} %shard_map.229.refs_14_.refs_1_), channel_id=1, source_target_pairs={{8,0},{16,8},{24,16},{32,24},{40,32},{48,40},{56,48},{64,56},{72,6... | collective-permute-start | bytes 147464 | tf_op jit(solution)/shard_map/ppermute | solution.py:573
  84.5 7.4 %collective-permute-start.3 = (f32[24,512]{1,0:T(8,128)S(1)}, f32[24,512]{1,0:T(8,128)S(1)}, u32[]{:S(2)}, u32[]{:S(2)}) collective-permute-start(f32[24,512]{1,0:T(8,128)S(1)} %shard_map.229.refs_14_.refs_1_), channel_id=1, source_target_pairs={{120,0},{0,8},{8,16},{16,24},{24,32},{32,40},{40,48},{48,56},{56,6... | collective-permute-start | bytes 147464 | tf_op jit(solution)/shard_map/ppermute | solution.py:573
  84.6 12.7 %copy-start.2 = (bf16[1536,512]{1,0:T(8,128)(2,1)S(1)}, bf16[1536,512]{1,0:T(8,128)(2,1)}, u32[]{:S(2)}) copy-start(bf16[1536,512]{1,0:T(8,128)(2,1)} %constant.49.clone.refs_6_) | copy-start | bytes 4718596
  84.6 12.7 %copy-start.16 = (bf16[160,240]{1,0:T(8,128)(2,1)S(1)}, bf16[160,240]{1,0:T(8,128)(2,1)}, u32[]{:S(2)}) copy-start(bf16[160,240]{1,0:T(8,128)(2,1)} %constant.48.clone.refs_5_) | copy-start | bytes 230404
  84.6 12.7 %copy-start.17 = (bf16[80,504]{1,0:T(8,128)(2,1)S(1)}, bf16[80,504]{1,0:T(8,128)(2,1)}, u32[]{:S(2)}) copy-start(bf16[80,504]{1,0:T(8,128)(2,1)} %constant.47.clone.refs_4_) | copy-start | bytes 241924
  91.9 7.6 %copy-start.3 = (bf16[384,1152]{1,0:T(8,128)(2,1)S(1)}, bf16[384,1152]{1,0:T(8,128)(2,1)}, u32[]{:S(2)}) copy-start(bf16[384,1152]{1,0:T(8,128)(2,1)} %constant.51.clone.refs_5_) | copy-start | bytes 2654212
  91.9 7.6 %copy-start.5 = (bf16[384,864]{1,0:T(8,128)(2,1)S(1)}, bf16[384,864]{1,0:T(8,128)(2,1)}, u32[]{:S(2)}) copy-start(bf16[384,864]{1,0:T(8,128)(2,1)} %constant.50.clone.refs_4_) | copy-start | bytes 1990660
  91.9 7.6 %copy-start.10 = (bf16[384,288]{1,0:T(8,128)(2,1)S(1)}, bf16[384,288]{1,0:T(8,128)(2,1)}, u32[]{:S(2)}) copy-start(bf16[384,288]{1,0:T(8,128)(2,1)} %constant.52.clone.refs_6_) | copy-start | bytes 663556
  92.0 5.3 %collective-permute-start.5 = (f32[48,512]{1,0:T(8,128)S(1)}, f32[48,512]{1,0:T(8,128)S(1)}, u32[]{:S(2)}, u32[]{:S(2)}) collective-permute-start(f32[48,512]{1,0:T(8,128)S(1)} %get-tuple-element.34), channel_id=1, source_target_pairs={{7,0},{0,1},{1,2},{2,3},{3,4},{4,5},{5,6},{6,7},{15,8},{8,9},{9,10... | collective-permute-start | bytes 294920 | tf_op jit(solution)/shard_map/ppermute | solution.py:575
  92.0 5.2 %collective-permute-start.6 = (f32[48,512]{1,0:T(8,128)S(1)}, f32[48,512]{1,0:T(8,128)S(1)}, u32[]{:S(2)}, u32[]{:S(2)}) collective-permute-start(f32[48,512]{1,0:T(8,128)S(1)} %get-tuple-element.36), channel_id=1, source_target_pairs={{1,0},{2,1},{3,2},{4,3},{5,4},{6,5},{7,6},{0,7},{9,8},{10,9},{11,1... | collective-permute-start | bytes 294920 | tf_op jit(solution)/shard_map/ppermute | solution.py:575
  99.1 13.5 %collective-permute-start.7 = (s16[128,1152]{1,0:T(8,128)(2,1)S(1)}, s16[128,1152]{1,0:T(8,128)(2,1)S(1)}, u32[]{:S(2)}, u32[]{:S(2)}) collective-permute-start(s16[128,1152]{1,0:T(8,128)(2,1)S(1)} %get-tuple-element.40), channel_id=1, source_target_pairs={{120,0},{0,8},{8,16},{16,24},{24,32},{32,40},{40,48},{48,56},{56,6... | collective-permute-start | bytes 884744 | tf_op jit(solution)/shard_map/ppermute | solution.py:573
  99.2 13.4 %collective-permute-start.8 = (s16[80,1152]{1,0:T(8,128)(2,1)S(1)}, s16[80,1152]{1,0:T(8,128)(2,1)S(1)}, u32[]{:S(2)}, u32[]{:S(2)}) collective-permute-start(s16[80,1152]{1,0:T(8,128)(2,1)S(1)} %get-tuple-element.41), channel_id=1, source_target_pairs={{7,0},{0,1},{1,2},{2,3},{3,4},{4,5},{5,6},{6,7},{15,8},{8,9},{9,10... | collective-permute-start | bytes 552968 | tf_op jit(solution)/shard_map/ppermute | solution.py:575
  99.2 13.4 %collective-permute-start.9 = (s16[32,1152]{1,0:T(8,128)(2,1)S(1)}, s16[32,1152]{1,0:T(8,128)(2,1)S(1)}, u32[]{:S(2)}, u32[]{:S(2)}) collective-permute-start(s16[32,1152]{1,0:T(8,128)(2,1)S(1)} %get-tuple-element.42), channel_id=1, source_target_pairs={{127,0},{120,1},{121,2},{122,3},{123,4},{124,5},{125,6},{126,7},{7... | collective-permute-start | bytes 221192 | tf_op jit(solution)/shard_map/ppermute | solution.py:581
  99.6 13.1 %copy-start.6 = (bf16[384,408]{1,0:T(8,128)(2,1)S(1)}, bf16[384,408]{1,0:T(8,128)(2,1)}, u32[]{:S(2)}) copy-start(bf16[384,408]{1,0:T(8,128)(2,1)} %constant.54.clone.refs_6_) | copy-start | bytes 940036
  99.6 13.1 %copy-start.7 = (bf16[768,256]{1,0:T(8,128)(2,1)S(1)}, bf16[768,256]{1,0:T(8,128)(2,1)}, u32[]{:S(2)}) copy-start(bf16[768,256]{1,0:T(8,128)(2,1)} %constant.53.clone.refs_5_) | copy-start | bytes 1179652

commit v6 on v5

--- a/solution.py
+++ b/solution.py
@@ -200,11 +200,24 @@
     return value - jnp.clip(value, -limit, limit)
 
 
-def tail_rows(rows, count):
-    row = lax.broadcasted_iota(jnp.int32, (rows, count), 0)
-    tail = lax.broadcasted_iota(jnp.int32, (rows, count), 1)
-    each = GROUP - SLOTS
-    return (row == tail // each * GROUP + SLOTS + tail % each).astype(f32).astype(bf16)
+def spread_rows(value):
+    count, width = value.shape
+    tiles = value.reshape(count // GROUP, GROUP, width)
+    turned = [tiles if q == 3 else pltpu.roll(tiles, SLOTS - 2 * q, 1) for q in range(4)]
+    return jnp.stack(turned, 1).reshape(4 * count, width)
+
+
+def gather_rows(value, first, second):
+    count, width = value.shape
+    tiles = value.reshape(count // (4 * GROUP), 4, GROUP, width)
+    row = lax.broadcasted_iota(jnp.int32, (count // (4 * GROUP), GROUP, width), 1)
+    result = None
+    for q in range(4):
+        for at, source in ((2 * q, first), (2 * q + 1, second)):
+            turn = (at - source) % GROUP
+            part = pltpu.roll(tiles[:, q], turn, 1) if turn else tiles[:, q]
+            result = part if result is None else jnp.where(row == at, part, result)
+    return result.reshape(count // 4, width)
 
 
 def route_kernel(dest_far, bin_far, traces_far, out_far, dest_ref, bin_ref, traces_ref, out_ref, in_sems, out_sems):
@@ -253,17 +266,16 @@
     send(3, 3 * span, LANES)
     count = GROUP - SLOTS
     tail_at = lax.broadcasted_iota(jnp.int32, (count * tiles, traces), 0)
-    put = tail_rows(rows, count * tiles)
+    is_tail = lax.broadcasted_iota(jnp.int32, (rows, span), 0) % GROUP >= SLOTS
     coming[2].wait()
     tail = traces_ref[:, 3 * span : samples]
     for j in range(3):
         tail_row = jnp.where(place == j, 0, jnp.where(place == 3 + j, 1, -rows))
         extra = (tail_at == dest * count + tail_row).astype(f32).astype(bf16)
-        rest = dot(extra, tail).astype(bf16)
+        rest = spread_rows(dot(extra, tail))
         at = slice(j * span, (j + 1) * span)
         coming[3 + j].wait()
-        both = jnp.concatenate([traces_ref[:, at], rest], 0)
-        out_ref[:, at] = dot(jnp.concatenate([main, put], 1), both).astype(bf16)
+        out_ref[:, at] = jnp.where(is_tail, rest, dot(main, traces_ref[:, at])).astype(bf16)
         send(j, j * span, span)
     for copy in going:
         copy.wait()
@@ -296,14 +308,17 @@
     for j in range(3):
         coming[1 + j].wait()
         pieces.append(dot(main, arrived_ref[:, j * span : (j + 1) * span]))
-    last = None
+    onehots, tails = [], []
+    wide = labels.astype(f32)
+    tail_at = lax.broadcasted_iota(jnp.int32, (bins, rows // 4), 0)
     for j in range(3):
-        first = pltpu.roll(code, SLOTS - j, 1)
-        second = pltpu.roll(code, SLOTS + 1 - 3 - j, 1)
-        tail_code = jnp.where(at == SLOTS, first, jnp.where(at == SLOTS + 1, second, -1))
-        onehot = (bin_at == tail_code[:1]).astype(f32).astype(bf16)
-        term = dot(onehot, arrived_ref[:, j * span : (j + 1) * span])
-        last = term if last is None else last + term
+        tail_labels = gather_rows(wide, j, 3 + j).astype(bf16)
+        tail_code = lax.dot_general(
+            weights, tail_labels, (((1,), (1,)), ((), ())), preferred_element_type=f32
+        ).astype(jnp.int32)
+        onehots.append((tail_at == tail_code[:1] - 1).astype(f32).astype(bf16))
+        tails.append(gather_rows(arrived_ref[:, j * span : (j + 1) * span].astype(f32), SLOTS, SLOTS + 1).astype(bf16))
+    last = dot(jnp.concatenate(onehots, 1), jnp.concatenate(tails, 0))
     pieces.append(last)
     matrix = state_ref[...]
     blocks = []

time: 117 us -> 116 us (level)
  no operation moved by 1% of the time
where the time goes in v6:
time: 116 us; the launch traced here: 115 us
  waiting for transfers between devices  61.1 us (53%)
  Pallas kernels  32.1 us (28%)
  starting transfers between devices  21.4 us (18%)
    all_to_all x1, waiting for transfers between devices, on_device(): lax.all_to_all(outgoing.reshape(devices, GROUP, width), ('inl', 'xl'), sp...  44 us
    pallas_call x9, Pallas kernels, call(): pl.pallas_call(body, out_shape=[jax.ShapeDtypeStruct(shape, dtype) for sh...  32.1 us
    all_to_all x1, starting transfers between devices, on_device(): lax.all_to_all(outgoing.reshape(devices, GROUP, width), ('inl', 'xl'), sp...  11.6 us
    ppermute x2, waiting for transfers between devices, shift(): return lax.ppermute(block, ('inl', 'xl'), route)  10.5 us
    ppermute x4, starting transfers between devices, shift(): lax.ppermute(block, 'inl', [((i + inline_by) % inline_devs, i) for i in r...  6.01 us
    ppermute x4, waiting for transfers between devices, shift(): lax.ppermute(block, 'inl', [((i + inline_by) % inline_devs, i) for i in r...  4.27 us
    ppermute x4, starting transfers between devices, shift(): lax.ppermute(block, 'xl', [((j + cross_by) % cross_devs, j) for j in rang...  2.98 us
  transfers between devices with their start and end apart: 11, of which 6 were waited for; matrix products, arithmetic and copies ran while one was open for 0% of the time, Pallas kernels for 12%

profile of v6, /device:TPU:0, one launch (start us, length us, event | category | flops | bytes accessed | tf_op | source)
XLA Modules:
  0.0 115.4 jit_solution(6534895652381795430)
XLA Ops:
  0.0 5.7 %shard_map.226 = bf16[1024,1664]{1,0:T(8,128)(2,1)} custom-call(s32[1,512]{1,0:T(1,128)} %bitcast.6, s32[1,512]{1,0:T(1,128)} %bitcast.7, bf16[512,2048]{1,0:T(8,128)(2,1)} %refs_2_.3), custom_call_target="tpu_custom_call" | custom-call | tf_op jit(solution)/shard_map/pallas_call | solution.py:570
  5.7 0.0 copy-start.19
  5.8 0.0 copy-start
  5.8 0.0 copy-start.9
  5.8 11.6 %all-to-all-start = ((bf16[128,8,1664]{2,1,0:T(8,128)(2,1)}), bf16[128,8,1664]{2,1,0:T(8,128)(2,1)}, u32[]{:S(2)}, u32[]{:S(2)}) async-start(bf16[128,8,1664]{2,1,0:T(8,128)(2,1)} %bitcast.5), calls=%async_computation | async-start | bytes 6815744 | tf_op jit(solution)/shard_map/all_to_all | solution.py:629
  17.4 0.0 copy-done.19
  17.4 0.1 reshape.24.refs_1_.refs_8_.refs_7_
  17.5 44.0 %all-to-all-done = bf16[128,8,1664]{2,1,0:T(8,128)(2,1)} async-done(((bf16[128,8,1664]{2,1,0:T(8,128)(2,1)}), bf16[128,8,1664]{2,1,0:T(8,128)(2,1)}, u32[]{:S(2)}, u32[]{:S(2)}) %all-to-all-start) | async-done | bytes 3407904 | tf_op jit(solution)/shard_map/all_to_all | solution.py:629
  61.6 0.0 copy-done
  61.6 0.0 copy-done.9
  61.6 6.1 %shard_map.227 = (f32[384,2048]{1,0:T(8,128)S(1)}, s16[128,1152]{1,0:T(8,128)(2,1)S(1)}, s16[80,1152]{1,0:T(8,128)(2,1)S(1)}, s16[32,1152]{1,0:T(8,128)(2,1)S(1)}) custom-call(bf16[1024,1664]{1,0:T(8,128)(2,1)} %bitcast.3.refs_0_, f32[384,1]{1,0:T(8,128)S(1)} %reshape.24.refs_1_.refs_8_.refs_7_, bf16[1152,256]{1,0:T(8,128)(2,1)S(1)} %copy-done, ...), custom_call_target="tpu_custom_call" | custom-call | tf_op jit(solution)/shard_map/pallas_call | solution.py:570
  67.7 1.3 %collective-permute-start = (s16[128,1152]{1,0:T(8,128)(2,1)S(1)}, s16[128,1152]{1,0:T(8,128)(2,1)S(1)}, u32[]{:S(2)}, u32[]{:S(2)}) collective-permute-start(s16[128,1152]{1,0:T(8,128)(2,1)S(1)} %get-tuple-element.27), channel_id=1, source_target_pairs={{8,0},{16,8},{24,16},{32,24},{40,32},{48,40},{56,48},{64,56},{72,6... | collective-permute-start | bytes 884744 | tf_op jit(solution)/shard_map/ppermute | solution.py:588
  69.0 0.0 collective-permute-start.1
  69.0 0.5 collective-permute-start.2
  69.6 0.0 copy-done.4
  69.6 0.0 copy-done.13
  69.6 0.0 copy-start.11
  69.6 0.0 copy-start.12
  69.6 0.0 copy-start.14
  69.6 0.0 copy-start.15
  69.7 0.0 copy-start.18
  69.7 4.6 %shard_map.228 = (f32[384,1024]{1,0:T(8,128)S(1)}, f32[384,1024]{1,0:T(8,128)S(1)}, f32[96,1024]{1,0:T(8,128)S(1)}) custom-call(f32[384,2048]{1,0:T(8,128)S(1)} %get-tuple-element.24.refs_0_, bf16[1152,256]{1,0:T(8,128)(2,1)S(1)} %copy-done, bf16[384,1152]{1,0:T(8,128)(2,1)S(1)} %copy-done.4, bf16[96,1152]{1,0:T(8,128)(2,1)S(1)} %copy-done.13), custom_call_target="tpu_custom_call" | custom-call | flops 1000000000 | tf_op jit(solution)/shard_map/pallas_call | solution.py:570
  74.3 2.5 %collective-permute-done.2.refs_4_.refs_6_ = s16[32,1152]{1,0:T(8,128)(2,1)S(1)} collective-permute-done((s16[32,1152]{1,0:T(8,128)(2,1)S(1)}, s16[32,1152]{1,0:T(8,128)(2,1)S(1)}, u32[]{:S(2)}, u32[]{:S(2)}) %collective-permute-start.2) | collective-permute-done | bytes 73760 | tf_op jit(solution)/shard_map/ppermute | solution.py:596
  76.8 0.0 collective-permute-done.1.refs_3_.refs_5_
  76.8 0.9 collective-permute-done.refs_2_.refs_4_
  77.7 0.0 copy-done.8
  77.7 1.1 shard_map.229.refs_14_.refs_1_
  78.8 4.6 %collective-permute-start.4 = (f32[24,512]{1,0:T(8,128)S(1)}, f32[24,512]{1,0:T(8,128)S(1)}, u32[]{:S(2)}, u32[]{:S(2)}) collective-permute-start(f32[24,512]{1,0:T(8,128)S(1)} %shard_map.229.refs_14_.refs_1_), channel_id=1, source_target_pairs={{8,0},{16,8},{24,16},{32,24},{40,32},{48,40},{56,48},{64,56},{72,6... | collective-permute-start | bytes 147464 | tf_op jit(solution)/shard_map/ppermute | solution.py:588
  83.4 0.0 collective-permute-start.3
  83.4 0.0 copy-done.1
  83.4 0.0 copy-done.11
  83.4 0.0 copy-done.12
  83.4 0.0 copy-done.14
  83.4 0.0 copy-done.15
  83.4 0.0 copy-done.18
  83.4 0.0 copy-start.2
  83.5 0.0 copy-start.16
  83.5 0.0 copy-start.17
  83.5 3.9 %shard_map.230 = (f32[288,1024]{1,0:T(8,128)S(1)}, f32[384,1024]{1,0:T(8,128)S(1)}, f32[136,1024]{1,0:T(8,128)S(1)}, f32[96,1024]{1,0:T(8,128)S(1)}, f32[96,1024]{1,0:T(8,128)S(1)}) custom-call(f32[3,7]{1,0:T(4,128)S(1)} %copy-done.18, f32[384,1024]{1,0:T(8,128)S(1)} %get-tuple-element.25.refs_1_, f32[384,1024]{1,0:T(8,128)S(1)} %get-tuple-element.26.refs_2_, ...), custom_call_target="tpu_custom_call" | custom-call | flops 1000000000 | tf_op jit(solution)/shard_map/pallas_call | solution.py:570
  87.4 0.0 collective-permute-done.4.refs_2_
  87.4 3.4 %collective-permute-done.3.refs_0_ = f32[24,512]{1,0:T(8,128)S(1)} collective-permute-done((f32[24,512]{1,0:T(8,128)S(1)}, f32[24,512]{1,0:T(8,128)S(1)}, u32[]{:S(2)}, u32[]{:S(2)}) %collective-permute-start.3) | collective-permute-done | bytes 49184 | tf_op jit(solution)/shard_map/ppermute | solution.py:588
  90.9 0.0 collective-permute-start.5
  90.9 2.9 %collective-permute-start.6 = (f32[48,512]{1,0:T(8,128)S(1)}, f32[48,512]{1,0:T(8,128)S(1)}, u32[]{:S(2)}, u32[]{:S(2)}) collective-permute-start(f32[48,512]{1,0:T(8,128)S(1)} %get-tuple-element.36), channel_id=1, source_target_pairs={{1,0},{2,1},{3,2},{4,3},{5,4},{6,5},{7,6},{0,7},{9,8},{10,9},{11,1... | collective-permute-start | bytes 294920 | tf_op jit(solution)/shard_map/ppermute | solution.py:590
  93.8 2.3 %collective-permute-done.5.refs_1_ = f32[48,512]{1,0:T(8,128)S(1)} collective-permute-done((f32[48,512]{1,0:T(8,128)S(1)}, f32[48,512]{1,0:T(8,128)S(1)}, u32[]{:S(2)}, u32[]{:S(2)}) %collective-permute-start.5) | collective-permute-done | bytes 98336 | tf_op jit(solution)/shard_map/ppermute | solution.py:590
  96.1 0.0 collective-permute-done.6.refs_3_
  96.1 0.0 copy-done.2
  96.1 0.0 copy-done.16
  96.1 0.0 copy-done.17
  96.1 1.9 %shard_map.232 = (f32[24,1024]{1,0:T(8,128)S(1)}, s16[128,1152]{1,0:T(8,128)(2,1)S(1)}, s16[80,1152]{1,0:T(8,128)(2,1)S(1)}, s16[32,1152]{1,0:T(8,128)(2,1)S(1)}) custom-call(f32[3,7]{1,0:T(4,128)S(1)} %copy-done.18, f32[48,512]{1,0:T(8,128)S(1)} %collective-permute-done.5.refs_1_, f32[72,512]{1,0:T(8,128)S(1)} %get-tuple-element.35.refs_2_, ...), custom_call_target="tpu_custom_call" | custom-call | tf_op jit(solution)/shard_map/pallas_call | solution.py:570
  98.0 0.1 collective-permute-start.7
  98.1 0.0 collective-permute-start.8
  98.1 0.3 collective-permute-start.9
  98.4 0.0 copy-done.3
  98.4 0.0 copy-done.5
  98.5 0.0 copy-done.10
  98.5 0.0 copy-start.6
  98.5 0.0 copy-start.7
  98.5 5.0 %shard_map.233.refs_0_ = f32[384,2048]{1,0:T(8,128)S(1)} custom-call(f32[288,1024]{1,0:T(8,128)S(1)} %get-tuple-element.31.refs_3_.refs_0_, f32[384,1024]{1,0:T(8,128)S(1)} %get-tuple-element.32.refs_1_, f32[96,1024]{1,0:T(8,128)S(1)} %get-tuple-element.33.refs_2_, f32[24,1024]{1,0:T(8,128)S(1)} %get-tuple-element.39.refs_3_, ...), custom_call_target="tpu_custom_call" | custom-call | flops 1000000000 | tf_op jit(solution)/shard_map/pallas_call | solution.py:570
  103.5 8.0 %collective-permute-done.9.refs_3_ = s16[32,1152]{1,0:T(8,128)(2,1)S(1)} collective-permute-done((s16[32,1152]{1,0:T(8,128)(2,1)S(1)}, s16[32,1152]{1,0:T(8,128)(2,1)S(1)}, u32[]{:S(2)}, u32[]{:S(2)}) %collective-permute-start.9) | collective-permute-done | bytes 73760 | tf_op jit(solution)/shard_map/ppermute | solution.py:596
  111.5 0.0 collective-permute-done.8.refs_2_
  111.5 0.0 collective-permute-done.7.refs_1_
  111.5 0.0 copy-done.6
  111.5 0.0 copy-done.7
  111.5 3.7 %shard_map.234 = f32[384,2048]{1,0:T(8,128)} custom-call(f32[384,2048]{1,0:T(8,128)S(1)} %shard_map.233.refs_0_, s16[128,1152]{1,0:T(8,128)(2,1)S(1)} %collective-permute-done.7.refs_1_, s16[80,1152]{1,0:T(8,128)(2,1)S(1)} %collective-permute-done.8.refs_2_, s16[32,1152]{1,0:T(8,128)(2,1)S(1)} %collective-permute-done.9.refs_3_, ...), custom_call_target="tpu_custom_call" | custom-call | tf_op jit(solution)/shard_map/pallas_call | solution.py:570
  (9 shorter events, 0.1 us)
Async XLA Ops:
  5.7 11.7 %copy-start.19 = (s32[16,24]{1,0:T(8,128)S(1)}, s32[16,24]{1,0:T(8,128)}, u32[]{:S(2)}) copy-start(s32[16,24]{1,0:T(8,128)} %param.27) | copy-start | bytes 4612
  5.8 55.8 %copy-start = (bf16[1152,256]{1,0:T(8,128)(2,1)S(1)}, bf16[1152,256]{1,0:T(8,128)(2,1)}, u32[]{:S(2)}) copy-start(bf16[1152,256]{1,0:T(8,128)(2,1)} %constant.18.clone.refs_2_.refs_1_.refs_5_.refs_11_) | copy-start | bytes 1769476
  5.8 55.8 %copy-start.9 = (bf16[136,1152]{1,0:T(8,128)(2,1)S(1)}, bf16[136,1152]{1,0:T(8,128)(2,1)}, u32[]{:S(2)}) copy-start(bf16[136,1152]{1,0:T(8,128)(2,1)} %constant.38.clone.refs_3_) | copy-start | bytes 940036
  5.8 55.8 %all-to-all-start = ((bf16[128,8,1664]{2,1,0:T(8,128)(2,1)}), bf16[128,8,1664]{2,1,0:T(8,128)(2,1)}, u32[]{:S(2)}, u32[]{:S(2)}) async-start(bf16[128,8,1664]{2,1,0:T(8,128)(2,1)} %bitcast.5), calls=%async_computation | async-start | bytes 6815744 | tf_op jit(solution)/shard_map/all_to_all | solution.py:629
  61.6 8.0 %copy-start.4 = (bf16[384,1152]{1,0:T(8,128)(2,1)S(1)}, bf16[384,1152]{1,0:T(8,128)(2,1)}, u32[]{:S(2)}) copy-start(bf16[384,1152]{1,0:T(8,128)(2,1)} %constant.39.clone.refs_2_) | copy-start | bytes 2654212
  61.6 8.0 %copy-start.13 = (bf16[96,1152]{1,0:T(8,128)(2,1)S(1)}, bf16[96,1152]{1,0:T(8,128)(2,1)}, u32[]{:S(2)}) copy-start(bf16[96,1152]{1,0:T(8,128)(2,1)} %constant.40.clone.refs_3_) | copy-start | bytes 663556
  67.7 9.9 %collective-permute-start = (s16[128,1152]{1,0:T(8,128)(2,1)S(1)}, s16[128,1152]{1,0:T(8,128)(2,1)S(1)}, u32[]{:S(2)}, u32[]{:S(2)}) collective-permute-start(s16[128,1152]{1,0:T(8,128)(2,1)S(1)} %get-tuple-element.27), channel_id=1, source_target_pairs={{8,0},{16,8},{24,16},{32,24},{40,32},{48,40},{56,48},{64,56},{72,6... | collective-permute-start | bytes 884744 | tf_op jit(solution)/shard_map/ppermute | solution.py:588
  69.0 7.8 %collective-permute-start.1 = (s16[80,1152]{1,0:T(8,128)(2,1)S(1)}, s16[80,1152]{1,0:T(8,128)(2,1)S(1)}, u32[]{:S(2)}, u32[]{:S(2)}) collective-permute-start(s16[80,1152]{1,0:T(8,128)(2,1)S(1)} %get-tuple-element.28), channel_id=1, source_target_pairs={{1,0},{2,1},{3,2},{4,3},{5,4},{6,5},{7,6},{0,7},{9,8},{10,9},{11,1... | collective-permute-start | bytes 552968 | tf_op jit(solution)/shard_map/ppermute | solution.py:590
  69.0 7.8 %collective-permute-start.2 = (s16[32,1152]{1,0:T(8,128)(2,1)S(1)}, s16[32,1152]{1,0:T(8,128)(2,1)S(1)}, u32[]{:S(2)}, u32[]{:S(2)}) collective-permute-start(s16[32,1152]{1,0:T(8,128)(2,1)S(1)} %get-tuple-element.29), channel_id=1, source_target_pairs={{9,0},{10,1},{11,2},{12,3},{13,4},{14,5},{15,6},{8,7},{17,8},{18,9... | collective-permute-start | bytes 221192 | tf_op jit(solution)/shard_map/ppermute | solution.py:596
  69.6 8.1 %copy-start.8 = (bf16[96,408]{1,0:T(8,128)(2,1)S(1)}, bf16[96,408]{1,0:T(8,128)(2,1)}, u32[]{:S(2)}) copy-start(bf16[96,408]{1,0:T(8,128)(2,1)} %constant.41.clone.refs_1_.refs_10_) | copy-start | bytes 235012
  69.6 13.8 %copy-start.1 = (bf16[1536,256]{1,0:T(8,128)(2,1)S(1)}, bf16[1536,256]{1,0:T(8,128)(2,1)}, u32[]{:S(2)}) copy-start(bf16[1536,256]{1,0:T(8,128)(2,1)} %constant.45.clone.refs_12_.refs_7_.refs_4_) | copy-start | bytes 2359300
  69.6 13.8 %copy-start.11 = (bf16[384,288]{1,0:T(8,128)(2,1)S(1)}, bf16[384,288]{1,0:T(8,128)(2,1)}, u32[]{:S(2)}) copy-start(bf16[384,288]{1,0:T(8,128)(2,1)} %constant.42.clone.refs_3_) | copy-start | bytes 663556
  69.6 13.8 %copy-start.12 = (bf16[96,1152]{1,0:T(8,128)(2,1)S(1)}, bf16[96,1152]{1,0:T(8,128)(2,1)}, u32[]{:S(2)}) copy-start(bf16[96,1152]{1,0:T(8,128)(2,1)} %constant.44.clone.refs_8_) | copy-start | bytes 663556
  69.6 13.8 %copy-start.14 = (bf16[96,864]{1,0:T(8,128)(2,1)S(1)}, bf16[96,864]{1,0:T(8,128)(2,1)}, u32[]{:S(2)}) copy-start(bf16[96,864]{1,0:T(8,128)(2,1)} %constant.43.clone.refs_7_) | copy-start | bytes 497668
  69.6 13.8 %copy-start.15 = (bf16[136,288]{1,0:T(8,128)(2,1)S(1)}, bf16[136,288]{1,0:T(8,128)(2,1)}, u32[]{:S(2)}) copy-start(bf16[136,288]{1,0:T(8,128)(2,1)} %constant.46.clone.refs_13_) | copy-start | bytes 235012
  69.7 13.8 %copy-start.18 = (f32[3,7]{1,0:T(4,128)S(1)}, f32[3,7]{1,0:T(4,128)}, u32[]{:S(2)}) copy-start(f32[3,7]{1,0:T(4,128)} %refs_0_.3) | copy-start | bytes 256
  78.8 8.6 %collective-permute-start.4 = (f32[24,512]{1,0:T(8,128)S(1)}, f32[24,512]{1,0:T(8,128)S(1)}, u32[]{:S(2)}, u32[]{:S(2)}) collective-permute-start(f32[24,512]{1,0:T(8,128)S(1)} %shard_map.229.refs_14_.refs_1_), channel_id=1, source_target_pairs={{8,0},{16,8},{24,16},{32,24},{40,32},{48,40},{56,48},{64,56},{72,6... | collective-permute-start | bytes 147464 | tf_op jit(solution)/shard_map/ppermute | solution.py:588
  83.4 7.4 %collective-permute-start.3 = (f32[24,512]{1,0:T(8,128)S(1)}, f32[24,512]{1,0:T(8,128)S(1)}, u32[]{:S(2)}, u32[]{:S(2)}) collective-permute-start(f32[24,512]{1,0:T(8,128)S(1)} %shard_map.229.refs_14_.refs_1_), channel_id=1, source_target_pairs={{120,0},{0,8},{8,16},{16,24},{24,32},{32,40},{40,48},{48,56},{56,6... | collective-permute-start | bytes 147464 | tf_op jit(solution)/shard_map/ppermute | solution.py:588
  83.4 12.7 %copy-start.2 = (bf16[1536,512]{1,0:T(8,128)(2,1)S(1)}, bf16[1536,512]{1,0:T(8,128)(2,1)}, u32[]{:S(2)}) copy-start(bf16[1536,512]{1,0:T(8,128)(2,1)} %constant.49.clone.refs_6_) | copy-start | bytes 4718596
  83.5 12.7 %copy-start.16 = (bf16[160,240]{1,0:T(8,128)(2,1)S(1)}, bf16[160,240]{1,0:T(8,128)(2,1)}, u32[]{:S(2)}) copy-start(bf16[160,240]{1,0:T(8,128)(2,1)} %constant.48.clone.refs_5_) | copy-start | bytes 230404
  83.5 12.7 %copy-start.17 = (bf16[80,504]{1,0:T(8,128)(2,1)S(1)}, bf16[80,504]{1,0:T(8,128)(2,1)}, u32[]{:S(2)}) copy-start(bf16[80,504]{1,0:T(8,128)(2,1)} %constant.47.clone.refs_4_) | copy-start | bytes 241924
  90.8 7.6 %copy-start.3 = (bf16[384,1152]{1,0:T(8,128)(2,1)S(1)}, bf16[384,1152]{1,0:T(8,128)(2,1)}, u32[]{:S(2)}) copy-start(bf16[384,1152]{1,0:T(8,128)(2,1)} %constant.51.clone.refs_5_) | copy-start | bytes 2654212
  90.8 7.6 %copy-start.5 = (bf16[384,864]{1,0:T(8,128)(2,1)S(1)}, bf16[384,864]{1,0:T(8,128)(2,1)}, u32[]{:S(2)}) copy-start(bf16[384,864]{1,0:T(8,128)(2,1)} %constant.50.clone.refs_4_) | copy-start | bytes 1990660
  90.8 7.7 %copy-start.10 = (bf16[384,288]{1,0:T(8,128)(2,1)S(1)}, bf16[384,288]{1,0:T(8,128)(2,1)}, u32[]{:S(2)}) copy-start(bf16[384,288]{1,0:T(8,128)(2,1)} %constant.52.clone.refs_6_) | copy-start | bytes 663556
  90.9 5.3 %collective-permute-start.5 = (f32[48,512]{1,0:T(8,128)S(1)}, f32[48,512]{1,0:T(8,128)S(1)}, u32[]{:S(2)}, u32[]{:S(2)}) collective-permute-start(f32[48,512]{1,0:T(8,128)S(1)} %get-tuple-element.34), channel_id=1, source_target_pairs={{7,0},{0,1},{1,2},{2,3},{3,4},{4,5},{5,6},{6,7},{15,8},{8,9},{9,10... | collective-permute-start | bytes 294920 | tf_op jit(solution)/shard_map/ppermute | solution.py:590
  90.9 5.2 %collective-permute-start.6 = (f32[48,512]{1,0:T(8,128)S(1)}, f32[48,512]{1,0:T(8,128)S(1)}, u32[]{:S(2)}, u32[]{:S(2)}) collective-permute-start(f32[48,512]{1,0:T(8,128)S(1)} %get-tuple-element.36), channel_id=1, source_target_pairs={{1,0},{2,1},{3,2},{4,3},{5,4},{6,5},{7,6},{0,7},{9,8},{10,9},{11,1... | collective-permute-start | bytes 294920 | tf_op jit(solution)/shard_map/ppermute | solution.py:590
  98.0 13.5 %collective-permute-start.7 = (s16[128,1152]{1,0:T(8,128)(2,1)S(1)}, s16[128,1152]{1,0:T(8,128)(2,1)S(1)}, u32[]{:S(2)}, u32[]{:S(2)}) collective-permute-start(s16[128,1152]{1,0:T(8,128)(2,1)S(1)} %get-tuple-element.40), channel_id=1, source_target_pairs={{120,0},{0,8},{8,16},{16,24},{24,32},{32,40},{40,48},{48,56},{56,6... | collective-permute-start | bytes 884744 | tf_op jit(solution)/shard_map/ppermute | solution.py:588
  98.1 13.4 %collective-permute-start.8 = (s16[80,1152]{1,0:T(8,128)(2,1)S(1)}, s16[80,1152]{1,0:T(8,128)(2,1)S(1)}, u32[]{:S(2)}, u32[]{:S(2)}) collective-permute-start(s16[80,1152]{1,0:T(8,128)(2,1)S(1)} %get-tuple-element.41), channel_id=1, source_target_pairs={{7,0},{0,1},{1,2},{2,3},{3,4},{4,5},{5,6},{6,7},{15,8},{8,9},{9,10... | collective-permute-start | bytes 552968 | tf_op jit(solution)/shard_map/ppermute | solution.py:590
  98.1 13.4 %collective-permute-start.9 = (s16[32,1152]{1,0:T(8,128)(2,1)S(1)}, s16[32,1152]{1,0:T(8,128)(2,1)S(1)}, u32[]{:S(2)}, u32[]{:S(2)}) collective-permute-start(s16[32,1152]{1,0:T(8,128)(2,1)S(1)} %get-tuple-element.42), channel_id=1, source_target_pairs={{127,0},{120,1},{121,2},{122,3},{123,4},{124,5},{125,6},{126,7},{7... | collective-permute-start | bytes 221192 | tf_op jit(solution)/shard_map/ppermute | solution.py:596
  98.5 13.1 %copy-start.6 = (bf16[384,408]{1,0:T(8,128)(2,1)S(1)}, bf16[384,408]{1,0:T(8,128)(2,1)}, u32[]{:S(2)}) copy-start(bf16[384,408]{1,0:T(8,128)(2,1)} %constant.54.clone.refs_6_) | copy-start | bytes 940036
  98.5 13.1 %copy-start.7 = (bf16[768,256]{1,0:T(8,128)(2,1)S(1)}, bf16[768,256]{1,0:T(8,128)(2,1)}, u32[]{:S(2)}) copy-start(bf16[768,256]{1,0:T(8,128)(2,1)} %constant.53.clone.refs_5_) | copy-start | bytes 1179652

commit v7 on v6

--- a/solution.py
+++ b/solution.py
@@ -18,6 +18,7 @@
 LARGE_LIMIT = 62 * 1024 * 1024
 MIDDLE_LIMIT = 48 * 1024 * 1024
 TOP_CODE = 32767.0
+FEW_ROWS = 160
 LAST_MARK = 880.0
 SIDE = 4
 
@@ -161,39 +162,29 @@
     return dot(matrix, jnp.concatenate([top, rest, top], 0))
 
 
+def beside(blocks, neighbours, matrix):
+    count = blocks[0].shape[0]
+    together = len(blocks) if count <= FEW_ROWS else 1
+    results = []
+    for b in range(0, len(blocks), together):
+        top, rest = split(jnp.concatenate(blocks[b : b + together], 0))
+        other, other_rest = split(jnp.concatenate(neighbours[b : b + together], 0))
+        result = dot(jnp.concatenate([top, rest, top, other, other_rest, other], 1), matrix)
+        results += [result[k * count : (k + 1) * count] for k in range(together)]
+    return results
+
+
 def time_analysis(blocks, matrix):
-    parts = [split(block) for block in blocks]
-    lows, highs = [], []
-    for b in range(len(blocks)):
-        top, rest = parts[b]
-        next_top, next_rest = [part[:, :LANES] for part in parts[(b + 1) % len(blocks)]]
-        joined = jnp.concatenate([top, rest, top, next_top, next_rest, next_top], 1)
-        result = dot(joined, matrix)
-        lows.append(result[:, :LANES])
-        highs.append(result[:, LANES:])
-    return lows, highs
+    results = beside(blocks, [block[:, :LANES] for block in blocks[1:] + blocks[:1]], matrix)
+    return [result[:, :LANES] for result in results], [result[:, LANES:] for result in results]
 
 
 def time_synthesis(blocks, matrix):
-    parts = [split(block) for block in blocks]
-    results = []
-    for b in range(len(blocks)):
-        top, rest = parts[b]
-        last_top, last_rest = parts[b - 1]
-        joined = jnp.concatenate([top, rest, top, last_top, last_rest, last_top], 1)
-        results.append(dot(joined, matrix))
-    return results
+    return beside(blocks, blocks[-1:] + blocks[:-1], matrix)
 
 
 def synthesis_from_low(lows, matrix):
-    parts = [split(low) for low in lows]
-    results = []
-    for b in range(len(lows)):
-        top, rest = parts[b]
-        last_top, last_rest = parts[b - 1]
-        joined = jnp.concatenate([top, rest, top, last_top, last_rest, last_top], 1)
-        results.append(dot(joined, matrix))
-    return results
+    return beside(lows, lows[-1:] + lows[:-1], matrix)
 
 
 def shrink(value, limit):

time: 116 us -> 115 us (level)
  no operation moved by 1% of the time
where the time goes in v7:
time: 115 us
  waiting for transfers between devices  60.3 us (52%)
  Pallas kernels  32.5 us (28%)
  starting transfers between devices  21.5 us (19%)
    all_to_all x1, waiting for transfers between devices, on_device(): lax.all_to_all(outgoing.reshape(devices, GROUP, width), ('inl', 'xl'), sp...  44 us
    pallas_call x9, Pallas kernels, call(): pl.pallas_call(body, out_shape=[jax.ShapeDtypeStruct(shape, dtype) for sh...  32.5 us
    all_to_all x1, starting transfers between devices, on_device(): lax.all_to_all(outgoing.reshape(devices, GROUP, width), ('inl', 'xl'), sp...  11.6 us
    ppermute x2, waiting for transfers between devices, shift(): return lax.ppermute(block, ('inl', 'xl'), route)  10.5 us
    ppermute x4, starting transfers between devices, shift(): lax.ppermute(block, 'inl', [((i + inline_by) % inline_devs, i) for i in r...  6.06 us
    ppermute x4, waiting for transfers between devices, shift(): lax.ppermute(block, 'inl', [((i + inline_by) % inline_devs, i) for i in r...  3.44 us
    ppermute x4, starting transfers between devices, shift(): lax.ppermute(block, 'xl', [((j + cross_by) % cross_devs, j) for j in rang...  2.98 us
    ppermute x4, waiting for transfers between devices, shift(): lax.ppermute(block, 'xl', [((j + cross_by) % cross_devs, j) for j in rang...  2.3 us
  transfers between devices with their start and end apart: 11, of which 6 were waited for; matrix products, arithmetic and copies ran while one was open for 0% of the time, Pallas kernels for 12%

profile of v7, /device:TPU:0, one launch (start us, length us, event | category | flops | bytes accessed | tf_op | source)
XLA Modules:
  0.0 115.1 jit_solution(8387774484492219974)
XLA Ops:
  0.0 5.7 %shard_map.226 = bf16[1024,1664]{1,0:T(8,128)(2,1)} custom-call(s32[1,512]{1,0:T(1,128)} %bitcast.6, s32[1,512]{1,0:T(1,128)} %bitcast.7, bf16[512,2048]{1,0:T(8,128)(2,1)} %refs_2_.3), custom_call_target="tpu_custom_call" | custom-call | tf_op jit(solution)/shard_map/pallas_call | solution.py:561
  5.7 0.0 copy-start.19
  5.8 0.0 copy-start
  5.8 0.0 copy-start.9
  5.8 11.6 %all-to-all-start = ((bf16[128,8,1664]{2,1,0:T(8,128)(2,1)}), bf16[128,8,1664]{2,1,0:T(8,128)(2,1)}, u32[]{:S(2)}, u32[]{:S(2)}) async-start(bf16[128,8,1664]{2,1,0:T(8,128)(2,1)} %bitcast.5), calls=%async_computation | async-start | bytes 6815744 | tf_op jit(solution)/shard_map/all_to_all | solution.py:620
  17.4 0.0 copy-done.19
  17.4 0.1 reshape.24.refs_1_.refs_8_.refs_7_
  17.5 44.0 %all-to-all-done = bf16[128,8,1664]{2,1,0:T(8,128)(2,1)} async-done(((bf16[128,8,1664]{2,1,0:T(8,128)(2,1)}), bf16[128,8,1664]{2,1,0:T(8,128)(2,1)}, u32[]{:S(2)}, u32[]{:S(2)}) %all-to-all-start) | async-done | bytes 3407904 | tf_op jit(solution)/shard_map/all_to_all | solution.py:620
  61.6 0.0 copy-done
  61.6 0.0 copy-done.9
  61.6 6.3 %shard_map.227 = (f32[384,2048]{1,0:T(8,128)S(1)}, s16[128,1152]{1,0:T(8,128)(2,1)S(1)}, s16[80,1152]{1,0:T(8,128)(2,1)S(1)}, s16[32,1152]{1,0:T(8,128)(2,1)S(1)}) custom-call(bf16[1024,1664]{1,0:T(8,128)(2,1)} %bitcast.3.refs_0_, f32[384,1]{1,0:T(8,128)S(1)} %reshape.24.refs_1_.refs_8_.refs_7_, bf16[1152,256]{1,0:T(8,128)(2,1)S(1)} %copy-done, ...), custom_call_target="tpu_custom_call" | custom-call | tf_op jit(solution)/shard_map/pallas_call | solution.py:561
  67.9 1.3 %collective-permute-start = (s16[128,1152]{1,0:T(8,128)(2,1)S(1)}, s16[128,1152]{1,0:T(8,128)(2,1)S(1)}, u32[]{:S(2)}, u32[]{:S(2)}) collective-permute-start(s16[128,1152]{1,0:T(8,128)(2,1)S(1)} %get-tuple-element.27), channel_id=1, source_target_pairs={{8,0},{16,8},{24,16},{32,24},{40,32},{48,40},{56,48},{64,56},{72,6... | collective-permute-start | bytes 884744 | tf_op jit(solution)/shard_map/ppermute | solution.py:579
  69.2 0.0 collective-permute-start.1
  69.2 0.5 collective-permute-start.2
  69.7 0.0 copy-done.4
  69.7 0.0 copy-done.13
  69.7 0.0 copy-start.11
  69.7 0.0 copy-start.12
  69.8 0.0 copy-start.14
  69.8 0.0 copy-start.15
  69.8 0.0 copy-start.18
  69.8 4.6 %shard_map.228 = (f32[384,1024]{1,0:T(8,128)S(1)}, f32[384,1024]{1,0:T(8,128)S(1)}, f32[96,1024]{1,0:T(8,128)S(1)}) custom-call(f32[384,2048]{1,0:T(8,128)S(1)} %get-tuple-element.24.refs_0_, bf16[1152,256]{1,0:T(8,128)(2,1)S(1)} %copy-done, bf16[384,1152]{1,0:T(8,128)(2,1)S(1)} %copy-done.4, bf16[96,1152]{1,0:T(8,128)(2,1)S(1)} %copy-done.13), custom_call_target="tpu_custom_call" | custom-call | flops 1000000000 | tf_op jit(solution)/shard_map/pallas_call | solution.py:561
  74.4 2.5 %collective-permute-done.2.refs_4_.refs_6_ = s16[32,1152]{1,0:T(8,128)(2,1)S(1)} collective-permute-done((s16[32,1152]{1,0:T(8,128)(2,1)S(1)}, s16[32,1152]{1,0:T(8,128)(2,1)S(1)}, u32[]{:S(2)}, u32[]{:S(2)}) %collective-permute-start.2) | collective-permute-done | bytes 73760 | tf_op jit(solution)/shard_map/ppermute | solution.py:587
  76.9 0.0 collective-permute-done.1.refs_3_.refs_5_
  76.9 0.9 collective-permute-done.refs_2_.refs_4_
  77.8 0.0 copy-done.8
  77.8 0.9 shard_map.229.refs_14_.refs_1_
  78.7 4.7 %collective-permute-start.4 = (f32[24,512]{1,0:T(8,128)S(1)}, f32[24,512]{1,0:T(8,128)S(1)}, u32[]{:S(2)}, u32[]{:S(2)}) collective-permute-start(f32[24,512]{1,0:T(8,128)S(1)} %shard_map.229.refs_14_.refs_1_), channel_id=1, source_target_pairs={{8,0},{16,8},{24,16},{32,24},{40,32},{48,40},{56,48},{64,56},{72,6... | collective-permute-start | bytes 147464 | tf_op jit(solution)/shard_map/ppermute | solution.py:579
  83.4 0.0 collective-permute-start.3
  83.4 0.0 copy-done.1
  83.4 0.0 copy-done.11
  83.4 0.0 copy-done.12
  83.4 0.0 copy-done.14
  83.4 0.0 copy-done.15
  83.4 0.0 copy-done.18
  83.4 0.0 copy-start.2
  83.5 0.0 copy-start.16
  83.5 0.0 copy-start.17
  83.5 4.7 %shard_map.230 = (f32[288,1024]{1,0:T(8,128)S(1)}, f32[384,1024]{1,0:T(8,128)S(1)}, f32[136,1024]{1,0:T(8,128)S(1)}, f32[96,1024]{1,0:T(8,128)S(1)}, f32[96,1024]{1,0:T(8,128)S(1)}) custom-call(f32[3,7]{1,0:T(4,128)S(1)} %copy-done.18, f32[384,1024]{1,0:T(8,128)S(1)} %get-tuple-element.25.refs_1_, f32[384,1024]{1,0:T(8,128)S(1)} %get-tuple-element.26.refs_2_, ...), custom_call_target="tpu_custom_call" | custom-call | flops 1000000000 | tf_op jit(solution)/shard_map/pallas_call | solution.py:561
  88.2 0.0 collective-permute-done.4.refs_2_
  88.2 2.6 %collective-permute-done.3.refs_0_ = f32[24,512]{1,0:T(8,128)S(1)} collective-permute-done((f32[24,512]{1,0:T(8,128)S(1)}, f32[24,512]{1,0:T(8,128)S(1)}, u32[]{:S(2)}, u32[]{:S(2)}) %collective-permute-start.3) | collective-permute-done | bytes 49184 | tf_op jit(solution)/shard_map/ppermute | solution.py:579
  90.9 0.0 collective-permute-start.5
  90.9 2.9 %collective-permute-start.6 = (f32[48,512]{1,0:T(8,128)S(1)}, f32[48,512]{1,0:T(8,128)S(1)}, u32[]{:S(2)}, u32[]{:S(2)}) collective-permute-start(f32[48,512]{1,0:T(8,128)S(1)} %get-tuple-element.36), channel_id=1, source_target_pairs={{1,0},{2,1},{3,2},{4,3},{5,4},{6,5},{7,6},{0,7},{9,8},{10,9},{11,1... | collective-permute-start | bytes 294920 | tf_op jit(solution)/shard_map/ppermute | solution.py:581
  93.8 2.3 %collective-permute-done.5.refs_1_ = f32[48,512]{1,0:T(8,128)S(1)} collective-permute-done((f32[48,512]{1,0:T(8,128)S(1)}, f32[48,512]{1,0:T(8,128)S(1)}, u32[]{:S(2)}, u32[]{:S(2)}) %collective-permute-start.5) | collective-permute-done | bytes 98336 | tf_op jit(solution)/shard_map/ppermute | solution.py:581
  96.1 0.0 collective-permute-done.6.refs_3_
  96.1 0.0 copy-done.2
  96.1 0.0 copy-done.16
  96.1 0.0 copy-done.17
  96.1 1.7 %shard_map.232 = (f32[24,1024]{1,0:T(8,128)S(1)}, s16[128,1152]{1,0:T(8,128)(2,1)S(1)}, s16[80,1152]{1,0:T(8,128)(2,1)S(1)}, s16[32,1152]{1,0:T(8,128)(2,1)S(1)}) custom-call(f32[3,7]{1,0:T(4,128)S(1)} %copy-done.18, f32[48,512]{1,0:T(8,128)S(1)} %collective-permute-done.5.refs_1_, f32[72,512]{1,0:T(8,128)S(1)} %get-tuple-element.35.refs_2_, ...), custom_call_target="tpu_custom_call" | custom-call | tf_op jit(solution)/shard_map/pallas_call | solution.py:561
  97.8 0.1 collective-permute-start.7
  97.9 0.0 collective-permute-start.8
  97.9 0.3 collective-permute-start.9
  98.2 0.0 copy-done.3
  98.2 0.0 copy-done.5
  98.2 0.0 copy-done.10
  98.3 0.0 copy-start.6
  98.3 0.0 copy-start.7
  98.3 5.0 %shard_map.233.refs_0_ = f32[384,2048]{1,0:T(8,128)S(1)} custom-call(f32[288,1024]{1,0:T(8,128)S(1)} %get-tuple-element.31.refs_3_.refs_0_, f32[384,1024]{1,0:T(8,128)S(1)} %get-tuple-element.32.refs_1_, f32[96,1024]{1,0:T(8,128)S(1)} %get-tuple-element.33.refs_2_, f32[24,1024]{1,0:T(8,128)S(1)} %get-tuple-element.39.refs_3_, ...), custom_call_target="tpu_custom_call" | custom-call | flops 1000000000 | tf_op jit(solution)/shard_map/pallas_call | solution.py:561
  103.3 8.0 %collective-permute-done.9.refs_3_ = s16[32,1152]{1,0:T(8,128)(2,1)S(1)} collective-permute-done((s16[32,1152]{1,0:T(8,128)(2,1)S(1)}, s16[32,1152]{1,0:T(8,128)(2,1)S(1)}, u32[]{:S(2)}, u32[]{:S(2)}) %collective-permute-start.9) | collective-permute-done | bytes 73760 | tf_op jit(solution)/shard_map/ppermute | solution.py:587
  111.3 0.0 collective-permute-done.8.refs_2_
  111.3 0.0 collective-permute-done.7.refs_1_
  111.3 0.0 copy-done.6
  111.3 0.0 copy-done.7
  111.3 3.6 %shard_map.234 = f32[384,2048]{1,0:T(8,128)} custom-call(f32[384,2048]{1,0:T(8,128)S(1)} %shard_map.233.refs_0_, s16[128,1152]{1,0:T(8,128)(2,1)S(1)} %collective-permute-done.7.refs_1_, s16[80,1152]{1,0:T(8,128)(2,1)S(1)} %collective-permute-done.8.refs_2_, s16[32,1152]{1,0:T(8,128)(2,1)S(1)} %collective-permute-done.9.refs_3_, ...), custom_call_target="tpu_custom_call" | custom-call | tf_op jit(solution)/shard_map/pallas_call | solution.py:561
  (9 shorter events, 0.1 us)
Async XLA Ops:
  5.7 11.7 %copy-start.19 = (s32[16,24]{1,0:T(8,128)S(1)}, s32[16,24]{1,0:T(8,128)}, u32[]{:S(2)}) copy-start(s32[16,24]{1,0:T(8,128)} %param.27) | copy-start | bytes 4612
  5.8 55.8 %copy-start = (bf16[1152,256]{1,0:T(8,128)(2,1)S(1)}, bf16[1152,256]{1,0:T(8,128)(2,1)}, u32[]{:S(2)}) copy-start(bf16[1152,256]{1,0:T(8,128)(2,1)} %constant.18.clone.refs_2_.refs_1_.refs_5_.refs_11_) | copy-start | bytes 1769476
  5.8 55.8 %copy-start.9 = (bf16[136,1152]{1,0:T(8,128)(2,1)S(1)}, bf16[136,1152]{1,0:T(8,128)(2,1)}, u32[]{:S(2)}) copy-start(bf16[136,1152]{1,0:T(8,128)(2,1)} %constant.38.clone.refs_3_) | copy-start | bytes 940036
  5.8 55.8 %all-to-all-start = ((bf16[128,8,1664]{2,1,0:T(8,128)(2,1)}), bf16[128,8,1664]{2,1,0:T(8,128)(2,1)}, u32[]{:S(2)}, u32[]{:S(2)}) async-start(bf16[128,8,1664]{2,1,0:T(8,128)(2,1)} %bitcast.5), calls=%async_computation | async-start | bytes 6815744 | tf_op jit(solution)/shard_map/all_to_all | solution.py:620
  61.6 8.1 %copy-start.4 = (bf16[384,1152]{1,0:T(8,128)(2,1)S(1)}, bf16[384,1152]{1,0:T(8,128)(2,1)}, u32[]{:S(2)}) copy-start(bf16[384,1152]{1,0:T(8,128)(2,1)} %constant.39.clone.refs_2_) | copy-start | bytes 2654212
  61.6 8.1 %copy-start.13 = (bf16[96,1152]{1,0:T(8,128)(2,1)S(1)}, bf16[96,1152]{1,0:T(8,128)(2,1)}, u32[]{:S(2)}) copy-start(bf16[96,1152]{1,0:T(8,128)(2,1)} %constant.40.clone.refs_3_) | copy-start | bytes 663556
  67.9 9.9 %collective-permute-start = (s16[128,1152]{1,0:T(8,128)(2,1)S(1)}, s16[128,1152]{1,0:T(8,128)(2,1)S(1)}, u32[]{:S(2)}, u32[]{:S(2)}) collective-permute-start(s16[128,1152]{1,0:T(8,128)(2,1)S(1)} %get-tuple-element.27), channel_id=1, source_target_pairs={{8,0},{16,8},{24,16},{32,24},{40,32},{48,40},{56,48},{64,56},{72,6... | collective-permute-start | bytes 884744 | tf_op jit(solution)/shard_map/ppermute | solution.py:579
  69.2 7.8 %collective-permute-start.1 = (s16[80,1152]{1,0:T(8,128)(2,1)S(1)}, s16[80,1152]{1,0:T(8,128)(2,1)S(1)}, u32[]{:S(2)}, u32[]{:S(2)}) collective-permute-start(s16[80,1152]{1,0:T(8,128)(2,1)S(1)} %get-tuple-element.28), channel_id=1, source_target_pairs={{1,0},{2,1},{3,2},{4,3},{5,4},{6,5},{7,6},{0,7},{9,8},{10,9},{11,1... | collective-permute-start | bytes 552968 | tf_op jit(solution)/shard_map/ppermute | solution.py:581
  69.2 7.8 %collective-permute-start.2 = (s16[32,1152]{1,0:T(8,128)(2,1)S(1)}, s16[32,1152]{1,0:T(8,128)(2,1)S(1)}, u32[]{:S(2)}, u32[]{:S(2)}) collective-permute-start(s16[32,1152]{1,0:T(8,128)(2,1)S(1)} %get-tuple-element.29), channel_id=1, source_target_pairs={{9,0},{10,1},{11,2},{12,3},{13,4},{14,5},{15,6},{8,7},{17,8},{18,9... | collective-permute-start | bytes 221192 | tf_op jit(solution)/shard_map/ppermute | solution.py:587
  69.7 8.1 %copy-start.8 = (bf16[96,408]{1,0:T(8,128)(2,1)S(1)}, bf16[96,408]{1,0:T(8,128)(2,1)}, u32[]{:S(2)}) copy-start(bf16[96,408]{1,0:T(8,128)(2,1)} %constant.41.clone.refs_1_.refs_10_) | copy-start | bytes 235012
  69.7 13.7 %copy-start.1 = (bf16[1536,256]{1,0:T(8,128)(2,1)S(1)}, bf16[1536,256]{1,0:T(8,128)(2,1)}, u32[]{:S(2)}) copy-start(bf16[1536,256]{1,0:T(8,128)(2,1)} %constant.45.clone.refs_12_.refs_7_.refs_4_) | copy-start | bytes 2359300
  69.7 13.7 %copy-start.11 = (bf16[384,288]{1,0:T(8,128)(2,1)S(1)}, bf16[384,288]{1,0:T(8,128)(2,1)}, u32[]{:S(2)}) copy-start(bf16[384,288]{1,0:T(8,128)(2,1)} %constant.42.clone.refs_3_) | copy-start | bytes 663556
  69.7 13.7 %copy-start.12 = (bf16[96,1152]{1,0:T(8,128)(2,1)S(1)}, bf16[96,1152]{1,0:T(8,128)(2,1)}, u32[]{:S(2)}) copy-start(bf16[96,1152]{1,0:T(8,128)(2,1)} %constant.44.clone.refs_8_) | copy-start | bytes 663556
  69.8 13.7 %copy-start.14 = (bf16[96,864]{1,0:T(8,128)(2,1)S(1)}, bf16[96,864]{1,0:T(8,128)(2,1)}, u32[]{:S(2)}) copy-start(bf16[96,864]{1,0:T(8,128)(2,1)} %constant.43.clone.refs_7_) | copy-start | bytes 497668
  69.8 13.7 %copy-start.15 = (bf16[136,288]{1,0:T(8,128)(2,1)S(1)}, bf16[136,288]{1,0:T(8,128)(2,1)}, u32[]{:S(2)}) copy-start(bf16[136,288]{1,0:T(8,128)(2,1)} %constant.46.clone.refs_13_) | copy-start | bytes 235012
  69.8 13.7 %copy-start.18 = (f32[3,7]{1,0:T(4,128)S(1)}, f32[3,7]{1,0:T(4,128)}, u32[]{:S(2)}) copy-start(f32[3,7]{1,0:T(4,128)} %refs_0_.3) | copy-start | bytes 256
  78.7 9.5 %collective-permute-start.4 = (f32[24,512]{1,0:T(8,128)S(1)}, f32[24,512]{1,0:T(8,128)S(1)}, u32[]{:S(2)}, u32[]{:S(2)}) collective-permute-start(f32[24,512]{1,0:T(8,128)S(1)} %shard_map.229.refs_14_.refs_1_), channel_id=1, source_target_pairs={{8,0},{16,8},{24,16},{32,24},{40,32},{48,40},{56,48},{64,56},{72,6... | collective-permute-start | bytes 147464 | tf_op jit(solution)/shard_map/ppermute | solution.py:579
  83.4 7.4 %collective-permute-start.3 = (f32[24,512]{1,0:T(8,128)S(1)}, f32[24,512]{1,0:T(8,128)S(1)}, u32[]{:S(2)}, u32[]{:S(2)}) collective-permute-start(f32[24,512]{1,0:T(8,128)S(1)} %shard_map.229.refs_14_.refs_1_), channel_id=1, source_target_pairs={{120,0},{0,8},{8,16},{16,24},{24,32},{32,40},{40,48},{48,56},{56,6... | collective-permute-start | bytes 147464 | tf_op jit(solution)/shard_map/ppermute | solution.py:579
  83.4 12.7 %copy-start.2 = (bf16[1536,512]{1,0:T(8,128)(2,1)S(1)}, bf16[1536,512]{1,0:T(8,128)(2,1)}, u32[]{:S(2)}) copy-start(bf16[1536,512]{1,0:T(8,128)(2,1)} %constant.49.clone.refs_6_) | copy-start | bytes 4718596
  83.5 12.7 %copy-start.16 = (bf16[160,240]{1,0:T(8,128)(2,1)S(1)}, bf16[160,240]{1,0:T(8,128)(2,1)}, u32[]{:S(2)}) copy-start(bf16[160,240]{1,0:T(8,128)(2,1)} %constant.48.clone.refs_5_) | copy-start | bytes 230404
  83.5 12.7 %copy-start.17 = (bf16[80,504]{1,0:T(8,128)(2,1)S(1)}, bf16[80,504]{1,0:T(8,128)(2,1)}, u32[]{:S(2)}) copy-start(bf16[80,504]{1,0:T(8,128)(2,1)} %constant.47.clone.refs_4_) | copy-start | bytes 241924
  90.8 7.4 %copy-start.3 = (bf16[384,1152]{1,0:T(8,128)(2,1)S(1)}, bf16[384,1152]{1,0:T(8,128)(2,1)}, u32[]{:S(2)}) copy-start(bf16[384,1152]{1,0:T(8,128)(2,1)} %constant.51.clone.refs_5_) | copy-start | bytes 2654212
  90.8 7.4 %copy-start.5 = (bf16[384,864]{1,0:T(8,128)(2,1)S(1)}, bf16[384,864]{1,0:T(8,128)(2,1)}, u32[]{:S(2)}) copy-start(bf16[384,864]{1,0:T(8,128)(2,1)} %constant.50.clone.refs_4_) | copy-start | bytes 1990660
  90.8 7.4 %copy-start.10 = (bf16[384,288]{1,0:T(8,128)(2,1)S(1)}, bf16[384,288]{1,0:T(8,128)(2,1)}, u32[]{:S(2)}) copy-start(bf16[384,288]{1,0:T(8,128)(2,1)} %constant.52.clone.refs_6_) | copy-start | bytes 663556
  90.9 5.3 %collective-permute-start.5 = (f32[48,512]{1,0:T(8,128)S(1)}, f32[48,512]{1,0:T(8,128)S(1)}, u32[]{:S(2)}, u32[]{:S(2)}) collective-permute-start(f32[48,512]{1,0:T(8,128)S(1)} %get-tuple-element.34), channel_id=1, source_target_pairs={{7,0},{0,1},{1,2},{2,3},{3,4},{4,5},{5,6},{6,7},{15,8},{8,9},{9,10... | collective-permute-start | bytes 294920 | tf_op jit(solution)/shard_map/ppermute | solution.py:581
  90.9 5.2 %collective-permute-start.6 = (f32[48,512]{1,0:T(8,128)S(1)}, f32[48,512]{1,0:T(8,128)S(1)}, u32[]{:S(2)}, u32[]{:S(2)}) collective-permute-start(f32[48,512]{1,0:T(8,128)S(1)} %get-tuple-element.36), channel_id=1, source_target_pairs={{1,0},{2,1},{3,2},{4,3},{5,4},{6,5},{7,6},{0,7},{9,8},{10,9},{11,1... | collective-permute-start | bytes 294920 | tf_op jit(solution)/shard_map/ppermute | solution.py:581
  97.8 13.5 %collective-permute-start.7 = (s16[128,1152]{1,0:T(8,128)(2,1)S(1)}, s16[128,1152]{1,0:T(8,128)(2,1)S(1)}, u32[]{:S(2)}, u32[]{:S(2)}) collective-permute-start(s16[128,1152]{1,0:T(8,128)(2,1)S(1)} %get-tuple-element.40), channel_id=1, source_target_pairs={{120,0},{0,8},{8,16},{16,24},{24,32},{32,40},{40,48},{48,56},{56,6... | collective-permute-start | bytes 884744 | tf_op jit(solution)/shard_map/ppermute | solution.py:579
  97.9 13.4 %collective-permute-start.8 = (s16[80,1152]{1,0:T(8,128)(2,1)S(1)}, s16[80,1152]{1,0:T(8,128)(2,1)S(1)}, u32[]{:S(2)}, u32[]{:S(2)}) collective-permute-start(s16[80,1152]{1,0:T(8,128)(2,1)S(1)} %get-tuple-element.41), channel_id=1, source_target_pairs={{7,0},{0,1},{1,2},{2,3},{3,4},{4,5},{5,6},{6,7},{15,8},{8,9},{9,10... | collective-permute-start | bytes 552968 | tf_op jit(solution)/shard_map/ppermute | solution.py:581
  97.9 13.4 %collective-permute-start.9 = (s16[32,1152]{1,0:T(8,128)(2,1)S(1)}, s16[32,1152]{1,0:T(8,128)(2,1)S(1)}, u32[]{:S(2)}, u32[]{:S(2)}) collective-permute-start(s16[32,1152]{1,0:T(8,128)(2,1)S(1)} %get-tuple-element.42), channel_id=1, source_target_pairs={{127,0},{120,1},{121,2},{122,3},{123,4},{124,5},{125,6},{126,7},{7... | collective-permute-start | bytes 221192 | tf_op jit(solution)/shard_map/ppermute | solution.py:587
  98.3 13.1 %copy-start.6 = (bf16[384,408]{1,0:T(8,128)(2,1)S(1)}, bf16[384,408]{1,0:T(8,128)(2,1)}, u32[]{:S(2)}) copy-start(bf16[384,408]{1,0:T(8,128)(2,1)} %constant.54.clone.refs_6_) | copy-start | bytes 940036
  98.3 13.1 %copy-start.7 = (bf16[768,256]{1,0:T(8,128)(2,1)S(1)}, bf16[768,256]{1,0:T(8,128)(2,1)}, u32[]{:S(2)}) copy-start(bf16[768,256]{1,0:T(8,128)(2,1)} %constant.53.clone.refs_5_) | copy-start | bytes 1179652

commit v8 on v7

--- a/solution.py
+++ b/solution.py
@@ -18,7 +18,7 @@
 LARGE_LIMIT = 62 * 1024 * 1024
 MIDDLE_LIMIT = 48 * 1024 * 1024
 TOP_CODE = 32767.0
-FEW_ROWS = 160
+FEW_ROWS = 80
 LAST_MARK = 880.0
 SIDE = 4
 

time: 115 us -> 115 us (level)
  no operation moved by 1% of the time
where the time goes in v8:
time: 115 us
  waiting for transfers between devices  61.1 us (53%)
  Pallas kernels  31.5 us (27%)
  starting transfers between devices  21.5 us (19%)
    all_to_all x1, waiting for transfers between devices, on_device(): lax.all_to_all(outgoing.reshape(devices, GROUP, width), ('inl', 'xl'), sp...  44 us
    pallas_call x9, Pallas kernels, call(): pl.pallas_call(body, out_shape=[jax.ShapeDtypeStruct(shape, dtype) for sh...  31.5 us
    all_to_all x1, starting transfers between devices, on_device(): lax.all_to_all(outgoing.reshape(devices, GROUP, width), ('inl', 'xl'), sp...  11.6 us
    ppermute x2, waiting for transfers between devices, shift(): return lax.ppermute(block, ('inl', 'xl'), route)  10.5 us
    ppermute x4, starting transfers between devices, shift(): lax.ppermute(block, 'inl', [((i + inline_by) % inline_devs, i) for i in r...  6.06 us
    ppermute x4, waiting for transfers between devices, shift(): lax.ppermute(block, 'inl', [((i + inline_by) % inline_devs, i) for i in r...  4.27 us
    ppermute x4, starting transfers between devices, shift(): lax.ppermute(block, 'xl', [((j + cross_by) % cross_devs, j) for j in rang...  2.98 us
    ppermute x4, waiting for transfers between devices, shift(): lax.ppermute(block, 'xl', [((j + cross_by) % cross_devs, j) for j in rang...  2.3 us
  transfers between devices with their start and end apart: 11, of which 6 were waited for; matrix products, arithmetic and copies ran while one was open for 0% of the time, Pallas kernels for 12%

profile of v8, /device:TPU:0, one launch (start us, length us, event | category | flops | bytes accessed | tf_op | source)
XLA Modules:
  0.0 114.8 jit_solution(12223843520732973453)
XLA Ops:
  0.0 5.7 %shard_map.226 = bf16[1024,1664]{1,0:T(8,128)(2,1)} custom-call(s32[1,512]{1,0:T(1,128)} %bitcast.6, s32[1,512]{1,0:T(1,128)} %bitcast.7, bf16[512,2048]{1,0:T(8,128)(2,1)} %refs_2_.3), custom_call_target="tpu_custom_call" | custom-call | tf_op jit(solution)/shard_map/pallas_call | solution.py:561
  5.7 0.0 copy-start.19
  5.8 0.0 copy-start
  5.8 0.0 copy-start.9
  5.8 11.6 %all-to-all-start = ((bf16[128,8,1664]{2,1,0:T(8,128)(2,1)}), bf16[128,8,1664]{2,1,0:T(8,128)(2,1)}, u32[]{:S(2)}, u32[]{:S(2)}) async-start(bf16[128,8,1664]{2,1,0:T(8,128)(2,1)} %bitcast.5), calls=%async_computation | async-start | bytes 6815744 | tf_op jit(solution)/shard_map/all_to_all | solution.py:620
  17.4 0.0 copy-done.19
  17.4 0.1 reshape.24.refs_1_.refs_8_.refs_7_
  17.5 44.0 %all-to-all-done = bf16[128,8,1664]{2,1,0:T(8,128)(2,1)} async-done(((bf16[128,8,1664]{2,1,0:T(8,128)(2,1)}), bf16[128,8,1664]{2,1,0:T(8,128)(2,1)}, u32[]{:S(2)}, u32[]{:S(2)}) %all-to-all-start) | async-done | bytes 3407904 | tf_op jit(solution)/shard_map/all_to_all | solution.py:620
  61.6 0.0 copy-done
  61.6 0.0 copy-done.9
  61.6 6.1 %shard_map.227 = (f32[384,2048]{1,0:T(8,128)S(1)}, s16[128,1152]{1,0:T(8,128)(2,1)S(1)}, s16[80,1152]{1,0:T(8,128)(2,1)S(1)}, s16[32,1152]{1,0:T(8,128)(2,1)S(1)}) custom-call(bf16[1024,1664]{1,0:T(8,128)(2,1)} %bitcast.3.refs_0_, f32[384,1]{1,0:T(8,128)S(1)} %reshape.24.refs_1_.refs_8_.refs_7_, bf16[1152,256]{1,0:T(8,128)(2,1)S(1)} %copy-done, ...), custom_call_target="tpu_custom_call" | custom-call | tf_op jit(solution)/shard_map/pallas_call | solution.py:561
  67.7 1.3 %collective-permute-start = (s16[128,1152]{1,0:T(8,128)(2,1)S(1)}, s16[128,1152]{1,0:T(8,128)(2,1)S(1)}, u32[]{:S(2)}, u32[]{:S(2)}) collective-permute-start(s16[128,1152]{1,0:T(8,128)(2,1)S(1)} %get-tuple-element.27), channel_id=1, source_target_pairs={{8,0},{16,8},{24,16},{32,24},{40,32},{48,40},{56,48},{64,56},{72,6... | collective-permute-start | bytes 884744 | tf_op jit(solution)/shard_map/ppermute | solution.py:579
  69.0 0.0 collective-permute-start.1
  69.0 0.5 collective-permute-start.2
  69.6 0.0 copy-done.4
  69.6 0.0 copy-done.13
  69.6 0.0 copy-start.11
  69.6 0.0 copy-start.12
  69.6 0.0 copy-start.14
  69.6 0.0 copy-start.15
  69.7 0.0 copy-start.18
  69.7 4.6 %shard_map.228 = (f32[384,1024]{1,0:T(8,128)S(1)}, f32[384,1024]{1,0:T(8,128)S(1)}, f32[96,1024]{1,0:T(8,128)S(1)}) custom-call(f32[384,2048]{1,0:T(8,128)S(1)} %get-tuple-element.24.refs_0_, bf16[1152,256]{1,0:T(8,128)(2,1)S(1)} %copy-done, bf16[384,1152]{1,0:T(8,128)(2,1)S(1)} %copy-done.4, bf16[96,1152]{1,0:T(8,128)(2,1)S(1)} %copy-done.13), custom_call_target="tpu_custom_call" | custom-call | flops 1000000000 | tf_op jit(solution)/shard_map/pallas_call | solution.py:561
  74.3 2.5 %collective-permute-done.2.refs_4_.refs_6_ = s16[32,1152]{1,0:T(8,128)(2,1)S(1)} collective-permute-done((s16[32,1152]{1,0:T(8,128)(2,1)S(1)}, s16[32,1152]{1,0:T(8,128)(2,1)S(1)}, u32[]{:S(2)}, u32[]{:S(2)}) %collective-permute-start.2) | collective-permute-done | bytes 73760 | tf_op jit(solution)/shard_map/ppermute | solution.py:587
  76.8 0.0 collective-permute-done.1.refs_3_.refs_5_
  76.8 0.9 collective-permute-done.refs_2_.refs_4_
  77.7 0.0 copy-done.8
  77.7 0.9 shard_map.229.refs_14_.refs_1_
  78.6 4.7 %collective-permute-start.4 = (f32[24,512]{1,0:T(8,128)S(1)}, f32[24,512]{1,0:T(8,128)S(1)}, u32[]{:S(2)}, u32[]{:S(2)}) collective-permute-start(f32[24,512]{1,0:T(8,128)S(1)} %shard_map.229.refs_14_.refs_1_), channel_id=1, source_target_pairs={{8,0},{16,8},{24,16},{32,24},{40,32},{48,40},{56,48},{64,56},{72,6... | collective-permute-start | bytes 147464 | tf_op jit(solution)/shard_map/ppermute | solution.py:579
  83.3 0.0 collective-permute-start.3
  83.3 0.0 copy-done.1
  83.3 0.0 copy-done.11
  83.3 0.0 copy-done.12
  83.3 0.0 copy-done.14
  83.3 0.0 copy-done.15
  83.3 0.0 copy-done.18
  83.3 0.0 copy-start.2
  83.3 0.0 copy-start.16
  83.3 0.0 copy-start.17
  83.3 3.9 %shard_map.230 = (f32[288,1024]{1,0:T(8,128)S(1)}, f32[384,1024]{1,0:T(8,128)S(1)}, f32[136,1024]{1,0:T(8,128)S(1)}, f32[96,1024]{1,0:T(8,128)S(1)}, f32[96,1024]{1,0:T(8,128)S(1)}) custom-call(f32[3,7]{1,0:T(4,128)S(1)} %copy-done.18, f32[384,1024]{1,0:T(8,128)S(1)} %get-tuple-element.25.refs_1_, f32[384,1024]{1,0:T(8,128)S(1)} %get-tuple-element.26.refs_2_, ...), custom_call_target="tpu_custom_call" | custom-call | flops 1000000000 | tf_op jit(solution)/shard_map/pallas_call | solution.py:561
  87.3 0.0 collective-permute-done.4.refs_2_
  87.3 3.4 %collective-permute-done.3.refs_0_ = f32[24,512]{1,0:T(8,128)S(1)} collective-permute-done((f32[24,512]{1,0:T(8,128)S(1)}, f32[24,512]{1,0:T(8,128)S(1)}, u32[]{:S(2)}, u32[]{:S(2)}) %collective-permute-start.3) | collective-permute-done | bytes 49184 | tf_op jit(solution)/shard_map/ppermute | solution.py:579
  90.7 0.0 collective-permute-start.5
  90.7 2.9 %collective-permute-start.6 = (f32[48,512]{1,0:T(8,128)S(1)}, f32[48,512]{1,0:T(8,128)S(1)}, u32[]{:S(2)}, u32[]{:S(2)}) collective-permute-start(f32[48,512]{1,0:T(8,128)S(1)} %get-tuple-element.36), channel_id=1, source_target_pairs={{1,0},{2,1},{3,2},{4,3},{5,4},{6,5},{7,6},{0,7},{9,8},{10,9},{11,1... | collective-permute-start | bytes 294920 | tf_op jit(solution)/shard_map/ppermute | solution.py:581
  93.7 2.3 %collective-permute-done.5.refs_1_ = f32[48,512]{1,0:T(8,128)S(1)} collective-permute-done((f32[48,512]{1,0:T(8,128)S(1)}, f32[48,512]{1,0:T(8,128)S(1)}, u32[]{:S(2)}, u32[]{:S(2)}) %collective-permute-start.5) | collective-permute-done | bytes 98336 | tf_op jit(solution)/shard_map/ppermute | solution.py:581
  96.0 0.0 collective-permute-done.6.refs_3_
  96.0 0.0 copy-done.2
  96.0 0.0 copy-done.16
  96.0 0.0 copy-done.17
  96.0 1.7 %shard_map.232 = (f32[24,1024]{1,0:T(8,128)S(1)}, s16[128,1152]{1,0:T(8,128)(2,1)S(1)}, s16[80,1152]{1,0:T(8,128)(2,1)S(1)}, s16[32,1152]{1,0:T(8,128)(2,1)S(1)}) custom-call(f32[3,7]{1,0:T(4,128)S(1)} %copy-done.18, f32[48,512]{1,0:T(8,128)S(1)} %collective-permute-done.5.refs_1_, f32[72,512]{1,0:T(8,128)S(1)} %get-tuple-element.35.refs_2_, ...), custom_call_target="tpu_custom_call" | custom-call | tf_op jit(solution)/shard_map/pallas_call | solution.py:561
  97.7 0.1 collective-permute-start.7
  97.8 0.0 collective-permute-start.8
  97.8 0.3 collective-permute-start.9
  98.1 0.0 copy-done.3
  98.1 0.0 copy-done.5
  98.1 0.0 copy-done.10
  98.1 0.0 copy-start.6
  98.1 0.0 copy-start.7
  98.2 5.0 %shard_map.233.refs_0_ = f32[384,2048]{1,0:T(8,128)S(1)} custom-call(f32[288,1024]{1,0:T(8,128)S(1)} %get-tuple-element.31.refs_3_.refs_0_, f32[384,1024]{1,0:T(8,128)S(1)} %get-tuple-element.32.refs_1_, f32[96,1024]{1,0:T(8,128)S(1)} %get-tuple-element.33.refs_2_, f32[24,1024]{1,0:T(8,128)S(1)} %get-tuple-element.39.refs_3_, ...), custom_call_target="tpu_custom_call" | custom-call | flops 1000000000 | tf_op jit(solution)/shard_map/pallas_call | solution.py:561
  103.2 8.0 %collective-permute-done.9.refs_3_ = s16[32,1152]{1,0:T(8,128)(2,1)S(1)} collective-permute-done((s16[32,1152]{1,0:T(8,128)(2,1)S(1)}, s16[32,1152]{1,0:T(8,128)(2,1)S(1)}, u32[]{:S(2)}, u32[]{:S(2)}) %collective-permute-start.9) | collective-permute-done | bytes 73760 | tf_op jit(solution)/shard_map/ppermute | solution.py:587
  111.2 0.0 collective-permute-done.8.refs_2_
  111.2 0.0 collective-permute-done.7.refs_1_
  111.2 0.0 copy-done.6
  111.2 0.0 copy-done.7
  111.2 3.4 %shard_map.234 = f32[384,2048]{1,0:T(8,128)} custom-call(f32[384,2048]{1,0:T(8,128)S(1)} %shard_map.233.refs_0_, s16[128,1152]{1,0:T(8,128)(2,1)S(1)} %collective-permute-done.7.refs_1_, s16[80,1152]{1,0:T(8,128)(2,1)S(1)} %collective-permute-done.8.refs_2_, s16[32,1152]{1,0:T(8,128)(2,1)S(1)} %collective-permute-done.9.refs_3_, ...), custom_call_target="tpu_custom_call" | custom-call | tf_op jit(solution)/shard_map/pallas_call | solution.py:561
  (9 shorter events, 0.1 us)
Async XLA Ops:
  5.7 11.7 %copy-start.19 = (s32[16,24]{1,0:T(8,128)S(1)}, s32[16,24]{1,0:T(8,128)}, u32[]{:S(2)}) copy-start(s32[16,24]{1,0:T(8,128)} %param.27) | copy-start | bytes 4612
  5.8 55.8 %copy-start = (bf16[1152,256]{1,0:T(8,128)(2,1)S(1)}, bf16[1152,256]{1,0:T(8,128)(2,1)}, u32[]{:S(2)}) copy-start(bf16[1152,256]{1,0:T(8,128)(2,1)} %constant.18.clone.refs_2_.refs_1_.refs_5_.refs_11_) | copy-start | bytes 1769476
  5.8 55.8 %copy-start.9 = (bf16[136,1152]{1,0:T(8,128)(2,1)S(1)}, bf16[136,1152]{1,0:T(8,128)(2,1)}, u32[]{:S(2)}) copy-start(bf16[136,1152]{1,0:T(8,128)(2,1)} %constant.38.clone.refs_3_) | copy-start | bytes 940036
  5.8 55.8 %all-to-all-start = ((bf16[128,8,1664]{2,1,0:T(8,128)(2,1)}), bf16[128,8,1664]{2,1,0:T(8,128)(2,1)}, u32[]{:S(2)}, u32[]{:S(2)}) async-start(bf16[128,8,1664]{2,1,0:T(8,128)(2,1)} %bitcast.5), calls=%async_computation | async-start | bytes 6815744 | tf_op jit(solution)/shard_map/all_to_all | solution.py:620
  61.6 8.0 %copy-start.4 = (bf16[384,1152]{1,0:T(8,128)(2,1)S(1)}, bf16[384,1152]{1,0:T(8,128)(2,1)}, u32[]{:S(2)}) copy-start(bf16[384,1152]{1,0:T(8,128)(2,1)} %constant.39.clone.refs_2_) | copy-start | bytes 2654212
  61.6 8.0 %copy-start.13 = (bf16[96,1152]{1,0:T(8,128)(2,1)S(1)}, bf16[96,1152]{1,0:T(8,128)(2,1)}, u32[]{:S(2)}) copy-start(bf16[96,1152]{1,0:T(8,128)(2,1)} %constant.40.clone.refs_3_) | copy-start | bytes 663556
  67.7 9.9 %collective-permute-start = (s16[128,1152]{1,0:T(8,128)(2,1)S(1)}, s16[128,1152]{1,0:T(8,128)(2,1)S(1)}, u32[]{:S(2)}, u32[]{:S(2)}) collective-permute-start(s16[128,1152]{1,0:T(8,128)(2,1)S(1)} %get-tuple-element.27), channel_id=1, source_target_pairs={{8,0},{16,8},{24,16},{32,24},{40,32},{48,40},{56,48},{64,56},{72,6... | collective-permute-start | bytes 884744 | tf_op jit(solution)/shard_map/ppermute | solution.py:579
  69.0 7.8 %collective-permute-start.1 = (s16[80,1152]{1,0:T(8,128)(2,1)S(1)}, s16[80,1152]{1,0:T(8,128)(2,1)S(1)}, u32[]{:S(2)}, u32[]{:S(2)}) collective-permute-start(s16[80,1152]{1,0:T(8,128)(2,1)S(1)} %get-tuple-element.28), channel_id=1, source_target_pairs={{1,0},{2,1},{3,2},{4,3},{5,4},{6,5},{7,6},{0,7},{9,8},{10,9},{11,1... | collective-permute-start | bytes 552968 | tf_op jit(solution)/shard_map/ppermute | solution.py:581
  69.0 7.8 %collective-permute-start.2 = (s16[32,1152]{1,0:T(8,128)(2,1)S(1)}, s16[32,1152]{1,0:T(8,128)(2,1)S(1)}, u32[]{:S(2)}, u32[]{:S(2)}) collective-permute-start(s16[32,1152]{1,0:T(8,128)(2,1)S(1)} %get-tuple-element.29), channel_id=1, source_target_pairs={{9,0},{10,1},{11,2},{12,3},{13,4},{14,5},{15,6},{8,7},{17,8},{18,9... | collective-permute-start | bytes 221192 | tf_op jit(solution)/shard_map/ppermute | solution.py:587
  69.6 8.1 %copy-start.8 = (bf16[96,408]{1,0:T(8,128)(2,1)S(1)}, bf16[96,408]{1,0:T(8,128)(2,1)}, u32[]{:S(2)}) copy-start(bf16[96,408]{1,0:T(8,128)(2,1)} %constant.41.clone.refs_1_.refs_10_) | copy-start | bytes 235012
  69.6 13.7 %copy-start.1 = (bf16[1536,256]{1,0:T(8,128)(2,1)S(1)}, bf16[1536,256]{1,0:T(8,128)(2,1)}, u32[]{:S(2)}) copy-start(bf16[1536,256]{1,0:T(8,128)(2,1)} %constant.45.clone.refs_12_.refs_7_.refs_4_) | copy-start | bytes 2359300
  69.6 13.7 %copy-start.11 = (bf16[384,288]{1,0:T(8,128)(2,1)S(1)}, bf16[384,288]{1,0:T(8,128)(2,1)}, u32[]{:S(2)}) copy-start(bf16[384,288]{1,0:T(8,128)(2,1)} %constant.42.clone.refs_3_) | copy-start | bytes 663556
  69.6 13.6 %copy-start.12 = (bf16[96,1152]{1,0:T(8,128)(2,1)S(1)}, bf16[96,1152]{1,0:T(8,128)(2,1)}, u32[]{:S(2)}) copy-start(bf16[96,1152]{1,0:T(8,128)(2,1)} %constant.44.clone.refs_8_) | copy-start | bytes 663556
  69.6 13.6 %copy-start.14 = (bf16[96,864]{1,0:T(8,128)(2,1)S(1)}, bf16[96,864]{1,0:T(8,128)(2,1)}, u32[]{:S(2)}) copy-start(bf16[96,864]{1,0:T(8,128)(2,1)} %constant.43.clone.refs_7_) | copy-start | bytes 497668
  69.6 13.6 %copy-start.15 = (bf16[136,288]{1,0:T(8,128)(2,1)S(1)}, bf16[136,288]{1,0:T(8,128)(2,1)}, u32[]{:S(2)}) copy-start(bf16[136,288]{1,0:T(8,128)(2,1)} %constant.46.clone.refs_13_) | copy-start | bytes 235012
  69.7 13.6 %copy-start.18 = (f32[3,7]{1,0:T(4,128)S(1)}, f32[3,7]{1,0:T(4,128)}, u32[]{:S(2)}) copy-start(f32[3,7]{1,0:T(4,128)} %refs_0_.3) | copy-start | bytes 256
  78.6 8.7 %collective-permute-start.4 = (f32[24,512]{1,0:T(8,128)S(1)}, f32[24,512]{1,0:T(8,128)S(1)}, u32[]{:S(2)}, u32[]{:S(2)}) collective-permute-start(f32[24,512]{1,0:T(8,128)S(1)} %shard_map.229.refs_14_.refs_1_), channel_id=1, source_target_pairs={{8,0},{16,8},{24,16},{32,24},{40,32},{48,40},{56,48},{64,56},{72,6... | collective-permute-start | bytes 147464 | tf_op jit(solution)/shard_map/ppermute | solution.py:579
  83.3 7.4 %collective-permute-start.3 = (f32[24,512]{1,0:T(8,128)S(1)}, f32[24,512]{1,0:T(8,128)S(1)}, u32[]{:S(2)}, u32[]{:S(2)}) collective-permute-start(f32[24,512]{1,0:T(8,128)S(1)} %shard_map.229.refs_14_.refs_1_), channel_id=1, source_target_pairs={{120,0},{0,8},{8,16},{16,24},{24,32},{32,40},{40,48},{48,56},{56,6... | collective-permute-start | bytes 147464 | tf_op jit(solution)/shard_map/ppermute | solution.py:579
  83.3 12.7 %copy-start.2 = (bf16[1536,512]{1,0:T(8,128)(2,1)S(1)}, bf16[1536,512]{1,0:T(8,128)(2,1)}, u32[]{:S(2)}) copy-start(bf16[1536,512]{1,0:T(8,128)(2,1)} %constant.49.clone.refs_6_) | copy-start | bytes 4718596
  83.3 12.7 %copy-start.16 = (bf16[160,240]{1,0:T(8,128)(2,1)S(1)}, bf16[160,240]{1,0:T(8,128)(2,1)}, u32[]{:S(2)}) copy-start(bf16[160,240]{1,0:T(8,128)(2,1)} %constant.48.clone.refs_5_) | copy-start | bytes 230404
  83.3 12.7 %copy-start.17 = (bf16[80,504]{1,0:T(8,128)(2,1)S(1)}, bf16[80,504]{1,0:T(8,128)(2,1)}, u32[]{:S(2)}) copy-start(bf16[80,504]{1,0:T(8,128)(2,1)} %constant.47.clone.refs_4_) | copy-start | bytes 241924
  90.7 7.4 %copy-start.3 = (bf16[384,1152]{1,0:T(8,128)(2,1)S(1)}, bf16[384,1152]{1,0:T(8,128)(2,1)}, u32[]{:S(2)}) copy-start(bf16[384,1152]{1,0:T(8,128)(2,1)} %constant.51.clone.refs_5_) | copy-start | bytes 2654212
  90.7 7.4 %copy-start.5 = (bf16[384,864]{1,0:T(8,128)(2,1)S(1)}, bf16[384,864]{1,0:T(8,128)(2,1)}, u32[]{:S(2)}) copy-start(bf16[384,864]{1,0:T(8,128)(2,1)} %constant.50.clone.refs_4_) | copy-start | bytes 1990660
  90.7 7.5 %copy-start.10 = (bf16[384,288]{1,0:T(8,128)(2,1)S(1)}, bf16[384,288]{1,0:T(8,128)(2,1)}, u32[]{:S(2)}) copy-start(bf16[384,288]{1,0:T(8,128)(2,1)} %constant.52.clone.refs_6_) | copy-start | bytes 663556
  90.7 5.3 %collective-permute-start.5 = (f32[48,512]{1,0:T(8,128)S(1)}, f32[48,512]{1,0:T(8,128)S(1)}, u32[]{:S(2)}, u32[]{:S(2)}) collective-permute-start(f32[48,512]{1,0:T(8,128)S(1)} %get-tuple-element.34), channel_id=1, source_target_pairs={{7,0},{0,1},{1,2},{2,3},{3,4},{4,5},{5,6},{6,7},{15,8},{8,9},{9,10... | collective-permute-start | bytes 294920 | tf_op jit(solution)/shard_map/ppermute | solution.py:581
  90.7 5.2 %collective-permute-start.6 = (f32[48,512]{1,0:T(8,128)S(1)}, f32[48,512]{1,0:T(8,128)S(1)}, u32[]{:S(2)}, u32[]{:S(2)}) collective-permute-start(f32[48,512]{1,0:T(8,128)S(1)} %get-tuple-element.36), channel_id=1, source_target_pairs={{1,0},{2,1},{3,2},{4,3},{5,4},{6,5},{7,6},{0,7},{9,8},{10,9},{11,1... | collective-permute-start | bytes 294920 | tf_op jit(solution)/shard_map/ppermute | solution.py:581
  97.7 13.5 %collective-permute-start.7 = (s16[128,1152]{1,0:T(8,128)(2,1)S(1)}, s16[128,1152]{1,0:T(8,128)(2,1)S(1)}, u32[]{:S(2)}, u32[]{:S(2)}) collective-permute-start(s16[128,1152]{1,0:T(8,128)(2,1)S(1)} %get-tuple-element.40), channel_id=1, source_target_pairs={{120,0},{0,8},{8,16},{16,24},{24,32},{32,40},{40,48},{48,56},{56,6... | collective-permute-start | bytes 884744 | tf_op jit(solution)/shard_map/ppermute | solution.py:579
  97.8 13.4 %collective-permute-start.8 = (s16[80,1152]{1,0:T(8,128)(2,1)S(1)}, s16[80,1152]{1,0:T(8,128)(2,1)S(1)}, u32[]{:S(2)}, u32[]{:S(2)}) collective-permute-start(s16[80,1152]{1,0:T(8,128)(2,1)S(1)} %get-tuple-element.41), channel_id=1, source_target_pairs={{7,0},{0,1},{1,2},{2,3},{3,4},{4,5},{5,6},{6,7},{15,8},{8,9},{9,10... | collective-permute-start | bytes 552968 | tf_op jit(solution)/shard_map/ppermute | solution.py:581
  97.8 13.4 %collective-permute-start.9 = (s16[32,1152]{1,0:T(8,128)(2,1)S(1)}, s16[32,1152]{1,0:T(8,128)(2,1)S(1)}, u32[]{:S(2)}, u32[]{:S(2)}) collective-permute-start(s16[32,1152]{1,0:T(8,128)(2,1)S(1)} %get-tuple-element.42), channel_id=1, source_target_pairs={{127,0},{120,1},{121,2},{122,3},{123,4},{124,5},{125,6},{126,7},{7... | collective-permute-start | bytes 221192 | tf_op jit(solution)/shard_map/ppermute | solution.py:587
  98.1 13.1 %copy-start.6 = (bf16[384,408]{1,0:T(8,128)(2,1)S(1)}, bf16[384,408]{1,0:T(8,128)(2,1)}, u32[]{:S(2)}) copy-start(bf16[384,408]{1,0:T(8,128)(2,1)} %constant.54.clone.refs_6_) | copy-start | bytes 940036
  98.1 13.1 %copy-start.7 = (bf16[768,256]{1,0:T(8,128)(2,1)S(1)}, bf16[768,256]{1,0:T(8,128)(2,1)}, u32[]{:S(2)}) copy-start(bf16[768,256]{1,0:T(8,128)(2,1)} %constant.53.clone.refs_5_) | copy-start | bytes 1179652

commit v9 on v7

--- a/solution.py
+++ b/solution.py
@@ -244,17 +244,6 @@
         going.append(pltpu.make_async_copy(out_ref.at[:, at], out_far.at[:, at], out_sems.at[number]))
         going[-1].start()
 
-    code = bin_ref[...] + 1
-    lane = lax.broadcasted_iota(jnp.int32, (LANES, traces), 0)
-    digits = jnp.where(lane == 0, code // 2, jnp.where(lane == 1, code % 2, 0))
-    labels = lax.dot_general(
-        main,
-        digits.astype(f32).astype(bf16),
-        (((1,), (1,)), ((), ())),
-        preferred_element_type=f32,
-    )
-    out_ref[:, 3 * span :] = labels.astype(bf16)
-    send(3, 3 * span, LANES)
     count = GROUP - SLOTS
     tail_at = lax.broadcasted_iota(jnp.int32, (count * tiles, traces), 0)
     is_tail = lax.broadcasted_iota(jnp.int32, (rows, span), 0) % GROUP >= SLOTS
@@ -268,6 +257,17 @@
         coming[3 + j].wait()
         out_ref[:, at] = jnp.where(is_tail, rest, dot(main, traces_ref[:, at])).astype(bf16)
         send(j, j * span, span)
+    code = bin_ref[...] + 1
+    lane = lax.broadcasted_iota(jnp.int32, (LANES, traces), 0)
+    digits = jnp.where(lane == 0, code // 2, jnp.where(lane == 1, code % 2, 0))
+    labels = lax.dot_general(
+        main,
+        digits.astype(f32).astype(bf16),
+        (((1,), (1,)), ((), ())),
+        preferred_element_type=f32,
+    )
+    out_ref[:, 3 * span :] = labels.astype(bf16)
+    send(3, 3 * span, LANES)
     for copy in going:
         copy.wait()
 

time: 115 us -> 115 us (level)
  transfers between devices with their start and end apart: 11 -> 11, of which waited for: 6 -> 6; matrix products, arithmetic and copies ran while one was open for 0% -> 0% of each run, Pallas kernels for 12% -> 13%
where the time goes in v9:
time: 115 us
  waiting for transfers between devices  60.3 us (52%)
  Pallas kernels  32.5 us (28%)
  starting transfers between devices  21.5 us (19%)
    all_to_all x1, waiting for transfers between devices, on_device(): lax.all_to_all(outgoing.reshape(devices, GROUP, width), ('inl', 'xl'), sp...  44 us
    pallas_call x9, Pallas kernels, call(): pl.pallas_call(body, out_shape=[jax.ShapeDtypeStruct(shape, dtype) for sh...  32.5 us
    all_to_all x1, starting transfers between devices, on_device(): lax.all_to_all(outgoing.reshape(devices, GROUP, width), ('inl', 'xl'), sp...  11.6 us
    ppermute x2, waiting for transfers between devices, shift(): return lax.ppermute(block, ('inl', 'xl'), route)  10.5 us
    ppermute x4, starting transfers between devices, shift(): lax.ppermute(block, 'inl', [((i + inline_by) % inline_devs, i) for i in r...  6.05 us
    ppermute x4, waiting for transfers between devices, shift(): lax.ppermute(block, 'inl', [((i + inline_by) % inline_devs, i) for i in r...  3.43 us
    ppermute x4, starting transfers between devices, shift(): lax.ppermute(block, 'xl', [((j + cross_by) % cross_devs, j) for j in rang...  2.98 us
    ppermute x4, waiting for transfers between devices, shift(): lax.ppermute(block, 'xl', [((j + cross_by) % cross_devs, j) for j in rang...  2.3 us
  transfers between devices with their start and end apart: 11, of which 6 were waited for; matrix products, arithmetic and copies ran while one was open for 0% of the time, Pallas kernels for 13%

profile of v9, /device:TPU:0, one launch (start us, length us, event | category | flops | bytes accessed | tf_op | source)
XLA Modules:
  0.0 115.0 jit_solution(8705830400569301186)
XLA Ops:
  0.0 5.7 %shard_map.226 = bf16[1024,1664]{1,0:T(8,128)(2,1)} custom-call(s32[1,512]{1,0:T(1,128)} %bitcast.6, s32[1,512]{1,0:T(1,128)} %bitcast.7, bf16[512,2048]{1,0:T(8,128)(2,1)} %refs_2_.3), custom_call_target="tpu_custom_call" | custom-call | tf_op jit(solution)/shard_map/pallas_call | solution.py:561
  5.7 0.0 copy-start.19
  5.7 0.0 copy-start
  5.7 0.0 copy-start.9
  5.7 11.6 %all-to-all-start = ((bf16[128,8,1664]{2,1,0:T(8,128)(2,1)}), bf16[128,8,1664]{2,1,0:T(8,128)(2,1)}, u32[]{:S(2)}, u32[]{:S(2)}) async-start(bf16[128,8,1664]{2,1,0:T(8,128)(2,1)} %bitcast.5), calls=%async_computation | async-start | bytes 6815744 | tf_op jit(solution)/shard_map/all_to_all | solution.py:620
  17.4 0.0 copy-done.19
  17.4 0.1 reshape.24.refs_1_.refs_8_.refs_7_
  17.5 44.0 %all-to-all-done = bf16[128,8,1664]{2,1,0:T(8,128)(2,1)} async-done(((bf16[128,8,1664]{2,1,0:T(8,128)(2,1)}), bf16[128,8,1664]{2,1,0:T(8,128)(2,1)}, u32[]{:S(2)}, u32[]{:S(2)}) %all-to-all-start) | async-done | bytes 3407904 | tf_op jit(solution)/shard_map/all_to_all | solution.py:620
  61.5 0.0 copy-done
  61.5 0.0 copy-done.9
  61.6 6.3 %shard_map.227 = (f32[384,2048]{1,0:T(8,128)S(1)}, s16[128,1152]{1,0:T(8,128)(2,1)S(1)}, s16[80,1152]{1,0:T(8,128)(2,1)S(1)}, s16[32,1152]{1,0:T(8,128)(2,1)S(1)}) custom-call(bf16[1024,1664]{1,0:T(8,128)(2,1)} %bitcast.3.refs_0_, f32[384,1]{1,0:T(8,128)S(1)} %reshape.24.refs_1_.refs_8_.refs_7_, bf16[1152,256]{1,0:T(8,128)(2,1)S(1)} %copy-done, ...), custom_call_target="tpu_custom_call" | custom-call | tf_op jit(solution)/shard_map/pallas_call | solution.py:561
  67.8 1.3 %collective-permute-start = (s16[128,1152]{1,0:T(8,128)(2,1)S(1)}, s16[128,1152]{1,0:T(8,128)(2,1)S(1)}, u32[]{:S(2)}, u32[]{:S(2)}) collective-permute-start(s16[128,1152]{1,0:T(8,128)(2,1)S(1)} %get-tuple-element.27), channel_id=1, source_target_pairs={{8,0},{16,8},{24,16},{32,24},{40,32},{48,40},{56,48},{64,56},{72,6... | collective-permute-start | bytes 884744 | tf_op jit(solution)/shard_map/ppermute | solution.py:579
  69.1 0.0 collective-permute-start.1
  69.1 0.5 collective-permute-start.2
  69.7 0.0 copy-done.4
  69.7 0.0 copy-done.13
  69.7 0.0 copy-start.11
  69.7 0.0 copy-start.12
  69.7 0.0 copy-start.14
  69.7 0.0 copy-start.15
  69.7 0.0 copy-start.18
  69.8 4.6 %shard_map.228 = (f32[384,1024]{1,0:T(8,128)S(1)}, f32[384,1024]{1,0:T(8,128)S(1)}, f32[96,1024]{1,0:T(8,128)S(1)}) custom-call(f32[384,2048]{1,0:T(8,128)S(1)} %get-tuple-element.24.refs_0_, bf16[1152,256]{1,0:T(8,128)(2,1)S(1)} %copy-done, bf16[384,1152]{1,0:T(8,128)(2,1)S(1)} %copy-done.4, bf16[96,1152]{1,0:T(8,128)(2,1)S(1)} %copy-done.13), custom_call_target="tpu_custom_call" | custom-call | flops 1000000000 | tf_op jit(solution)/shard_map/pallas_call | solution.py:561
  74.4 2.5 %collective-permute-done.2.refs_4_.refs_6_ = s16[32,1152]{1,0:T(8,128)(2,1)S(1)} collective-permute-done((s16[32,1152]{1,0:T(8,128)(2,1)S(1)}, s16[32,1152]{1,0:T(8,128)(2,1)S(1)}, u32[]{:S(2)}, u32[]{:S(2)}) %collective-permute-start.2) | collective-permute-done | bytes 73760 | tf_op jit(solution)/shard_map/ppermute | solution.py:587
  76.9 0.0 collective-permute-done.1.refs_3_.refs_5_
  76.9 0.9 collective-permute-done.refs_2_.refs_4_
  77.8 0.0 copy-done.8
  77.8 0.9 shard_map.229.refs_14_.refs_1_
  78.7 4.7 %collective-permute-start.4 = (f32[24,512]{1,0:T(8,128)S(1)}, f32[24,512]{1,0:T(8,128)S(1)}, u32[]{:S(2)}, u32[]{:S(2)}) collective-permute-start(f32[24,512]{1,0:T(8,128)S(1)} %shard_map.229.refs_14_.refs_1_), channel_id=1, source_target_pairs={{8,0},{16,8},{24,16},{32,24},{40,32},{48,40},{56,48},{64,56},{72,6... | collective-permute-start | bytes 147464 | tf_op jit(solution)/shard_map/ppermute | solution.py:579
  83.3 0.0 collective-permute-start.3
  83.3 0.0 copy-done.1
  83.3 0.0 copy-done.11
  83.3 0.0 copy-done.12
  83.3 0.0 copy-done.14
  83.4 0.0 copy-done.15
  83.4 0.0 copy-done.18
  83.4 0.0 copy-start.2
  83.4 0.0 copy-start.16
  83.4 0.0 copy-start.17
  83.4 4.7 %shard_map.230 = (f32[288,1024]{1,0:T(8,128)S(1)}, f32[384,1024]{1,0:T(8,128)S(1)}, f32[136,1024]{1,0:T(8,128)S(1)}, f32[96,1024]{1,0:T(8,128)S(1)}, f32[96,1024]{1,0:T(8,128)S(1)}) custom-call(f32[3,7]{1,0:T(4,128)S(1)} %copy-done.18, f32[384,1024]{1,0:T(8,128)S(1)} %get-tuple-element.25.refs_1_, f32[384,1024]{1,0:T(8,128)S(1)} %get-tuple-element.26.refs_2_, ...), custom_call_target="tpu_custom_call" | custom-call | flops 1000000000 | tf_op jit(solution)/shard_map/pallas_call | solution.py:561
  88.2 0.0 collective-permute-done.4.refs_2_
  88.2 2.6 %collective-permute-done.3.refs_0_ = f32[24,512]{1,0:T(8,128)S(1)} collective-permute-done((f32[24,512]{1,0:T(8,128)S(1)}, f32[24,512]{1,0:T(8,128)S(1)}, u32[]{:S(2)}, u32[]{:S(2)}) %collective-permute-start.3) | collective-permute-done | bytes 49184 | tf_op jit(solution)/shard_map/ppermute | solution.py:579
  90.8 0.0 collective-permute-start.5
  90.8 2.9 %collective-permute-start.6 = (f32[48,512]{1,0:T(8,128)S(1)}, f32[48,512]{1,0:T(8,128)S(1)}, u32[]{:S(2)}, u32[]{:S(2)}) collective-permute-start(f32[48,512]{1,0:T(8,128)S(1)} %get-tuple-element.36), channel_id=1, source_target_pairs={{1,0},{2,1},{3,2},{4,3},{5,4},{6,5},{7,6},{0,7},{9,8},{10,9},{11,1... | collective-permute-start | bytes 294920 | tf_op jit(solution)/shard_map/ppermute | solution.py:581
  93.8 2.3 %collective-permute-done.5.refs_1_ = f32[48,512]{1,0:T(8,128)S(1)} collective-permute-done((f32[48,512]{1,0:T(8,128)S(1)}, f32[48,512]{1,0:T(8,128)S(1)}, u32[]{:S(2)}, u32[]{:S(2)}) %collective-permute-start.5) | collective-permute-done | bytes 98336 | tf_op jit(solution)/shard_map/ppermute | solution.py:581
  96.1 0.0 collective-permute-done.6.refs_3_
  96.1 0.0 copy-done.2
  96.1 0.0 copy-done.16
  96.1 0.0 copy-done.17
  96.1 1.7 %shard_map.232 = (f32[24,1024]{1,0:T(8,128)S(1)}, s16[128,1152]{1,0:T(8,128)(2,1)S(1)}, s16[80,1152]{1,0:T(8,128)(2,1)S(1)}, s16[32,1152]{1,0:T(8,128)(2,1)S(1)}) custom-call(f32[3,7]{1,0:T(4,128)S(1)} %copy-done.18, f32[48,512]{1,0:T(8,128)S(1)} %collective-permute-done.5.refs_1_, f32[72,512]{1,0:T(8,128)S(1)} %get-tuple-element.35.refs_2_, ...), custom_call_target="tpu_custom_call" | custom-call | tf_op jit(solution)/shard_map/pallas_call | solution.py:561
  97.8 0.1 collective-permute-start.7
  97.8 0.0 collective-permute-start.8
  97.9 0.3 collective-permute-start.9
  98.2 0.0 copy-done.3
  98.2 0.0 copy-done.5
  98.2 0.0 copy-done.10
  98.2 0.0 copy-start.6
  98.2 0.0 copy-start.7
  98.2 5.0 %shard_map.233.refs_0_ = f32[384,2048]{1,0:T(8,128)S(1)} custom-call(f32[288,1024]{1,0:T(8,128)S(1)} %get-tuple-element.31.refs_3_.refs_0_, f32[384,1024]{1,0:T(8,128)S(1)} %get-tuple-element.32.refs_1_, f32[96,1024]{1,0:T(8,128)S(1)} %get-tuple-element.33.refs_2_, f32[24,1024]{1,0:T(8,128)S(1)} %get-tuple-element.39.refs_3_, ...), custom_call_target="tpu_custom_call" | custom-call | flops 1000000000 | tf_op jit(solution)/shard_map/pallas_call | solution.py:561
  103.3 8.0 %collective-permute-done.9.refs_3_ = s16[32,1152]{1,0:T(8,128)(2,1)S(1)} collective-permute-done((s16[32,1152]{1,0:T(8,128)(2,1)S(1)}, s16[32,1152]{1,0:T(8,128)(2,1)S(1)}, u32[]{:S(2)}, u32[]{:S(2)}) %collective-permute-start.9) | collective-permute-done | bytes 73760 | tf_op jit(solution)/shard_map/ppermute | solution.py:587
  111.3 0.0 collective-permute-done.8.refs_2_
  111.3 0.0 collective-permute-done.7.refs_1_
  111.3 0.0 copy-done.6
  111.3 0.0 copy-done.7
  111.3 3.6 %shard_map.234 = f32[384,2048]{1,0:T(8,128)} custom-call(f32[384,2048]{1,0:T(8,128)S(1)} %shard_map.233.refs_0_, s16[128,1152]{1,0:T(8,128)(2,1)S(1)} %collective-permute-done.7.refs_1_, s16[80,1152]{1,0:T(8,128)(2,1)S(1)} %collective-permute-done.8.refs_2_, s16[32,1152]{1,0:T(8,128)(2,1)S(1)} %collective-permute-done.9.refs_3_, ...), custom_call_target="tpu_custom_call" | custom-call | tf_op jit(solution)/shard_map/pallas_call | solution.py:561
  (9 shorter events, 0.1 us)
Async XLA Ops:
  5.7 11.7 %copy-start.19 = (s32[16,24]{1,0:T(8,128)S(1)}, s32[16,24]{1,0:T(8,128)}, u32[]{:S(2)}) copy-start(s32[16,24]{1,0:T(8,128)} %param.27) | copy-start | bytes 4612
  5.7 55.8 %copy-start = (bf16[1152,256]{1,0:T(8,128)(2,1)S(1)}, bf16[1152,256]{1,0:T(8,128)(2,1)}, u32[]{:S(2)}) copy-start(bf16[1152,256]{1,0:T(8,128)(2,1)} %constant.18.clone.refs_2_.refs_1_.refs_5_.refs_11_) | copy-start | bytes 1769476
  5.7 55.8 %copy-start.9 = (bf16[136,1152]{1,0:T(8,128)(2,1)S(1)}, bf16[136,1152]{1,0:T(8,128)(2,1)}, u32[]{:S(2)}) copy-start(bf16[136,1152]{1,0:T(8,128)(2,1)} %constant.38.clone.refs_3_) | copy-start | bytes 940036
  5.7 55.8 %all-to-all-start = ((bf16[128,8,1664]{2,1,0:T(8,128)(2,1)}), bf16[128,8,1664]{2,1,0:T(8,128)(2,1)}, u32[]{:S(2)}, u32[]{:S(2)}) async-start(bf16[128,8,1664]{2,1,0:T(8,128)(2,1)} %bitcast.5), calls=%async_computation | async-start | bytes 6815744 | tf_op jit(solution)/shard_map/all_to_all | solution.py:620
  61.5 8.1 %copy-start.4 = (bf16[384,1152]{1,0:T(8,128)(2,1)S(1)}, bf16[384,1152]{1,0:T(8,128)(2,1)}, u32[]{:S(2)}) copy-start(bf16[384,1152]{1,0:T(8,128)(2,1)} %constant.39.clone.refs_2_) | copy-start | bytes 2654212
  61.5 8.1 %copy-start.13 = (bf16[96,1152]{1,0:T(8,128)(2,1)S(1)}, bf16[96,1152]{1,0:T(8,128)(2,1)}, u32[]{:S(2)}) copy-start(bf16[96,1152]{1,0:T(8,128)(2,1)} %constant.40.clone.refs_3_) | copy-start | bytes 663556
  67.8 9.9 %collective-permute-start = (s16[128,1152]{1,0:T(8,128)(2,1)S(1)}, s16[128,1152]{1,0:T(8,128)(2,1)S(1)}, u32[]{:S(2)}, u32[]{:S(2)}) collective-permute-start(s16[128,1152]{1,0:T(8,128)(2,1)S(1)} %get-tuple-element.27), channel_id=1, source_target_pairs={{8,0},{16,8},{24,16},{32,24},{40,32},{48,40},{56,48},{64,56},{72,6... | collective-permute-start | bytes 884744 | tf_op jit(solution)/shard_map/ppermute | solution.py:579
  69.1 7.8 %collective-permute-start.1 = (s16[80,1152]{1,0:T(8,128)(2,1)S(1)}, s16[80,1152]{1,0:T(8,128)(2,1)S(1)}, u32[]{:S(2)}, u32[]{:S(2)}) collective-permute-start(s16[80,1152]{1,0:T(8,128)(2,1)S(1)} %get-tuple-element.28), channel_id=1, source_target_pairs={{1,0},{2,1},{3,2},{4,3},{5,4},{6,5},{7,6},{0,7},{9,8},{10,9},{11,1... | collective-permute-start | bytes 552968 | tf_op jit(solution)/shard_map/ppermute | solution.py:581
  69.1 7.8 %collective-permute-start.2 = (s16[32,1152]{1,0:T(8,128)(2,1)S(1)}, s16[32,1152]{1,0:T(8,128)(2,1)S(1)}, u32[]{:S(2)}, u32[]{:S(2)}) collective-permute-start(s16[32,1152]{1,0:T(8,128)(2,1)S(1)} %get-tuple-element.29), channel_id=1, source_target_pairs={{9,0},{10,1},{11,2},{12,3},{13,4},{14,5},{15,6},{8,7},{17,8},{18,9... | collective-permute-start | bytes 221192 | tf_op jit(solution)/shard_map/ppermute | solution.py:587
  69.7 8.1 %copy-start.8 = (bf16[96,408]{1,0:T(8,128)(2,1)S(1)}, bf16[96,408]{1,0:T(8,128)(2,1)}, u32[]{:S(2)}) copy-start(bf16[96,408]{1,0:T(8,128)(2,1)} %constant.41.clone.refs_1_.refs_10_) | copy-start | bytes 235012
  69.7 13.7 %copy-start.1 = (bf16[1536,256]{1,0:T(8,128)(2,1)S(1)}, bf16[1536,256]{1,0:T(8,128)(2,1)}, u32[]{:S(2)}) copy-start(bf16[1536,256]{1,0:T(8,128)(2,1)} %constant.45.clone.refs_12_.refs_7_.refs_4_) | copy-start | bytes 2359300
  69.7 13.6 %copy-start.11 = (bf16[384,288]{1,0:T(8,128)(2,1)S(1)}, bf16[384,288]{1,0:T(8,128)(2,1)}, u32[]{:S(2)}) copy-start(bf16[384,288]{1,0:T(8,128)(2,1)} %constant.42.clone.refs_3_) | copy-start | bytes 663556
  69.7 13.6 %copy-start.12 = (bf16[96,1152]{1,0:T(8,128)(2,1)S(1)}, bf16[96,1152]{1,0:T(8,128)(2,1)}, u32[]{:S(2)}) copy-start(bf16[96,1152]{1,0:T(8,128)(2,1)} %constant.44.clone.refs_8_) | copy-start | bytes 663556
  69.7 13.6 %copy-start.14 = (bf16[96,864]{1,0:T(8,128)(2,1)S(1)}, bf16[96,864]{1,0:T(8,128)(2,1)}, u32[]{:S(2)}) copy-start(bf16[96,864]{1,0:T(8,128)(2,1)} %constant.43.clone.refs_7_) | copy-start | bytes 497668
  69.7 13.6 %copy-start.15 = (bf16[136,288]{1,0:T(8,128)(2,1)S(1)}, bf16[136,288]{1,0:T(8,128)(2,1)}, u32[]{:S(2)}) copy-start(bf16[136,288]{1,0:T(8,128)(2,1)} %constant.46.clone.refs_13_) | copy-start | bytes 235012
  69.7 13.6 %copy-start.18 = (f32[3,7]{1,0:T(4,128)S(1)}, f32[3,7]{1,0:T(4,128)}, u32[]{:S(2)}) copy-start(f32[3,7]{1,0:T(4,128)} %refs_0_.3) | copy-start | bytes 256
  78.7 9.5 %collective-permute-start.4 = (f32[24,512]{1,0:T(8,128)S(1)}, f32[24,512]{1,0:T(8,128)S(1)}, u32[]{:S(2)}, u32[]{:S(2)}) collective-permute-start(f32[24,512]{1,0:T(8,128)S(1)} %shard_map.229.refs_14_.refs_1_), channel_id=1, source_target_pairs={{8,0},{16,8},{24,16},{32,24},{40,32},{48,40},{56,48},{64,56},{72,6... | collective-permute-start | bytes 147464 | tf_op jit(solution)/shard_map/ppermute | solution.py:579
  83.3 7.4 %collective-permute-start.3 = (f32[24,512]{1,0:T(8,128)S(1)}, f32[24,512]{1,0:T(8,128)S(1)}, u32[]{:S(2)}, u32[]{:S(2)}) collective-permute-start(f32[24,512]{1,0:T(8,128)S(1)} %shard_map.229.refs_14_.refs_1_), channel_id=1, source_target_pairs={{120,0},{0,8},{8,16},{16,24},{24,32},{32,40},{40,48},{48,56},{56,6... | collective-permute-start | bytes 147464 | tf_op jit(solution)/shard_map/ppermute | solution.py:579
  83.4 12.7 %copy-start.2 = (bf16[1536,512]{1,0:T(8,128)(2,1)S(1)}, bf16[1536,512]{1,0:T(8,128)(2,1)}, u32[]{:S(2)}) copy-start(bf16[1536,512]{1,0:T(8,128)(2,1)} %constant.49.clone.refs_6_) | copy-start | bytes 4718596
  83.4 12.7 %copy-start.16 = (bf16[160,240]{1,0:T(8,128)(2,1)S(1)}, bf16[160,240]{1,0:T(8,128)(2,1)}, u32[]{:S(2)}) copy-start(bf16[160,240]{1,0:T(8,128)(2,1)} %constant.48.clone.refs_5_) | copy-start | bytes 230404
  83.4 12.7 %copy-start.17 = (bf16[80,504]{1,0:T(8,128)(2,1)S(1)}, bf16[80,504]{1,0:T(8,128)(2,1)}, u32[]{:S(2)}) copy-start(bf16[80,504]{1,0:T(8,128)(2,1)} %constant.47.clone.refs_4_) | copy-start | bytes 241924
  90.7 7.4 %copy-start.3 = (bf16[384,1152]{1,0:T(8,128)(2,1)S(1)}, bf16[384,1152]{1,0:T(8,128)(2,1)}, u32[]{:S(2)}) copy-start(bf16[384,1152]{1,0:T(8,128)(2,1)} %constant.51.clone.refs_5_) | copy-start | bytes 2654212
  90.7 7.4 %copy-start.5 = (bf16[384,864]{1,0:T(8,128)(2,1)S(1)}, bf16[384,864]{1,0:T(8,128)(2,1)}, u32[]{:S(2)}) copy-start(bf16[384,864]{1,0:T(8,128)(2,1)} %constant.50.clone.refs_4_) | copy-start | bytes 1990660
  90.7 7.5 %copy-start.10 = (bf16[384,288]{1,0:T(8,128)(2,1)S(1)}, bf16[384,288]{1,0:T(8,128)(2,1)}, u32[]{:S(2)}) copy-start(bf16[384,288]{1,0:T(8,128)(2,1)} %constant.52.clone.refs_6_) | copy-start | bytes 663556
  90.8 5.3 %collective-permute-start.5 = (f32[48,512]{1,0:T(8,128)S(1)}, f32[48,512]{1,0:T(8,128)S(1)}, u32[]{:S(2)}, u32[]{:S(2)}) collective-permute-start(f32[48,512]{1,0:T(8,128)S(1)} %get-tuple-element.34), channel_id=1, source_target_pairs={{7,0},{0,1},{1,2},{2,3},{3,4},{4,5},{5,6},{6,7},{15,8},{8,9},{9,10... | collective-permute-start | bytes 294920 | tf_op jit(solution)/shard_map/ppermute | solution.py:581
  90.8 5.2 %collective-permute-start.6 = (f32[48,512]{1,0:T(8,128)S(1)}, f32[48,512]{1,0:T(8,128)S(1)}, u32[]{:S(2)}, u32[]{:S(2)}) collective-permute-start(f32[48,512]{1,0:T(8,128)S(1)} %get-tuple-element.36), channel_id=1, source_target_pairs={{1,0},{2,1},{3,2},{4,3},{5,4},{6,5},{7,6},{0,7},{9,8},{10,9},{11,1... | collective-permute-start | bytes 294920 | tf_op jit(solution)/shard_map/ppermute | solution.py:581
  97.8 13.5 %collective-permute-start.7 = (s16[128,1152]{1,0:T(8,128)(2,1)S(1)}, s16[128,1152]{1,0:T(8,128)(2,1)S(1)}, u32[]{:S(2)}, u32[]{:S(2)}) collective-permute-start(s16[128,1152]{1,0:T(8,128)(2,1)S(1)} %get-tuple-element.40), channel_id=1, source_target_pairs={{120,0},{0,8},{8,16},{16,24},{24,32},{32,40},{40,48},{48,56},{56,6... | collective-permute-start | bytes 884744 | tf_op jit(solution)/shard_map/ppermute | solution.py:579
  97.8 13.4 %collective-permute-start.8 = (s16[80,1152]{1,0:T(8,128)(2,1)S(1)}, s16[80,1152]{1,0:T(8,128)(2,1)S(1)}, u32[]{:S(2)}, u32[]{:S(2)}) collective-permute-start(s16[80,1152]{1,0:T(8,128)(2,1)S(1)} %get-tuple-element.41), channel_id=1, source_target_pairs={{7,0},{0,1},{1,2},{2,3},{3,4},{4,5},{5,6},{6,7},{15,8},{8,9},{9,10... | collective-permute-start | bytes 552968 | tf_op jit(solution)/shard_map/ppermute | solution.py:581
  97.9 13.4 %collective-permute-start.9 = (s16[32,1152]{1,0:T(8,128)(2,1)S(1)}, s16[32,1152]{1,0:T(8,128)(2,1)S(1)}, u32[]{:S(2)}, u32[]{:S(2)}) collective-permute-start(s16[32,1152]{1,0:T(8,128)(2,1)S(1)} %get-tuple-element.42), channel_id=1, source_target_pairs={{127,0},{120,1},{121,2},{122,3},{123,4},{124,5},{125,6},{126,7},{7... | collective-permute-start | bytes 221192 | tf_op jit(solution)/shard_map/ppermute | solution.py:587
  98.2 13.1 %copy-start.6 = (bf16[384,408]{1,0:T(8,128)(2,1)S(1)}, bf16[384,408]{1,0:T(8,128)(2,1)}, u32[]{:S(2)}) copy-start(bf16[384,408]{1,0:T(8,128)(2,1)} %constant.54.clone.refs_6_) | copy-start | bytes 940036
  98.2 13.1 %copy-start.7 = (bf16[768,256]{1,0:T(8,128)(2,1)S(1)}, bf16[768,256]{1,0:T(8,128)(2,1)}, u32[]{:S(2)}) copy-start(bf16[768,256]{1,0:T(8,128)(2,1)} %constant.53.clone.refs_5_) | copy-start | bytes 1179652
